TPU v7x, 32 devices: a whole 2x2x4 slice. The times are simulated.
32 devices in a mesh: wide: 8 (over z, x), narrow: 4 (over y, core).
Axes of the slice: x: 2, y: 2, z: 4, core: 2. Of those that a mesh axis runs over, the one named last changes fastest.
Arguments:
- snapshot: float32 [512, 16, 64, 128], P('wide', 'narrow'), may hold values from -81 to 81
Outputs:
- core: float32 [256, 16, 64, 128], P(None, 'narrow', 'wide')
- factor: float32 [512, 256], replicated
All inputs are finite; a program needn't handle non-finite values.
Results may differ from a plain program's by a relative error of at most 0.000071.
Values sent between devices are 32-bit elements; how exact they have to be, the bound alone decides.
No kernel may reach another device: no remote copies, remote signals or barrier semaphores. Data moves between devices by JAX's collectives and lax.ppermute only.
A program may use at most 320 MiB of HBM per device.

v0:
```python
import jax
import jax.numpy as jnp
from jax import lax
from jax.sharding import PartitionSpec as P

RANK = 256


def on_device(snapshot):
    regrouped = lax.all_to_all(snapshot, "wide", split_axis=2, concat_axis=0, tiled=True)
    rows_all = regrouped.shape[0]
    unfold = regrouped.reshape(rows_all, -1)
    gram = jnp.dot(
        unfold, unfold.T, precision=lax.Precision.HIGHEST, preferred_element_type=jnp.float32
    )
    gram = lax.psum(gram, "narrow")
    gram = lax.psum(gram, "wide")
    upper = jnp.linalg.cholesky(gram).T
    rows_kept = upper[:RANK, :]
    lengths = jnp.sqrt(jnp.sum(rows_kept * rows_kept, axis=1))
    factor = (rows_kept / lengths[:, None]).T
    core = jnp.dot(
        factor.T, unfold, precision=lax.Precision.HIGHEST, preferred_element_type=jnp.float32
    )
    core = core.reshape(RANK, regrouped.shape[1], regrouped.shape[2], regrouped.shape[3])
    return (core, factor)


def solution(mesh):
    in_specs = (P("wide", "narrow", None, None),)
    out_specs = (P(None, "narrow", "wide", None), P())
    return jax.shard_map(
        on_device, mesh=mesh, in_specs=in_specs, out_specs=out_specs, check_vma=False
    )
```

profile of v0, /device:TPU:1, one launch (start us, length us, event | category | flops | bytes accessed | tf_op | source)
XLA Modules:
  0.0 471.9 jit_solution(2083413374057106725)
XLA Ops:
  7.2 8.2 %copy.21 = f32[64,4,64,128]{3,0,1,2:T(8,128)S(1)} copy(f32[64,4,64,128]{3,2,1,0:T(8,128)} %param.1) | data formatting | bytes 16777216 | tf_op args[0]
  15.4 188.8 %all_to_all.15 = f32[64,4,64,128]{3,0,1,2:T(8,128)S(1)} all-to-all(f32[64,4,64,128]{3,0,1,2:T(8,128)S(1)} %copy.21), channel_id=1, replica_groups=mesh['wide'=8,'narrow'=4] {'wide'}, dimensions={2} | all-to-all | bytes 16777216 | tf_op jit(solution)/shard_map/all_to_all | solution.py:10
  204.3 8.0 %copy.32 = f32[64,4,8,8,128]{4,3,1,0,2:T(8,128)} copy(f32[64,4,8,8,128]{4,0,1,3,2:T(8,128)S(1)} %bitcast.42) | data formatting | bytes 16777216 | tf_op jit(solution)/shard_map/all_to_all | solution.py:10
  212.3 9.4 %reshape.40 = f32[512,4096]{1,0:T(8,128)} reshape(f32[8,64,4,8,128]{4,3,2,1,0:T(8,128)} %bitcast.43) | data formatting | bytes 16777216 | tf_op jit(solution)/shard_map/reshape | solution.py:12
  221.7 17.2 %fusion.15 = f32[512,512]{0,1:T(8,128)} fusion(f32[512,4096]{1,0:T(8,128)} %reshape.40), kind=kOutput, calls=%fused_computation.43 | convolution fusion | flops 12884901888 | bytes 9437184 | tf_op jit(solution)/shard_map/dot_general | solution.py:13
  239.0 36.1 %all-reduce.4.cloned.1.call-done = f32[512,512]{0,1:T(8,128)} async-done(((f32[512,512]{0,1:T(8,128)}), f32[512,512]{0,1:T(8,128)}) %all-reduce.4.cloned.1.call-update) | async-done | bytes 1048592 | tf_op jit(solution)/shard_map/psum | solution.py:16
  275.1 9.2 %copy.25 = f32[4096,512]{1,0:T(8,128)} copy(f32[4096,512]{0,1:T(8,128)} %bitcast.40) | data formatting | bytes 16777216 | tf_op jit(solution)/shard_map/dot_general | solution.py:22
  284.3 72.7 %all-reduce.6.cloned.1.call-done = f32[512,512]{0,1:T(8,128)} async-done(((f32[512,512]{0,1:T(8,128)}), f32[512,512]{0,1:T(8,128)}) %all-reduce.6.cloned.1.call-update) | async-done | bytes 1048592 | tf_op jit(solution)/shard_map/psum | solution.py:17
  356.9 1.6 copy.24
  358.5 1.4 fusion
  360.0 11.7 %cholesky.104 = f32[128,128]{1,0:T(8,128)S(1)} custom-call(f32[128,128]{1,0:T(8,128)S(1)} %cholesky.266), custom_call_target="Cholesky" | custom-call | tf_op jit(solution)/shard_map/jit(cholesky)/cholesky | solution.py:18
  371.7 0.1 cholesky.224
  371.9 9.8 %custom-call.27 = f32[1,128,128]{1,2,0:T(8,128)S(1)} custom-call(f32[1,128,128]{2,1,0:T(8,128)S(1)} %get-tuple-element.19), custom_call_target="InvertDiagBlocksLowerTriangular" | custom-call | tf_op jit(solution)/shard_map/jit(cholesky)/cholesky | solution.py:18
  381.7 0.3 constant_dynamic-update-slice_fusion.2
  382.0 0.3 convolution_subtract_fusion
  382.3 11.7 %cholesky.217 = f32[128,128]{1,0:T(8,128)S(1)} custom-call(f32[128,128]{1,0:T(8,128)S(1)} %cholesky.270), custom_call_target="Cholesky" | custom-call | tf_op jit(solution)/shard_map/jit(cholesky)/cholesky | solution.py:18
  394.1 10.0 %custom-call.28 = f32[1,128,128]{1,2,0:T(8,128)S(1)} custom-call(f32[1,128,128]{2,1,0:T(8,128)S(1)} %get-tuple-element.16), custom_call_target="InvertDiagBlocksLowerTriangular" | custom-call | tf_op jit(solution)/shard_map/jit(cholesky)/cholesky | solution.py:18
  404.1 0.3 convolution_dynamic-update-slice_fusion
  404.4 0.4 convolution_subtract_fusion.1
  404.8 11.7 %cholesky.238 = f32[128,128]{1,0:T(8,128)S(1)} custom-call(f32[128,128]{1,0:T(8,128)S(1)} %cholesky.275), custom_call_target="Cholesky" | custom-call | tf_op jit(solution)/shard_map/jit(cholesky)/cholesky | solution.py:18
  416.5 9.8 %custom-call.29 = f32[1,128,128]{1,2,0:T(8,128)S(1)} custom-call(f32[1,128,128]{2,1,0:T(8,128)S(1)} %get-tuple-element.13), custom_call_target="InvertDiagBlocksLowerTriangular" | custom-call | tf_op jit(solution)/shard_map/jit(cholesky)/cholesky | solution.py:18
  426.3 0.2 convolution_dynamic-update-slice_fusion.1
  426.5 0.4 convolution_subtract_fusion.2
  426.9 11.7 %cholesky.255 = f32[128,128]{1,0:T(8,128)S(1)} custom-call(f32[128,128]{1,0:T(8,128)S(1)} %convolution_subtract_fusion.2), custom_call_target="Cholesky" | custom-call | tf_op jit(solution)/shard_map/jit(cholesky)/cholesky | solution.py:18
  438.7 0.6 compare_reduce_fusion.1
  439.3 0.6 compare_reduce_fusion
  439.9 0.6 compare_reduce_fusion.2
  443.1 0.1 select_bitcast_fusion
  443.2 0.3 multiply_reduce_fusion
  443.5 0.9 fusion.7
  444.4 15.8 %fusion.1 = f32[256,4,8,128]{3,0,2,1:T(8,128)S(1)} fusion(f32[4,8,128,512]{3,2,1,0:T(8,128)} %bitcast.41, f32[512,512]{0,1:T(8,128)S(1)} %select_bitcast_fusion, f32[256]{0:T(256)S(1)} %sqrt.7), kind=kOutput, calls=%fused_computation.10 | convolution fusion | flops 6442582016 | bytes 13108224 | tf_op jit(solution)/shard_map/dot_general | solution.py:22
  460.2 4.4 copy.27
  (12 shorter events, 0.3 us)
Async XLA Ops:
  7.2 267.9 %all-reduce.4.cloned.1.call-start = ((), (), s32[]{:S(2)}) async-start(), calls=%async_computation.1 | async-start | bytes 2097152 | tf_op jit(solution)/shard_map/psum | solution.py:16
  238.9 118.0 %all-reduce.6.cloned.1.call-start = ((), (), s32[]{:S(2)}) async-start(), calls=%async_computation.2 | async-start | bytes 2097152 | tf_op jit(solution)/shard_map/psum | solution.py:17
Sparse Core Ops, SparseCore 0:
  239.0 36.0 all-reduce.3
  279.0 77.9 all-reduce.5
where the time goes:
time: 478 us; the launch traced here: 472 us
  blocking collectives  189 us (40%)
  waiting for transfers between devices  109 us (23%)
  other arithmetic  81.3 us (17%)
  local copies, waits for them, and re-layouts  40.9 us (9%)
  matrix products  34.9 us (7%)
  between operations  17.1 us (4%)
    all_to_all x1, blocking collectives, on_device(): lax.all_to_all(snapshot, 'wide', split_axis=2, concat_axis=0, tiled=True)  189 us
    another operation x14, other arithmetic, on_device(): upper = jnp.linalg.cholesky(gram).T  78.5 us
    psum x1, waiting for transfers between devices, on_device(): gram = lax.psum(gram, 'wide')  72.7 us
    psum x1, waiting for transfers between devices, on_device(): gram = lax.psum(gram, 'narrow')  36.1 us
    dot_general x1, matrix products, on_device(): jnp.dot(unfold, unfold.T, precision=lax.Precision.HIGHEST, preferred_elem...  17.2 us
    dot_general x1, matrix products, on_device(): jnp.dot(factor.T, unfold, precision=lax.Precision.HIGHEST, preferred_elem...  15.8 us
    unnamed x2, local copies, waits for them, and re-layouts  12.7 us
  transfers between devices with their start and end apart: 2, of which 2 were waited for; matrix products, arithmetic and copies ran while one was open for 2% of the time, Pallas kernels for 0%

commit v1 on v0

v1 whole, which is shorter than its diff:
```python
import functools

import jax
import jax.numpy as jnp
from jax import lax
from jax.experimental import pallas as pl
from jax.experimental.pallas import tpu as pltpu
from jax.sharding import PartitionSpec as P

RANK = 256
LANES = 128
FAST_WIDE = 8
HIGHEST = lax.Precision.HIGHEST
VMEM_LIMIT = 48 * 1024 * 1024


def swapped(flag, blocks, distance):
    return [jnp.where(flag, blocks[i ^ distance], blocks[i]) for i in range(len(blocks))]


def in_row_order(place, blocks):
    distance = 1
    while distance < len(blocks):
        blocks = swapped((place & distance) != 0, blocks, distance)
        distance *= 2
    return blocks


def two_slabs(place, refs, s):
    sides = []
    for t in (s, s + 1):
        blocks = in_row_order(place, [r[t] for r in refs])
        sides.append(jnp.concatenate(blocks, axis=0))
    return jnp.concatenate(sides, axis=1)


def rows_dot(a, b):
    return lax.dot_general(
        a, b, (((1,), (1,)), ((), ())), precision=HIGHEST, preferred_element_type=jnp.float32
    )


def own_gram_kernel(place_ref, *refs):
    blocks, out_ref = refs[:-1], refs[-1]

    @pl.when(pl.program_id(0) == 0)
    def _():
        out_ref[...] = jnp.zeros_like(out_ref)

    total = out_ref[...]
    for s in range(0, blocks[0].shape[0], 2):
        own = two_slabs(place_ref[0], blocks, s)
        total += rows_dot(own, own)
    out_ref[...] = total


def gram_kernel(place_ref, own_gram_ref, *refs):
    half = (len(refs) - 2) // 2
    own_refs, other_refs, out_ref, cross_ref = refs[:half], refs[half:-2], refs[-2], refs[-1]
    place = place_ref[0]
    first = pl.program_id(0) == 0

    @pl.when(first)
    def _():
        out_ref[...] = jnp.zeros_like(out_ref)
        cross_ref[...] = jnp.zeros_like(cross_ref)

    cross = cross_ref[...]
    total = out_ref[:RANK, :]
    for s in range(0, own_refs[0].shape[0], 2):
        own = two_slabs(place, own_refs, s)
        other = two_slabs(place, other_refs, s)
        cross += rows_dot(other, own)
        total += rows_dot(other, other)
    cross_ref[...] = cross
    out_ref[:RANK, :] = total

    @pl.when(pl.program_id(0) == pl.num_programs(0) - 1)
    def _():
        low = place < half
        out_ref[:RANK, :] = jnp.where(low, own_gram_ref[...], total)
        out_ref[RANK:, :] = jnp.where(low, cross, cross.T)


def whole(shape):
    return pl.BlockSpec(shape, lambda i: (0,) * len(shape))


def own_gram(place, blocks, steps):
    cells, rows, fields = blocks[0].shape
    part = pl.BlockSpec((cells // steps, rows, fields), lambda i: (i, 0, 0))
    size = rows * len(blocks)
    return pl.pallas_call(
        own_gram_kernel,
        grid=(steps,),
        in_specs=[pl.BlockSpec(memory_space=pltpu.SMEM)] + [part] * len(blocks),
        out_specs=whole((size, size)),
        out_shape=jax.ShapeDtypeStruct((size, size), jnp.float32),
        compiler_params=pltpu.CompilerParams(vmem_limit_bytes=VMEM_LIMIT),
        cost_estimate=pl.CostEstimate(
            flops=12 * size * size * cells * fields, bytes_accessed=4 * size * cells * fields, transcendentals=0
        ),
        name="own_gram",
    )(place, *blocks)


def full_gram(place, own, blocks, steps):
    cells, rows, fields = blocks[0].shape
    part = pl.BlockSpec((cells // steps, rows, fields), lambda i: (i, 0, 0))
    size = rows * len(blocks)
    return pl.pallas_call(
        gram_kernel,
        grid=(steps,),
        in_specs=[pl.BlockSpec(memory_space=pltpu.SMEM), whole(own.shape)] + [part] * len(blocks),
        out_specs=whole((size, RANK)),
        out_shape=jax.ShapeDtypeStruct((size, RANK), jnp.float32),
        scratch_shapes=[pltpu.VMEM((RANK, RANK), jnp.float32)],
        compiler_params=pltpu.CompilerParams(vmem_limit_bytes=VMEM_LIMIT),
        cost_estimate=pl.CostEstimate(
            flops=12 * size * RANK * cells * fields, bytes_accessed=4 * size * cells * fields, transcendentals=0
        ),
        name="full_gram",
    )(place, own, *blocks)


def over(axis, n, distance):
    return functools.partial(lax.ppermute, axis_name=axis, perm=[(i, i ^ distance) for i in range(n)])


def sum_over_all(x, wide, narrow):
    place = lax.axis_index("narrow")
    distances = [1 << b for b in range(narrow.bit_length() - 1)]
    for d in distances:
        side = (place & d) != 0
        n = x.shape[0] // 2
        keep = jnp.where(side, x[n:], x[:n])
        send = jnp.where(side, x[:n], x[n:])
        x = keep + over("narrow", narrow, d)(send)
    for b in range(wide.bit_length() - 1):
        x = x + over("wide", wide, 1 << b)(x)
    for d in reversed(distances):
        side = (place & d) != 0
        got = over("narrow", narrow, d)(x)
        x = jnp.where(side, jnp.concatenate([got, x]), jnp.concatenate([x, got]))
    return x


PANEL = 64
SUB = 8


def refine_reciprocal(d):
    r = pl.reciprocal(d, approx=True)
    r = r * (2.0 - d * r)
    return r * (2.0 - d * r)


def refine_rsqrt(d):
    r = lax.rsqrt(d)
    return r * (1.5 - 0.5 * d * r * r)


def cholesky_kernel(gram_ref, upper_ref, inverse_ref, work):
    n = gram_ref.shape[0]
    tiles = n // LANES
    sub = lax.broadcasted_iota(jnp.int32, (SUB, LANES), 0)
    lane = lax.broadcasted_iota(jnp.int32, (SUB, LANES), 1)
    row_id = lax.broadcasted_iota(jnp.int32, (n, n), 0)
    col_id = lax.broadcasted_iota(jnp.int32, (n, n), 1)
    work[:, :n] = gram_ref[...]
    work[:, n:] = jnp.where(row_id == col_id, 1.0, 0.0)
    for p in range(n // PANEL):
        top = p * PANEL
        t0 = top // LANES
        cols = [t for t in range(t0, tiles)] + [tiles + t for t in range(0, t0 + 1)]
        groups = PANEL // SUB
        grp = [
            [work[top + SUB * g : top + SUB * (g + 1), LANES * t : LANES * (t + 1)] for t in cols]
            for g in range(groups)
        ]
        pivots = [jnp.ones((SUB, LANES), jnp.float32) for _ in range(groups)]
        for i in range(PANEL):
            g0, s = divmod(i, SUB)
            c = (top + i) % LANES
            row = [jnp.broadcast_to(v[s : s + 1, :], (SUB, LANES)) for v in grp[g0]]
            d = jnp.broadcast_to(row[0][:, c : c + 1], (SUB, LANES))
            pivots[g0] = jnp.where(sub == s, d, pivots[g0])
            inv = refine_reciprocal(d)
            row = [v * inv for v in row]
            for g in range(g0, groups):
                m = jnp.broadcast_to(grp[g][0][:, c : c + 1], (SUB, LANES))
                if g == g0:
                    m = jnp.where(sub > s, m, 0.0)
                grp[g] = [v - m * r for v, r in zip(grp[g], row)]
        left = len(cols) - (t0 + 1)
        for g in range(groups):
            rs = refine_rsqrt(pivots[g])
            rows = slice(top + SUB * g, top + SUB * (g + 1))
            for v, t in zip(grp[g], cols):
                v = v * rs
                if t < tiles:
                    v = jnp.where(lane + LANES * t >= sub + (top + SUB * g), v, 0.0)
                work[rows, LANES * t : LANES * (t + 1)] = v
        for t in range(t0):
            work[top : top + PANEL, LANES * t : LANES * (t + 1)] = jnp.zeros((PANEL, LANES), jnp.float32)
        below = top + PANEL
        if below < n:
            lo, hi = LANES * t0, n + LANES * (t0 + 1)
            update = lax.dot_general(
                work[top:below, :n],
                work[top:below, lo:hi],
                (((0,), (0,)), ((), ())),
                precision=HIGHEST,
                preferred_element_type=jnp.float32,
            )
            work[below:, lo:hi] = work[below:, lo:hi] - update[below:, :]
    upper_ref[...] = work[:, :n]
    inverse_ref[...] = work[:, n:]


def cholesky(gram):
    n = gram.shape[0]
    return pl.pallas_call(
        cholesky_kernel,
        out_shape=[jax.ShapeDtypeStruct((n, n), jnp.float32)] * 2,
        scratch_shapes=[pltpu.VMEM((n, 2 * n), jnp.float32)],
        compiler_params=pltpu.CompilerParams(vmem_limit_bytes=VMEM_LIMIT),
        cost_estimate=pl.CostEstimate(flops=2 * n * n * n, bytes_accessed=12 * n * n, transcendentals=n),
        name="cholesky256",
    )(gram)


def split(x):
    high = x.astype(jnp.bfloat16)
    return high, (x - high.astype(jnp.float32)).astype(jnp.bfloat16)


def bf16_dot(a, b):
    return jnp.dot(a, b, preferred_element_type=jnp.float32)


def core_kernel(place_ref, gram_ref, upper_ref, inverse_ref, *refs):
    blocks, (out_ref, factor_ref, high, low) = refs[:-4], refs[-4:]
    place = place_ref[0]

    @pl.when(pl.program_id(0) == 0)
    def _():
        left = upper_ref[...]
        right = rows_dot(inverse_ref[...], gram_ref[...])
        squares = jnp.sum(left * left, axis=1, keepdims=True) + jnp.sum(right * right, axis=1, keepdims=True)
        length = jnp.sqrt(squares)
        rows = jnp.concatenate([left / length, right / length], axis=1)
        factor_ref[...] = rows.T
        high[...], low[...] = split(rows)

    fh, fl = high[...], low[...]
    for s in range(0, blocks[0].shape[0], 2):
        uh, ul = split(two_slabs(place, blocks, s))
        both = bf16_dot(fh, uh) + (bf16_dot(fl, uh) + bf16_dot(fh, ul))
        out_ref[:, 0, s, :] = both[:, :LANES]
        out_ref[:, 0, s + 1, :] = both[:, LANES:]


def core_and_factor(place, gram21, upper, inverse, blocks, ny, nz):
    cells, rows, fields = blocks[0].shape
    size = rows * len(blocks)
    part = pl.BlockSpec((nz, rows, fields), lambda i: (i, 0, 0))
    return pl.pallas_call(
        core_kernel,
        grid=(ny,),
        in_specs=[pl.BlockSpec(memory_space=pltpu.SMEM)]
        + [whole((RANK, RANK))] * 3
        + [part] * len(blocks),
        out_specs=[
            pl.BlockSpec((RANK, 1, nz, fields), lambda i: (0, i, 0, 0)),
            whole((size, RANK)),
        ],
        out_shape=[
            jax.ShapeDtypeStruct((RANK, ny, nz, fields), jnp.float32),
            jax.ShapeDtypeStruct((size, RANK), jnp.float32),
        ],
        scratch_shapes=[pltpu.VMEM((RANK, size), jnp.bfloat16)] * 2,
        compiler_params=pltpu.CompilerParams(vmem_limit_bytes=VMEM_LIMIT),
        cost_estimate=pl.CostEstimate(
            flops=6 * size * RANK * cells * fields,
            bytes_accessed=4 * (size + RANK) * cells * fields,
            transcendentals=0,
        ),
        name="core",
    )(place, gram21, upper, inverse, *blocks)


def tie(x, *deps):
    return lax.optimization_barrier((x,) + deps)[0]


def block_for(snapshot, device, nz):
    rows, ny, _, fields = snapshot.shape
    cut = lax.dynamic_slice_in_dim(snapshot, device * nz, nz, axis=2)
    return cut.transpose(1, 2, 0, 3).reshape(ny * nz, rows, fields)


def on_device_blocks(snapshot, wide, narrow):
    ny, nz = snapshot.shape[1], snapshot.shape[2] // wide
    here = lax.axis_index("wide")
    place = here.astype(jnp.int32).reshape(1)
    half = wide // 2
    got = {}
    send = lambda k, *deps: over("wide", wide, k)(tie(block_for(snapshot, here ^ k, nz), *deps))
    for k in (6, 4, 7, 5):
        got[k] = send(k)
    got[2] = send(2)
    got[3] = send(3, got[2])
    got[1] = send(1, got[3])
    got[0] = block_for(snapshot, here, nz)
    blocks = [got[k] for k in range(wide)]
    own = own_gram(place, blocks[:half], ny)
    gram = full_gram(place, own, blocks, ny)
    gram = sum_over_all(gram, wide, narrow)
    upper, inverse = cholesky(gram[:RANK])
    return core_and_factor(place, gram[RANK:], upper, inverse, blocks, ny, nz)


def on_device_any(snapshot):
    regrouped = lax.all_to_all(snapshot, "wide", split_axis=2, concat_axis=0, tiled=True)
    rows_all = regrouped.shape[0]
    unfold = regrouped.reshape(rows_all, -1)
    gram = lax.dot_general(
        unfold, unfold[:RANK], (((1,), (1,)), ((), ())), precision=HIGHEST, preferred_element_type=jnp.float32
    )
    gram = lax.psum(lax.psum(gram, "narrow"), "wide")
    lower = jnp.linalg.cholesky(gram[:RANK])
    upper = jnp.concatenate(
        [lower.T, lax.linalg.triangular_solve(lower, gram[RANK:].T, left_side=True, lower=True)], axis=1
    )
    lengths = jnp.sqrt(jnp.sum(upper * upper, axis=1))
    factor = (upper / lengths[:, None]).T
    core = jnp.dot(factor.T, unfold, precision=HIGHEST, preferred_element_type=jnp.float32)
    return core.reshape((RANK,) + regrouped.shape[1:]), factor


def solution(mesh):
    wide, narrow = mesh.shape["wide"], mesh.shape["narrow"]
    if wide == FAST_WIDE:
        on_device = functools.partial(on_device_blocks, wide=wide, narrow=narrow)
    else:
        on_device = on_device_any
    return jax.shard_map(
        on_device,
        mesh=mesh,
        in_specs=(P("wide", "narrow", None, None),),
        out_specs=(P(None, "narrow", "wide", None), P()),
        check_vma=False,
    )
```

time: 478 us -> 331 us (0.69); the launches traced: 472 us -> 331 us
  blocking collectives: 189 us -> 0 us
  waiting for transfers between devices: 109 us -> 201 us
  other arithmetic: 81.3 us -> 0.24 us
  Pallas kernels: 0 us -> 62 us
  starting transfers between devices: 0.08 us -> 48.7 us
  matrix products: 34.9 us -> 0 us
  local copies, waits for them, and re-layouts: 40.9 us -> 17.9 us
  between operations: 17.1 us -> 0.8 us
    ppermute x0 -> x14, waiting for transfers between devices: none -> 201 us  [the longest x7 184 us: on_device_blocks(): over('wide', wide, k)(tie(block_for(snapshot, here ^ k, nz), *deps))]
    all_to_all x1 -> x0, blocking collectives: 189 us -> none  [on_device(): lax.all_to_all(snapshot, 'wide', split_axis=2, concat_axis=0, tiled=True)]
    psum x2 -> x0, waiting for transfers between devices: 109 us -> none  [the longest x1 72.7 us: on_device(): gram = lax.psum(gram, 'wide')]
    another operation x14 -> x0, other arithmetic: 78.5 us -> none  [on_device(): upper = jnp.linalg.cholesky(gram).T]
    pallas_call x0 -> x4, Pallas kernels: none -> 62 us  [the longest x1 37.5 us: cholesky(): pl.pallas_call(cholesky_kernel, out_shape=[jax.ShapeDtypeStruct((n, n), j...]
    ppermute x0 -> x14, starting transfers between devices: none -> 48.7 us  [the longest x3 24.8 us: sum_over_all(): x = x + over('wide', wide, 1 << b)(x)]
    dot_general x2 -> x0, matrix products: 33 us -> none  [the longest x1 17.2 us: on_device(): jnp.dot(unfold, unfold.T, precision=lax.Precision.HIGHEST, preferred_elem...]
    transpose x0 -> x9, local copies, waits for them, and re-layouts: none -> 14.5 us  [block_for(): return cut.transpose(1, 2, 0, 3).reshape(ny * nz, rows, fields)]
  transfers between devices with their start and end apart: 2 -> 14, of which waited for: 2 -> 12; matrix products, arithmetic and copies ran while one was open for 2% -> 3% of each run, Pallas kernels for 0% -> 2%
where the time goes in v1:
time: 331 us
  waiting for transfers between devices  201 us (61%)
  Pallas kernels  62 us (19%)
  starting transfers between devices  48.7 us (15%)
  local copies, waits for them, and re-layouts  17.9 us (5%)
    ppermute x7, waiting for transfers between devices, on_device_blocks(): over('wide', wide, k)(tie(block_for(snapshot, here ^ k, nz), *deps))  184 us
    pallas_call x1, Pallas kernels, cholesky(): pl.pallas_call(cholesky_kernel, out_shape=[jax.ShapeDtypeStruct((n, n), j...  37.5 us
    ppermute x3, starting transfers between devices, sum_over_all(): x = x + over('wide', wide, 1 << b)(x)  24.8 us
    transpose x9, local copies, waits for them, and re-layouts, block_for(): return cut.transpose(1, 2, 0, 3).reshape(ny * nz, rows, fields)  14.5 us
    ppermute x7, starting transfers between devices, on_device_blocks(): over('wide', wide, k)(tie(block_for(snapshot, here ^ k, nz), *deps))  11.6 us
    pallas_call x1, Pallas kernels, core_and_factor(): pl.pallas_call(core_kernel, grid=(ny,), in_specs=[pl.BlockSpec(memory_spa...  9.62 us
    pallas_call x1, Pallas kernels, full_gram(): pl.pallas_call(gram_kernel, grid=(steps,), in_specs=[pl.BlockSpec(memory_...  9.34 us
    ppermute x2, starting transfers between devices, sum_over_all(): got = over('narrow', narrow, d)(x)  8.09 us
  transfers between devices with their start and end apart: 14, of which 12 were waited for; matrix products, arithmetic and copies ran while one was open for 3% of the time, Pallas kernels for 2%

profile of v1, /device:TPU:1, one launch (start us, length us, event | category | flops | bytes accessed | tf_op | source)
XLA Modules:
  0.0 330.7 jit_solution(17452839853022343296)
XLA Ops:
  0.7 4.6 %dynamic-slice_bitcast_fusion = (f32[4,8,64,128]{3,1,0,2:T(8,128)S(1)}, f32[4,8,64,128]{3,1,0,2:T(8,128)S(1)}, f32[4,8,64,128]{3,1,0,2:T(8,128)S(1)}, f32[4,8,64...) fusion(f32[64,4,64,128]{3,2,1,0:T(8,128)} %param.1, ...), kind=kLoop, calls=%fused_computation | loop fusion | bytes 16777248 | tf_op jit(solution)/shard_map/transpose | solution.py:300
  5.9 2.2 collective-permute-start
  8.7 22.3 %collective-permute-done.refs_2_ = f32[32,64,128]{2,1,0:T(8,128)S(1)} collective-permute-done((f32[32,64,128]{2,1,0:T(8,128)S(1)}, f32[32,64,128]{2,1,0:T(8,128)S(1)}, u32[]{:S(2)}, u32[]{:S(2)}) %collective-permute-start) | collective-permute-done | bytes 1048608 | tf_op jit(solution)/shard_map/ppermute | solution.py:309
  30.9 2.1 collective-permute-start.1
  33.0 1.6 copy.4
  34.6 20.7 %collective-permute-done.1.refs_3_ = f32[32,64,128]{2,1,0:T(8,128)S(1)} collective-permute-done((f32[32,64,128]{2,1,0:T(8,128)S(1)}, f32[32,64,128]{2,1,0:T(8,128)S(1)}, u32[]{:S(2)}, u32[]{:S(2)}) %collective-permute-start.1) | collective-permute-done | bytes 1048608 | tf_op jit(solution)/shard_map/ppermute | solution.py:309
  57.0 1.6 copy.9
  58.6 3.3 %collective-permute-start.5 = (f32[32,64,128]{2,1,0:T(8,128)}, f32[32,64,128]{2,1,0:T(8,128)}, u32[]{:S(2)}, u32[]{:S(2)}) collective-permute-start(f32[32,64,128]{2,1,0:T(8,128)} %bitcast.14), channel_id=1, source_target_pairs={{0,24},{4,28},{8,16},{12,20},{16,8},{20,12},{24,0},{28,4},{1,25},{... | collective-permute-start | bytes 3145736 | tf_op jit(solution)/shard_map/ppermute | solution.py:309
  61.9 1.7 copy.7
  63.6 1.7 copy.8
  65.2 2.3 collective-permute-start.4
  67.6 1.6 copy.10
  70.7 8.4 %collective-permute-done.2.refs_1_ = f32[32,64,128]{2,1,0:T(8,128)} collective-permute-done((f32[32,64,128]{2,1,0:T(8,128)}, f32[32,64,128]{2,1,0:T(8,128)}, u32[]{:S(2)}, u32[]{:S(2)}) %collective-permute-start.2) | collective-permute-done | bytes 1048608 | tf_op jit(solution)/shard_map/ppermute | solution.py:309
  79.1 1.2 copy-done.1
  80.3 5.6 %own_gram.1.own_gram_ref = f32[256,256]{1,0:T(8,128)S(1)} custom-call(s32[1]{0:T(128)} %bitcast.place_ref, f32[32,64,128]{2,1,0:T(8,128)S(1)} %bitcast.25, f32[32,64,128]{2,1,0:T(8,128)} %collective-permute-done.2.refs_1_, f32[32,64,128]{2,1,0:T(8,128)S(1)} %collective-permute-done.refs_2_, f32[32,64,128]{2,1,0:T(8,128)S(1)} %copy-done.1), custom_call_target="tpu_custom_call" | custom-call | flops 3221225472 | bytes 4194304 | tf_op jit(solution)/shard_map/own_gram/pallas_call | solution.py:93
  85.9 110.5 %collective-permute-done.3.refs_4_ = f32[32,64,128]{2,1,0:T(8,128)} collective-permute-done((f32[32,64,128]{2,1,0:T(8,128)}, f32[32,64,128]{2,1,0:T(8,128)}, u32[]{:S(2)}, u32[]{:S(2)}) %collective-permute-start.3) | collective-permute-done | bytes 1048608 | tf_op jit(solution)/shard_map/ppermute | solution.py:309
  196.4 22.0 %collective-permute-done.4.refs_5_ = f32[32,64,128]{2,1,0:T(8,128)} collective-permute-done((f32[32,64,128]{2,1,0:T(8,128)}, f32[32,64,128]{2,1,0:T(8,128)}, u32[]{:S(2)}, u32[]{:S(2)}) %collective-permute-start.4) | collective-permute-done | bytes 1048608 | tf_op jit(solution)/shard_map/ppermute | solution.py:309
  218.5 9.3 %full_gram.1 = f32[512,256]{1,0:T(8,128)S(1)} custom-call(s32[1]{0:T(128)} %bitcast.place_ref, f32[256,256]{1,0:T(8,128)S(1)} %own_gram.1.own_gram_ref, f32[32,64,128]{2,1,0:T(8,128)S(1)} %bitcast.26, f32[32,64,128]{2,1,0:T(8,128)} %collective-permute-done.2.refs_1_, f32[32,64,128]{2,1,0:T(8,128)S(1)} %collective-permute-done.refs_2_, ...), custom_call_target="tpu_custom_call" | custom-call | flops 6442450944 | bytes 8388608 | tf_op jit(solution)/shard_map/full_gram/pallas_call | solution.py:111
  227.8 3.3 collective-permute-start.7
  231.2 1.2 collective-permute-done.7
  233.3 3.9 %collective-permute-done.8 = f32[128,256]{1,0:T(8,128)S(1)} collective-permute-done((f32[128,256]{1,0:T(8,128)S(1)}, f32[128,256]{1,0:T(8,128)S(1)}, u32[]{:S(2)}, u32[]{:S(2)}) %collective-permute-start.8) | collective-permute-done | bytes 131104 | tf_op jit(solution)/shard_map/ppermute | solution.py:138
  238.1 3.0 collective-permute-done.9
  241.1 21.4 %collective-permute-start.10 = (f32[128,256]{1,0:T(8,128)S(1)}, f32[128,256]{1,0:T(8,128)S(1)}, u32[]{:S(2)}, u32[]{:S(2)}) collective-permute-start(f32[128,256]{1,0:T(8,128)S(1)} %add.49), channel_id=1, source_target_pairs={{0,8},{4,12},{8,0},{12,4},{16,24},{20,28},{24,16},{28,20},{1,9},{5... | collective-permute-start | bytes 393224 | tf_op jit(solution)/shard_map/ppermute | solution.py:140
  262.5 2.4 collective-permute-done.10
  264.9 2.5 collective-permute-start.11
  267.4 2.7 collective-permute-done.11
  270.1 1.3 collective-permute-start.12
  271.4 2.9 collective-permute-done.12
  274.3 6.8 %collective-permute-start.13 = (f32[256,256]{1,0:T(8,128)S(1)}, f32[256,256]{1,0:T(8,128)S(1)}, u32[]{:S(2)}, u32[]{:S(2)}) collective-permute-start(f32[256,256]{1,0:T(8,128)S(1)} %maximum_select_fusion.1), channel_id=1, source_target_pairs={{0,1},{1,0},{2,3},{3,2},{4,5},{5,4},{6,7},{7,6},{8,9},{9,8},{10,11... | collective-permute-start | bytes 786440 | tf_op jit(solution)/shard_map/ppermute | solution.py:143
  282.4 37.5 %cholesky256.1 = (f32[256,256]{1,0:T(8,128)S(1)}, f32[256,256]{1,0:T(8,128)S(1)}) custom-call(f32[256,256]{1,0:T(8,128)S(1)} %get-tuple-element.18.gram_ref), custom_call_target="tpu_custom_call" | custom-call | flops 33554432 | bytes 786432 | tf_op jit(solution)/shard_map/cholesky256/pallas_call | solution.py:223
  319.9 1.2 copy-done.2
  321.1 9.6 %core.1 = (f32[256,4,8,128]{3,2,1,0:T(8,128)}, f32[512,256]{1,0:T(8,128)}) custom-call(s32[1]{0:T(128)} %bitcast.place_ref, f32[256,256]{1,0:T(8,128)S(1)} %get-tuple-element.19.gram_ref, f32[256,256]{1,0:T(8,128)S(1)} %get-tuple-element.8.upper_ref, f32[256,256]{1,0:T(8,128)S(1)} %get-tuple-element.9.inverse_ref, f32[32,64,128]{2,1,0:T(8,128)S(1)} %bitcast.27, ...), custom_call_target="tpu_custom_call" | custom-call | flops 3221225472 | bytes 12582912 | tf_op jit(solution)/shard_map/core/pallas_call | solution.py:268
  (25 shorter events, 7.7 us)
Async XLA Ops:
  5.9 25.1 %collective-permute-start = (f32[32,64,128]{2,1,0:T(8,128)S(1)}, f32[32,64,128]{2,1,0:T(8,128)S(1)}, u32[]{:S(2)}, u32[]{:S(2)}) collective-permute-start(f32[32,64,128]{2,1,0:T(8,128)S(1)} %bitcast.29), channel_id=1, source_target_pairs={{0,8},{4,12},{8,0},{12,4},{16,24},{20,28},{24,16},{28,20},{1,9},{5... | collective-permute-start | bytes 3145736 | tf_op jit(solution)/shard_map/ppermute | solution.py:309
  30.9 24.3 %collective-permute-start.1 = (f32[32,64,128]{2,1,0:T(8,128)S(1)}, f32[32,64,128]{2,1,0:T(8,128)S(1)}, u32[]{:S(2)}, u32[]{:S(2)}) collective-permute-start(f32[32,64,128]{2,1,0:T(8,128)S(1)} %bitcast.28), channel_id=1, source_target_pairs={{0,12},{4,8},{8,4},{12,0},{16,28},{20,24},{24,20},{28,16},{1,13},{... | collective-permute-start | bytes 3145736 | tf_op jit(solution)/shard_map/ppermute | solution.py:309
  55.3 1.0 copy-start
  56.2 22.8 %collective-permute-start.2 = (f32[32,64,128]{2,1,0:T(8,128)}, f32[32,64,128]{2,1,0:T(8,128)}, u32[]{:S(2)}, u32[]{:S(2)}) collective-permute-start(f32[32,64,128]{2,1,0:T(8,128)} %bitcast.4), channel_id=1, source_target_pairs={{0,4},{4,0},{8,12},{12,8},{16,20},{20,16},{24,28},{28,24},{1,5},{5... | collective-permute-start | bytes 3145736 | tf_op jit(solution)/shard_map/ppermute | solution.py:309
  58.6 27.3 %collective-permute-start.5 = (f32[32,64,128]{2,1,0:T(8,128)}, f32[32,64,128]{2,1,0:T(8,128)}, u32[]{:S(2)}, u32[]{:S(2)}) collective-permute-start(f32[32,64,128]{2,1,0:T(8,128)} %bitcast.14), channel_id=1, source_target_pairs={{0,24},{4,28},{8,16},{12,20},{16,8},{20,12},{24,0},{28,4},{1,25},{... | collective-permute-start | bytes 3145736 | tf_op jit(solution)/shard_map/ppermute | solution.py:309
  63.6 132.9 %collective-permute-start.3 = (f32[32,64,128]{2,1,0:T(8,128)}, f32[32,64,128]{2,1,0:T(8,128)}, u32[]{:S(2)}, u32[]{:S(2)}) collective-permute-start(f32[32,64,128]{2,1,0:T(8,128)} %bitcast.10), channel_id=1, source_target_pairs={{0,16},{4,20},{8,24},{12,28},{16,0},{20,4},{24,8},{28,12},{1,17},{... | collective-permute-start | bytes 3145736 | tf_op jit(solution)/shard_map/ppermute | solution.py:309
  65.2 153.2 %collective-permute-start.4 = (f32[32,64,128]{2,1,0:T(8,128)}, f32[32,64,128]{2,1,0:T(8,128)}, u32[]{:S(2)}, u32[]{:S(2)}) collective-permute-start(f32[32,64,128]{2,1,0:T(8,128)} %bitcast.12), channel_id=1, source_target_pairs={{0,20},{4,16},{8,28},{12,24},{16,4},{20,0},{24,12},{28,8},{1,21},{... | collective-permute-start | bytes 3145736 | tf_op jit(solution)/shard_map/ppermute | solution.py:309
  69.2 149.3 %collective-permute-start.6 = (f32[32,64,128]{2,1,0:T(8,128)}, f32[32,64,128]{2,1,0:T(8,128)}, u32[]{:S(2)}, u32[]{:S(2)}) collective-permute-start(f32[32,64,128]{2,1,0:T(8,128)} %bitcast.16), channel_id=1, source_target_pairs={{0,28},{4,24},{8,20},{12,16},{16,12},{20,8},{24,4},{28,0},{1,29},{... | collective-permute-start | bytes 3145736 | tf_op jit(solution)/shard_map/ppermute | solution.py:309
  79.1 1.2 copy-start.1
  227.8 4.5 %collective-permute-start.7 = (f32[256,256]{1,0:T(8,128)S(1)}, f32[256,256]{1,0:T(8,128)S(1)}, u32[]{:S(2)}, u32[]{:S(2)}) collective-permute-start(f32[256,256]{1,0:T(8,128)S(1)} %slice_select_fusion), channel_id=1, source_target_pairs={{0,1},{1,0},{2,3},{3,2},{4,5},{5,4},{6,7},{7,6},{8,9},{9,8},{10,11... | collective-permute-start | bytes 786440 | tf_op jit(solution)/shard_map/ppermute | solution.py:138
  232.4 4.8 %collective-permute-start.8 = (f32[128,256]{1,0:T(8,128)S(1)}, f32[128,256]{1,0:T(8,128)S(1)}, u32[]{:S(2)}, u32[]{:S(2)}) collective-permute-start(f32[128,256]{1,0:T(8,128)S(1)} %slice_select_fusion.1), channel_id=1, source_target_pairs={{0,2},{1,3},{2,0},{3,1},{4,6},{5,7},{6,4},{7,5},{8,10},{9,11},{10,... | collective-permute-start | bytes 393224 | tf_op jit(solution)/shard_map/ppermute | solution.py:138
  237.2 3.9 %collective-permute-start.9 = (f32[128,256]{1,0:T(8,128)S(1)}, f32[128,256]{1,0:T(8,128)S(1)}, u32[]{:S(2)}, u32[]{:S(2)}) collective-permute-start(f32[128,256]{1,0:T(8,128)S(1)} %select_add_fusion.1), channel_id=1, source_target_pairs={{0,4},{4,0},{8,12},{12,8},{16,20},{20,16},{24,28},{28,24},{1,5},{5... | collective-permute-start | bytes 393224 | tf_op jit(solution)/shard_map/ppermute | solution.py:140
  241.1 23.8 %collective-permute-start.10 = (f32[128,256]{1,0:T(8,128)S(1)}, f32[128,256]{1,0:T(8,128)S(1)}, u32[]{:S(2)}, u32[]{:S(2)}) collective-permute-start(f32[128,256]{1,0:T(8,128)S(1)} %add.49), channel_id=1, source_target_pairs={{0,8},{4,12},{8,0},{12,4},{16,24},{20,28},{24,16},{28,20},{1,9},{5... | collective-permute-start | bytes 393224 | tf_op jit(solution)/shard_map/ppermute | solution.py:140
  264.9 5.2 %collective-permute-start.11 = (f32[128,256]{1,0:T(8,128)S(1)}, f32[128,256]{1,0:T(8,128)S(1)}, u32[]{:S(2)}, u32[]{:S(2)}) collective-permute-start(f32[128,256]{1,0:T(8,128)S(1)} %add.50), channel_id=1, source_target_pairs={{0,16},{4,20},{8,24},{12,28},{16,0},{20,4},{24,8},{28,12},{1,17},{... | collective-permute-start | bytes 393224 | tf_op jit(solution)/shard_map/ppermute | solution.py:140
  270.1 4.2 %collective-permute-start.12 = (f32[128,256]{1,0:T(8,128)S(1)}, f32[128,256]{1,0:T(8,128)S(1)}, u32[]{:S(2)}, u32[]{:S(2)}) collective-permute-start(f32[128,256]{1,0:T(8,128)S(1)} %add.51), channel_id=1, source_target_pairs={{0,2},{1,3},{2,0},{3,1},{4,6},{5,7},{6,4},{7,5},{8,10},{9,11},{10,... | collective-permute-start | bytes 393224 | tf_op jit(solution)/shard_map/ppermute | solution.py:143
  274.3 7.9 %collective-permute-start.13 = (f32[256,256]{1,0:T(8,128)S(1)}, f32[256,256]{1,0:T(8,128)S(1)}, u32[]{:S(2)}, u32[]{:S(2)}) collective-permute-start(f32[256,256]{1,0:T(8,128)S(1)} %maximum_select_fusion.1), channel_id=1, source_target_pairs={{0,1},{1,0},{2,3},{3,2},{4,5},{5,4},{6,7},{7,6},{8,9},{9,8},{10,11... | collective-permute-start | bytes 786440 | tf_op jit(solution)/shard_map/ppermute | solution.py:143
  319.8 1.2 copy-start.2

commit v2 on v1

--- a/solution.py
+++ b/solution.py
@@ -149,71 +149,74 @@
 SUB = 8
 
 
-def refine_reciprocal(d):
-    r = pl.reciprocal(d, approx=True)
-    r = r * (2.0 - d * r)
-    return r * (2.0 - d * r)
-
-
 def refine_rsqrt(d):
     r = lax.rsqrt(d)
     return r * (1.5 - 0.5 * d * r * r)
 
 
+def from_row(v, i):
+    return jnp.broadcast_to(v[i : i + 1, :], (SUB, LANES))
+
+
+def from_lane(v, c):
+    return jnp.broadcast_to(v[:, c : c + 1], (SUB, LANES))
+
+
 def cholesky_kernel(gram_ref, upper_ref, inverse_ref, work):
     n = gram_ref.shape[0]
     tiles = n // LANES
+    groups = PANEL // SUB
     sub = lax.broadcasted_iota(jnp.int32, (SUB, LANES), 0)
     lane = lax.broadcasted_iota(jnp.int32, (SUB, LANES), 1)
     row_id = lax.broadcasted_iota(jnp.int32, (n, n), 0)
     col_id = lax.broadcasted_iota(jnp.int32, (n, n), 1)
     work[:, :n] = gram_ref[...]
     work[:, n:] = jnp.where(row_id == col_id, 1.0, 0.0)
-    for p in range(n // PANEL):
-        top = p * PANEL
+    for top in range(0, n, PANEL):
         t0 = top // LANES
-        cols = [t for t in range(t0, tiles)] + [tiles + t for t in range(0, t0 + 1)]
-        groups = PANEL // SUB
-        grp = [
-            [work[top + SUB * g : top + SUB * (g + 1), LANES * t : LANES * (t + 1)] for t in cols]
-            for g in range(groups)
-        ]
+        cols = list(range(t0, tiles)) + [tiles + t for t in range(t0 + 1)]
+        rows_of = lambda g: slice(top + SUB * g, top + SUB * (g + 1))
+        lanes_of = lambda t: slice(LANES * t, LANES * (t + 1))
+        grp = [[work[rows_of(g), lanes_of(t)] for t in cols] for g in range(groups)]
         pivots = [jnp.ones((SUB, LANES), jnp.float32) for _ in range(groups)]
-        for i in range(PANEL):
-            g0, s = divmod(i, SUB)
-            c = (top + i) % LANES
-            row = [jnp.broadcast_to(v[s : s + 1, :], (SUB, LANES)) for v in grp[g0]]
-            d = jnp.broadcast_to(row[0][:, c : c + 1], (SUB, LANES))
-            pivots[g0] = jnp.where(sub == s, d, pivots[g0])
-            inv = refine_reciprocal(d)
-            row = [v * inv for v in row]
-            for g in range(g0, groups):
-                m = jnp.broadcast_to(grp[g][0][:, c : c + 1], (SUB, LANES))
-                if g == g0:
-                    m = jnp.where(sub > s, m, 0.0)
-                grp[g] = [v - m * r for v, r in zip(grp[g], row)]
-        left = len(cols) - (t0 + 1)
+        for g0 in range(groups):
+            c0 = (top + SUB * g0) % LANES
+            heads = [[from_lane(grp[g][0], c0 + j) for j in range(SUB)] for g in range(g0, groups)]
+            for i in range(SUB):
+                pivot = from_row(heads[0][i], i)
+                pivots[g0] = jnp.where(sub == i, pivot, pivots[g0])
+                inverse = pl.reciprocal(pivot, approx=True)
+                head_row = {j: from_row(heads[0][j], i) for j in range(i + 1, SUB)}
+                row = [from_row(v, i) for v in grp[g0]]
+                for g in range(g0, groups):
+                    head = heads[g - g0]
+                    factor = head[i] * inverse
+                    if g == g0:
+                        factor = jnp.where(sub > i, factor, 0.0)
+                    for j in range(i + 1, SUB):
+                        head[j] = head[j] - factor * head_row[j]
+                    grp[g] = [v - factor * r for v, r in zip(grp[g], row)]
         for g in range(groups):
-            rs = refine_rsqrt(pivots[g])
-            rows = slice(top + SUB * g, top + SUB * (g + 1))
+            scale = refine_rsqrt(pivots[g])
             for v, t in zip(grp[g], cols):
-                v = v * rs
+                v = v * scale
                 if t < tiles:
                     v = jnp.where(lane + LANES * t >= sub + (top + SUB * g), v, 0.0)
-                work[rows, LANES * t : LANES * (t + 1)] = v
+                work[rows_of(g), lanes_of(t)] = v
         for t in range(t0):
-            work[top : top + PANEL, LANES * t : LANES * (t + 1)] = jnp.zeros((PANEL, LANES), jnp.float32)
+            work[top : top + PANEL, lanes_of(t)] = jnp.zeros((PANEL, LANES), jnp.float32)
         below = top + PANEL
         if below < n:
             lo, hi = LANES * t0, n + LANES * (t0 + 1)
+            first = below // LANES * LANES
             update = lax.dot_general(
-                work[top:below, :n],
+                work[top:below, first:n],
                 work[top:below, lo:hi],
                 (((0,), (0,)), ((), ())),
                 precision=HIGHEST,
                 preferred_element_type=jnp.float32,
             )
-            work[below:, lo:hi] = work[below:, lo:hi] - update[below:, :]
+            work[below:, lo:hi] = work[below:, lo:hi] - update[below - first :, :]
     upper_ref[...] = work[:, :n]
     inverse_ref[...] = work[:, n:]
 
@@ -305,13 +308,15 @@
     here = lax.axis_index("wide")
     place = here.astype(jnp.int32).reshape(1)
     half = wide // 2
+    first = block_for(snapshot, here ^ 6, nz)
+    snapshot = tie(snapshot, first)
     got = {}
     send = lambda k, *deps: over("wide", wide, k)(tie(block_for(snapshot, here ^ k, nz), *deps))
-    for k in (6, 4, 7, 5):
-        got[k] = send(k)
-    got[2] = send(2)
+    got[6] = over("wide", wide, 6)(first)
+    got[4], got[7], got[2] = send(4), send(7), send(2)
+    got[5] = send(5, got[6])
     got[3] = send(3, got[2])
-    got[1] = send(1, got[3])
+    got[1] = send(1, got[6])
     got[0] = block_for(snapshot, here, nz)
     blocks = [got[k] for k in range(wide)]
     own = own_gram(place, blocks[:half], ny)

time: 331 us -> 255 us (0.77)
  Pallas kernels: 62 us -> 33.2 us
  starting transfers between devices: 48.7 us -> 23.3 us
  waiting for transfers between devices: 201 us -> 181 us
    ppermute x7 -> x6, waiting for transfers between devices: 184 us -> 146 us  [on_device_blocks(): over('wide', wide, k)(tie(block_for(snapshot, here ^ k, nz), *deps))]
    pallas_call x1, Pallas kernels: 37.5 us -> 8.33 us  [cholesky(): pl.pallas_call(cholesky_kernel, out_shape=[jax.ShapeDtypeStruct((n, n), j...]
    ppermute x3, starting transfers between devices: 24.8 us -> 2.35 us  [sum_over_all(): x = x + over('wide', wide, 1 << b)(x)]
    ppermute x0 -> x1, waiting for transfers between devices: none -> 15.1 us  [on_device_blocks(): got[6] = over('wide', wide, 6)(first)]
    ppermute x7 -> x6, starting transfers between devices: 11.6 us -> 6.79 us  [on_device_blocks(): over('wide', wide, k)(tie(block_for(snapshot, here ^ k, nz), *deps))]
    ppermute x0 -> x1, starting transfers between devices: none -> 4.22 us  [on_device_blocks(): got[6] = over('wide', wide, 6)(first)]
    unnamed x6 -> x0, local copies, waits for them, and re-layouts: 3.43 us -> none
    ppermute x3, waiting for transfers between devices: 8.07 us -> 11.4 us  [sum_over_all(): x = x + over('wide', wide, 1 << b)(x)]
  transfers between devices with their start and end apart: 14 -> 14, of which waited for: 12 -> 12; matrix products, arithmetic and copies ran while one was open for 3% -> 5% of each run, Pallas kernels for 2% -> 2%
where the time goes in v2:
time: 255 us; the launch traced here: 254 us
  waiting for transfers between devices  181 us (71%)
  Pallas kernels  33.2 us (13%)
  starting transfers between devices  23.3 us (9%)
  local copies, waits for them, and re-layouts  15.3 us (6%)
    ppermute x6, waiting for transfers between devices, on_device_blocks(): over('wide', wide, k)(tie(block_for(snapshot, here ^ k, nz), *deps))  146 us
    transpose x10, local copies, waits for them, and re-layouts, block_for(): return cut.transpose(1, 2, 0, 3).reshape(ny * nz, rows, fields)  15.3 us
    ppermute x1, waiting for transfers between devices, on_device_blocks(): got[6] = over('wide', wide, 6)(first)  15.1 us
    ppermute x3, waiting for transfers between devices, sum_over_all(): x = x + over('wide', wide, 1 << b)(x)  11.4 us
    pallas_call x1, Pallas kernels, core_and_factor(): pl.pallas_call(core_kernel, grid=(ny,), in_specs=[pl.BlockSpec(memory_spa...  9.73 us
    pallas_call x1, Pallas kernels, full_gram(): pl.pallas_call(gram_kernel, grid=(steps,), in_specs=[pl.BlockSpec(memory_...  9.43 us
    pallas_call x1, Pallas kernels, cholesky(): pl.pallas_call(cholesky_kernel, out_shape=[jax.ShapeDtypeStruct((n, n), j...  8.33 us
    ppermute x2, starting transfers between devices, sum_over_all(): got = over('narrow', narrow, d)(x)  6.82 us
  transfers between devices with their start and end apart: 14, of which 12 were waited for; matrix products, arithmetic and copies ran while one was open for 5% of the time, Pallas kernels for 2%

profile of v2, /device:TPU:1, one launch (start us, length us, event | category | flops | bytes accessed | tf_op | source)
XLA Modules:
  0.0 254.2 jit_solution(2737063818725400821)
XLA Ops:
  0.6 1.3 dynamic-slice_bitcast_fusion.7
  2.6 4.2 %collective-permute-start = (f32[32,64,128]{2,1,0:T(8,128)S(1)}, f32[32,64,128]{2,1,0:T(8,128)}, u32[]{:S(2)}, u32[]{:S(2)}) collective-permute-start(f32[32,64,128]{2,1,0:T(8,128)S(1)} %bitcast.28), channel_id=1, source_target_pairs={{0,24},{4,28},{8,16},{12,20},{16,8},{20,12},{24,0},{28,4},{1,25},{... | collective-permute-start | bytes 3145736 | tf_op jit(solution)/shard_map/ppermute | solution.py:315
  6.8 4.1 %dynamic-slice_bitcast_fusion = (f32[4,8,64,128]{3,1,0,2:T(8,128)S(1)}, f32[4,8,64,128]{3,1,0,2:T(8,128)S(1)}, f32[4,8,64,128]{3,1,0,2:T(8,128)S(1)}, f32[4,8,64...) fusion(f32[64,4,64,128]{3,2,1,0:T(8,128)} %param.1, ...), kind=kLoop, calls=%fused_computation | loop fusion | bytes 14680092 | tf_op jit(solution)/shard_map/transpose | solution.py:303
  11.5 1.6 copy.7
  13.2 1.6 copy.5
  14.7 15.1 %collective-permute-done.refs_6_ = f32[32,64,128]{2,1,0:T(8,128)} collective-permute-done((f32[32,64,128]{2,1,0:T(8,128)S(1)}, f32[32,64,128]{2,1,0:T(8,128)}, u32[]{:S(2)}, u32[]{:S(2)}) %collective-permute-start) | collective-permute-done | bytes 1048608 | tf_op jit(solution)/shard_map/ppermute | solution.py:315
  30.9 22.2 %collective-permute-done.2.refs_2_ = f32[32,64,128]{2,1,0:T(8,128)S(1)} collective-permute-done((f32[32,64,128]{2,1,0:T(8,128)S(1)}, f32[32,64,128]{2,1,0:T(8,128)S(1)}, u32[]{:S(2)}, u32[]{:S(2)}) %collective-permute-start.2) | collective-permute-done | bytes 1048608 | tf_op jit(solution)/shard_map/ppermute | solution.py:314
  53.1 1.3 collective-permute-start.3
  54.3 1.7 copy.8
  56.0 3.2 %collective-permute-start.4 = (f32[32,64,128]{2,1,0:T(8,128)}, f32[32,64,128]{2,1,0:T(8,128)}, u32[]{:S(2)}, u32[]{:S(2)}) collective-permute-start(f32[32,64,128]{2,1,0:T(8,128)} %bitcast.12), channel_id=1, source_target_pairs={{0,16},{4,20},{8,24},{12,28},{16,0},{20,4},{24,8},{28,12},{1,17},{... | collective-permute-start | bytes 3145736 | tf_op jit(solution)/shard_map/ppermute | solution.py:314
  59.2 1.7 copy.10
  60.9 1.6 copy.9
  62.5 1.2 collective-permute-start.5
  64.3 35.0 %collective-permute-done.3.refs_3_ = f32[32,64,128]{2,1,0:T(8,128)} collective-permute-done((f32[32,64,128]{2,1,0:T(8,128)}, f32[32,64,128]{2,1,0:T(8,128)}, u32[]{:S(2)}, u32[]{:S(2)}) %collective-permute-start.3) | collective-permute-done | bytes 1048608 | tf_op jit(solution)/shard_map/ppermute | solution.py:314
  99.3 5.7 %own_gram.1.own_gram_ref = f32[256,256]{1,0:T(8,128)S(1)} custom-call(s32[1]{0:T(128)} %bitcast.place_ref, f32[32,64,128]{2,1,0:T(8,128)S(1)} %bitcast.25, f32[32,64,128]{2,1,0:T(8,128)} %collective-permute-done.1.refs_1_, f32[32,64,128]{2,1,0:T(8,128)S(1)} %collective-permute-done.2.refs_2_, f32[32,64,128]{2,1,0:T(8,128)} %collective-permute-done.3.refs_3_), custom_call_target="tpu_custom_call" | custom-call | flops 3221225472 | bytes 4194304 | tf_op jit(solution)/shard_map/own_gram/pallas_call | solution.py:93
  105.0 44.3 %collective-permute-done.4.refs_4_ = f32[32,64,128]{2,1,0:T(8,128)} collective-permute-done((f32[32,64,128]{2,1,0:T(8,128)}, f32[32,64,128]{2,1,0:T(8,128)}, u32[]{:S(2)}, u32[]{:S(2)}) %collective-permute-start.4) | collective-permute-done | bytes 1048608 | tf_op jit(solution)/shard_map/ppermute | solution.py:314
  149.3 44.9 %collective-permute-done.5.refs_5_ = f32[32,64,128]{2,1,0:T(8,128)} collective-permute-done((f32[32,64,128]{2,1,0:T(8,128)}, f32[32,64,128]{2,1,0:T(8,128)}, u32[]{:S(2)}, u32[]{:S(2)}) %collective-permute-start.5) | collective-permute-done | bytes 1048608 | tf_op jit(solution)/shard_map/ppermute | solution.py:314
  194.2 9.4 %full_gram.1 = f32[512,256]{1,0:T(8,128)S(1)} custom-call(s32[1]{0:T(128)} %bitcast.place_ref, f32[256,256]{1,0:T(8,128)S(1)} %own_gram.1.own_gram_ref, f32[32,64,128]{2,1,0:T(8,128)S(1)} %bitcast.26, f32[32,64,128]{2,1,0:T(8,128)} %collective-permute-done.1.refs_1_, f32[32,64,128]{2,1,0:T(8,128)S(1)} %collective-permute-done.2.refs_2_, ...), custom_call_target="tpu_custom_call" | custom-call | flops 6442450944 | bytes 8388608 | tf_op jit(solution)/shard_map/full_gram/pallas_call | solution.py:111
  203.7 1.9 collective-permute-start.7
  205.5 1.2 collective-permute-done.7
  206.8 1.3 collective-permute-start.8
  208.1 3.5 %collective-permute-done.8 = f32[128,256]{1,0:T(8,128)S(1)} collective-permute-done((f32[128,256]{1,0:T(8,128)S(1)}, f32[128,256]{1,0:T(8,128)S(1)}, u32[]{:S(2)}, u32[]{:S(2)}) %collective-permute-start.8) | collective-permute-done | bytes 131104 | tf_op jit(solution)/shard_map/ppermute | solution.py:138
  211.6 1.3 collective-permute-start.9
  212.9 2.6 %collective-permute-done.9 = f32[128,256]{1,0:T(8,128)S(1)} collective-permute-done((f32[128,256]{1,0:T(8,128)S(1)}, f32[128,256]{1,0:T(8,128)S(1)}, u32[]{:S(2)}, u32[]{:S(2)}) %collective-permute-start.9) | collective-permute-done | bytes 131104 | tf_op jit(solution)/shard_map/ppermute | solution.py:140
  215.6 3.8 %collective-permute-done.10 = f32[128,256]{1,0:T(8,128)S(1)} collective-permute-done((f32[128,256]{1,0:T(8,128)S(1)}, f32[128,256]{1,0:T(8,128)S(1)}, u32[]{:S(2)}, u32[]{:S(2)}) %collective-permute-start.10) | collective-permute-done | bytes 131104 | tf_op jit(solution)/shard_map/ppermute | solution.py:140
  220.4 5.0 %collective-permute-done.11 = f32[128,256]{1,0:T(8,128)S(1)} collective-permute-done((f32[128,256]{1,0:T(8,128)S(1)}, f32[128,256]{1,0:T(8,128)S(1)}, u32[]{:S(2)}, u32[]{:S(2)}) %collective-permute-start.11) | collective-permute-done | bytes 131104 | tf_op jit(solution)/shard_map/ppermute | solution.py:140
  225.4 1.3 collective-permute-start.12
  226.7 2.6 %collective-permute-done.12 = f32[128,256]{1,0:T(8,128)S(1)} collective-permute-done((f32[128,256]{1,0:T(8,128)S(1)}, f32[128,256]{1,0:T(8,128)S(1)}, u32[]{:S(2)}, u32[]{:S(2)}) %collective-permute-start.12) | collective-permute-done | bytes 131104 | tf_op jit(solution)/shard_map/ppermute | solution.py:143
  229.3 5.5 %collective-permute-start.13 = (f32[256,256]{1,0:T(8,128)S(1)}, f32[256,256]{1,0:T(8,128)S(1)}, u32[]{:S(2)}, u32[]{:S(2)}) collective-permute-start(f32[256,256]{1,0:T(8,128)S(1)} %maximum_select_fusion.1), channel_id=1, source_target_pairs={{0,1},{1,0},{2,3},{3,2},{4,5},{5,4},{6,7},{7,6},{8,9},{9,8},{10,11... | collective-permute-start | bytes 786440 | tf_op jit(solution)/shard_map/ppermute | solution.py:143
  234.9 1.2 collective-permute-done.13
  236.1 8.3 %cholesky256.1 = (f32[256,256]{1,0:T(8,128)S(1)}, f32[256,256]{1,0:T(8,128)S(1)}) custom-call(f32[256,256]{1,0:T(8,128)S(1)} %get-tuple-element.21.gram_ref), custom_call_target="tpu_custom_call" | custom-call | flops 33554432 | bytes 786432 | tf_op jit(solution)/shard_map/cholesky256/pallas_call | solution.py:226
  244.4 9.7 %core.1 = (f32[256,4,8,128]{3,2,1,0:T(8,128)}, f32[512,256]{1,0:T(8,128)}) custom-call(s32[1]{0:T(128)} %bitcast.place_ref, f32[256,256]{1,0:T(8,128)S(1)} %get-tuple-element.22.gram_ref, f32[256,256]{1,0:T(8,128)S(1)} %get-tuple-element.12.upper_ref, f32[256,256]{1,0:T(8,128)S(1)} %get-tuple-element.13.inverse_ref, f32[32,64,128]{2,1,0:T(8,128)S(1)} %bitcast.27, ...), custom_call_target="tpu_custom_call" | custom-call | flops 3221225472 | bytes 12582912 | tf_op jit(solution)/shard_map/core/pallas_call | solution.py:271
  (20 shorter events, 4.3 us)
Async XLA Ops:
  2.6 27.3 %collective-permute-start = (f32[32,64,128]{2,1,0:T(8,128)S(1)}, f32[32,64,128]{2,1,0:T(8,128)}, u32[]{:S(2)}, u32[]{:S(2)}) collective-permute-start(f32[32,64,128]{2,1,0:T(8,128)S(1)} %bitcast.28), channel_id=1, source_target_pairs={{0,24},{4,28},{8,16},{12,20},{16,8},{20,12},{24,0},{28,4},{1,25},{... | collective-permute-start | bytes 3145736 | tf_op jit(solution)/shard_map/ppermute | solution.py:315
  11.5 41.6 %collective-permute-start.2 = (f32[32,64,128]{2,1,0:T(8,128)S(1)}, f32[32,64,128]{2,1,0:T(8,128)S(1)}, u32[]{:S(2)}, u32[]{:S(2)}) collective-permute-start(f32[32,64,128]{2,1,0:T(8,128)S(1)} %bitcast.29), channel_id=1, source_target_pairs={{0,8},{4,12},{8,0},{12,4},{16,24},{20,28},{24,16},{28,20},{1,9},{5... | collective-permute-start | bytes 3145736 | tf_op jit(solution)/shard_map/ppermute | solution.py:314
  29.9 34.5 %collective-permute-start.1 = (f32[32,64,128]{2,1,0:T(8,128)}, f32[32,64,128]{2,1,0:T(8,128)}, u32[]{:S(2)}, u32[]{:S(2)}) collective-permute-start(f32[32,64,128]{2,1,0:T(8,128)} %bitcast.6), channel_id=1, source_target_pairs={{0,4},{4,0},{8,12},{12,8},{16,20},{20,16},{24,28},{28,24},{1,5},{5... | collective-permute-start | bytes 3145736 | tf_op jit(solution)/shard_map/ppermute | solution.py:314
  53.1 46.2 %collective-permute-start.3 = (f32[32,64,128]{2,1,0:T(8,128)}, f32[32,64,128]{2,1,0:T(8,128)}, u32[]{:S(2)}, u32[]{:S(2)}) collective-permute-start(f32[32,64,128]{2,1,0:T(8,128)} %bitcast.10), channel_id=1, source_target_pairs={{0,12},{4,8},{8,4},{12,0},{16,28},{20,24},{24,20},{28,16},{1,13},{... | collective-permute-start | bytes 3145736 | tf_op jit(solution)/shard_map/ppermute | solution.py:314
  56.0 93.3 %collective-permute-start.4 = (f32[32,64,128]{2,1,0:T(8,128)}, f32[32,64,128]{2,1,0:T(8,128)}, u32[]{:S(2)}, u32[]{:S(2)}) collective-permute-start(f32[32,64,128]{2,1,0:T(8,128)} %bitcast.12), channel_id=1, source_target_pairs={{0,16},{4,20},{8,24},{12,28},{16,0},{20,4},{24,8},{28,12},{1,17},{... | collective-permute-start | bytes 3145736 | tf_op jit(solution)/shard_map/ppermute | solution.py:314
  60.9 88.4 %collective-permute-start.6 = (f32[32,64,128]{2,1,0:T(8,128)}, f32[32,64,128]{2,1,0:T(8,128)}, u32[]{:S(2)}, u32[]{:S(2)}) collective-permute-start(f32[32,64,128]{2,1,0:T(8,128)} %bitcast.16), channel_id=1, source_target_pairs={{0,28},{4,24},{8,20},{12,16},{16,12},{20,8},{24,4},{28,0},{1,29},{... | collective-permute-start | bytes 3145736 | tf_op jit(solution)/shard_map/ppermute | solution.py:314
  62.5 131.7 %collective-permute-start.5 = (f32[32,64,128]{2,1,0:T(8,128)}, f32[32,64,128]{2,1,0:T(8,128)}, u32[]{:S(2)}, u32[]{:S(2)}) collective-permute-start(f32[32,64,128]{2,1,0:T(8,128)} %bitcast.14), channel_id=1, source_target_pairs={{0,20},{4,16},{8,28},{12,24},{16,4},{20,0},{24,12},{28,8},{1,21},{... | collective-permute-start | bytes 3145736 | tf_op jit(solution)/shard_map/ppermute | solution.py:314
  203.7 3.0 %collective-permute-start.7 = (f32[256,256]{1,0:T(8,128)S(1)}, f32[256,256]{1,0:T(8,128)S(1)}, u32[]{:S(2)}, u32[]{:S(2)}) collective-permute-start(f32[256,256]{1,0:T(8,128)S(1)} %slice_select_fusion), channel_id=1, source_target_pairs={{0,1},{1,0},{2,3},{3,2},{4,5},{5,4},{6,7},{7,6},{8,9},{9,8},{10,11... | collective-permute-start | bytes 786440 | tf_op jit(solution)/shard_map/ppermute | solution.py:138
  206.8 4.8 %collective-permute-start.8 = (f32[128,256]{1,0:T(8,128)S(1)}, f32[128,256]{1,0:T(8,128)S(1)}, u32[]{:S(2)}, u32[]{:S(2)}) collective-permute-start(f32[128,256]{1,0:T(8,128)S(1)} %slice_select_fusion.1), channel_id=1, source_target_pairs={{0,2},{1,3},{2,0},{3,1},{4,6},{5,7},{6,4},{7,5},{8,10},{9,11},{10,... | collective-permute-start | bytes 393224 | tf_op jit(solution)/shard_map/ppermute | solution.py:138
  211.6 3.9 %collective-permute-start.9 = (f32[128,256]{1,0:T(8,128)S(1)}, f32[128,256]{1,0:T(8,128)S(1)}, u32[]{:S(2)}, u32[]{:S(2)}) collective-permute-start(f32[128,256]{1,0:T(8,128)S(1)} %select_add_fusion.1), channel_id=1, source_target_pairs={{0,4},{4,0},{8,12},{12,8},{16,20},{20,16},{24,28},{28,24},{1,5},{5... | collective-permute-start | bytes 393224 | tf_op jit(solution)/shard_map/ppermute | solution.py:140
  215.5 3.9 %collective-permute-start.10 = (f32[128,256]{1,0:T(8,128)S(1)}, f32[128,256]{1,0:T(8,128)S(1)}, u32[]{:S(2)}, u32[]{:S(2)}) collective-permute-start(f32[128,256]{1,0:T(8,128)S(1)} %add.49), channel_id=1, source_target_pairs={{0,8},{4,12},{8,0},{12,4},{16,24},{20,28},{24,16},{28,20},{1,9},{5... | collective-permute-start | bytes 393224 | tf_op jit(solution)/shard_map/ppermute | solution.py:140
  219.4 6.0 %collective-permute-start.11 = (f32[128,256]{1,0:T(8,128)S(1)}, f32[128,256]{1,0:T(8,128)S(1)}, u32[]{:S(2)}, u32[]{:S(2)}) collective-permute-start(f32[128,256]{1,0:T(8,128)S(1)} %add.50), channel_id=1, source_target_pairs={{0,16},{4,20},{8,24},{12,28},{16,0},{20,4},{24,8},{28,12},{1,17},{... | collective-permute-start | bytes 393224 | tf_op jit(solution)/shard_map/ppermute | solution.py:140
  225.4 3.9 %collective-permute-start.12 = (f32[128,256]{1,0:T(8,128)S(1)}, f32[128,256]{1,0:T(8,128)S(1)}, u32[]{:S(2)}, u32[]{:S(2)}) collective-permute-start(f32[128,256]{1,0:T(8,128)S(1)} %add.51), channel_id=1, source_target_pairs={{0,2},{1,3},{2,0},{3,1},{4,6},{5,7},{6,4},{7,5},{8,10},{9,11},{10,... | collective-permute-start | bytes 393224 | tf_op jit(solution)/shard_map/ppermute | solution.py:143
  229.3 6.7 %collective-permute-start.13 = (f32[256,256]{1,0:T(8,128)S(1)}, f32[256,256]{1,0:T(8,128)S(1)}, u32[]{:S(2)}, u32[]{:S(2)}) collective-permute-start(f32[256,256]{1,0:T(8,128)S(1)} %maximum_select_fusion.1), channel_id=1, source_target_pairs={{0,1},{1,0},{2,3},{3,2},{4,5},{5,4},{6,7},{7,6},{8,9},{9,8},{10,11... | collective-permute-start | bytes 786440 | tf_op jit(solution)/shard_map/ppermute | solution.py:143

commit v3 on v2

v3 whole, which is shorter than its diff:
```python
import functools

import jax
import jax.numpy as jnp
from jax import lax
from jax.experimental import pallas as pl
from jax.experimental.pallas import tpu as pltpu
from jax.sharding import PartitionSpec as P

RANK = 256
LANES = 128
FAST_WIDE = 8
HIGHEST = lax.Precision.HIGHEST
VMEM_LIMIT = 16 * 1024 * 1024


def split(x):
    high = x.astype(jnp.bfloat16)
    return high, (x - high.astype(jnp.float32)).astype(jnp.bfloat16)


def by_device(place, blocks):
    distance = 1
    while distance < len(blocks):
        flag = (place & distance) != 0
        blocks = [jnp.where(flag, blocks[i ^ distance], blocks[i]) for i in range(len(blocks))]
        distance *= 2
    return blocks


def two_cells(place, refs, t):
    sides = [jnp.concatenate(by_device(place, [r[c] for r in refs]), axis=0) for c in (2 * t, 2 * t + 1)]
    return jnp.concatenate(sides, axis=1)


def rows_dot(a, b, precision=None):
    return lax.dot_general(
        a, b, (((1,), (1,)), ((), ())), precision=precision, preferred_element_type=jnp.float32
    )


def product(a, b):
    (ah, al), (bh, bl) = a, b
    left = jnp.concatenate([ah, ah, al, al], axis=1)
    right = jnp.concatenate([bh, bl, bh, bl], axis=1)
    return rows_dot(left, right)


def read(pair, t):
    return pair[0][t], pair[1][t]


def write(pair, t, value):
    pair[0][t], pair[1][t] = value


def add_to(ref, value):
    ref[...] = ref[...] + value


def start_at_zero(*refs):
    @pl.when(pl.program_id(0) == 0)
    def _():
        for ref in refs:
            ref[...] = jnp.zeros_like(ref)


def own_kernel(place_ref, *refs):
    blocks, (gram_ref, *own) = refs[:-3], refs[-3:]
    start_at_zero(gram_ref)
    for t in range(blocks[0].shape[0] // 2):
        x = split(two_cells(place_ref[0], blocks, t))
        write(own, t, x)
        add_to(gram_ref, product(x, x))


def even_kernel(place_ref, near, far, own_h, own_l, cross_ref, gram_ref, *even):
    start_at_zero(cross_ref, gram_ref)
    place = place_ref[0] // 2
    for t in range(near.shape[0] // 2):
        x = split(two_cells(place, (near, far), t))
        write(even, t, x)
        add_to(cross_ref, product(x, read((own_h, own_l), t)))
        add_to(gram_ref, product(x, x))


def odd_kernel(
    place_ref, own_gram, cross_even, gram_even, near, far, own_h, own_l, even_h, even_l,
    corner_ref, below_ref, odd_h, odd_l, all_ref,
):
    start_at_zero(all_ref)
    place = place_ref[0]
    for t in range(near.shape[0] // 2):
        x = split(two_cells(place // 2, (near, far), t))
        write((odd_h, odd_l), t, x)
        both = jnp.concatenate(x, axis=0)
        n = both.shape[0] // 2
        high = rows_dot(jnp.concatenate([own_h[t], even_h[t], x[0]], axis=0), both)
        low = rows_dot(jnp.concatenate([own_l[t], even_l[t], x[1]], axis=0), both)
        add_to(all_ref, (high[:, :n] + high[:, n:]) + (low[:, :n] + low[:, n:]))

    @pl.when(pl.program_id(0) == pl.num_programs(0) - 1)
    def _():
        n = all_ref.shape[1] // 2
        first_even = (place & 1) == 0

        def interleave(even, odd):
            a = jnp.where(first_even, even, odd)
            b = jnp.where(first_even, odd, even)
            return jnp.concatenate([a[:n], b[:n], a[n:], b[n:]], axis=0)

        low = place < FAST_WIDE // 2
        cross = interleave(cross_even[...], all_ref[:RANK].T)
        mixed = all_ref[RANK : RANK + 2 * n]
        other = interleave(
            jnp.concatenate([gram_even[...], mixed], axis=1),
            jnp.concatenate([mixed.T, all_ref[RANK + 2 * n :]], axis=1),
        ).T
        other = interleave(other[: 2 * n], other[2 * n :])
        corner = jnp.where(low, own_gram[...], other)
        corner_ref[...] = jnp.concatenate(
            [corner[:LANES, :LANES], corner[:LANES, LANES:], corner[LANES:, LANES:]], axis=0
        )
        below_ref[...] = jnp.where(low, cross, cross.T)


def whole(shape):
    return pl.BlockSpec(shape, lambda i: (0,) * len(shape))


def stepped(shape, steps):
    return pl.BlockSpec((shape[0] // steps,) + shape[1:], lambda i: (i,) + (0,) * (len(shape) - 1))


def call(kernel, name, steps, place, kept, streamed, kept_out, streamed_out, scratch=(), flops=0):
    moved = sum(4 * x.size for x in streamed) + sum(2 * s.size for s in streamed_out)
    return pl.pallas_call(
        kernel,
        grid=(steps,),
        in_specs=[pl.BlockSpec(memory_space=pltpu.SMEM)]
        + [whole(x.shape) for x in kept]
        + [stepped(x.shape, steps) for x in streamed],
        out_specs=[whole(s.shape) for s in kept_out] + [stepped(s.shape, steps) for s in streamed_out],
        out_shape=list(kept_out) + list(streamed_out),
        scratch_shapes=list(scratch),
        compiler_params=pltpu.CompilerParams(vmem_limit_bytes=VMEM_LIMIT),
        cost_estimate=pl.CostEstimate(flops=flops, bytes_accessed=moved, transcendentals=0),
        name=name,
    )(place, *kept, *streamed)


def f32(*shape):
    return jax.ShapeDtypeStruct(shape, jnp.float32)


def halves(cells, rows, fields):
    return [jax.ShapeDtypeStruct((cells // 2, rows, 2 * fields), jnp.bfloat16)] * 2


def gram_of_own(place, blocks, steps):
    cells, rows, fields = blocks[0].shape
    n = rows * len(blocks)
    return call(
        own_kernel, "own_gram", steps, place, [], blocks, [f32(n, n)], halves(cells, n, fields),
        flops=8 * n * n * cells * fields,
    )


def gram_of_even(place, near, far, own, steps):
    cells, rows, fields = near.shape
    n = 2 * rows
    return call(
        even_kernel, "even_gram", steps, place, [], [near, far, *own],
        [f32(n, 2 * n), f32(n, n)], halves(cells, n, fields), flops=24 * n * n * cells * fields,
    )


def gram_of_odd(place, kept, near, far, own, even, steps):
    cells, rows, fields = near.shape
    n = 2 * rows
    return call(
        odd_kernel, "odd_gram", steps, place, kept, [near, far, *own, *even],
        [f32(3 * LANES, LANES), f32(RANK, RANK)], halves(cells, n, fields),
        [pltpu.VMEM((4 * n, n), jnp.float32)],
        flops=32 * n * n * cells * fields,
    )


def over(axis, n, distance):
    return functools.partial(lax.ppermute, axis_name=axis, perm=[(i, i ^ distance) for i in range(n)])


def sum_over_all(x, wide, narrow):
    place = lax.axis_index("narrow")
    distances = [1 << b for b in range(narrow.bit_length() - 1)]
    for d in distances:
        side = (place & d) != 0
        n = x.shape[0] // 2
        keep = jnp.where(side, x[n:], x[:n])
        send = jnp.where(side, x[:n], x[n:])
        x = keep + over("narrow", narrow, d)(send)
    for b in range(wide.bit_length() - 1):
        x = x + over("wide", wide, 1 << b)(x)
    for d in reversed(distances):
        side = (place & d) != 0
        got = over("narrow", narrow, d)(x)
        x = jnp.where(side, jnp.concatenate([got, x]), jnp.concatenate([x, got]))
    return x


PANEL = 64
SUB = 8


def refine_rsqrt(d):
    r = lax.rsqrt(d)
    return r * (1.5 - 0.5 * d * r * r)


def from_row(v, i):
    return jnp.broadcast_to(v[i : i + 1, :], (SUB, LANES))


def from_lane(v, c):
    return jnp.broadcast_to(v[:, c : c + 1], (SUB, LANES))


def cholesky_kernel(gram_ref, upper_ref, inverse_ref, work):
    n = upper_ref.shape[0]
    tiles = n // LANES
    groups = PANEL // SUB
    sub = lax.broadcasted_iota(jnp.int32, (SUB, LANES), 0)
    lane = lax.broadcasted_iota(jnp.int32, (SUB, LANES), 1)
    row_id = lax.broadcasted_iota(jnp.int32, (n, n), 0)
    col_id = lax.broadcasted_iota(jnp.int32, (n, n), 1)
    work[:LANES, :LANES] = gram_ref[:LANES]
    work[:LANES, LANES:n] = gram_ref[LANES : 2 * LANES]
    work[LANES:, LANES:n] = gram_ref[2 * LANES :]
    work[:, n:] = jnp.where(row_id == col_id, 1.0, 0.0)
    for top in range(0, n, PANEL):
        t0 = top // LANES
        cols = list(range(t0, tiles)) + [tiles + t for t in range(t0 + 1)]
        rows_of = lambda g: slice(top + SUB * g, top + SUB * (g + 1))
        lanes_of = lambda t: slice(LANES * t, LANES * (t + 1))
        grp = [[work[rows_of(g), lanes_of(t)] for t in cols] for g in range(groups)]
        pivots = [jnp.ones((SUB, LANES), jnp.float32) for _ in range(groups)]
        for g0 in range(groups):
            c0 = (top + SUB * g0) % LANES
            heads = [[from_lane(grp[g][0], c0 + j) for j in range(SUB)] for g in range(g0, groups)]
            for i in range(SUB):
                pivot = from_row(heads[0][i], i)
                pivots[g0] = jnp.where(sub == i, pivot, pivots[g0])
                inverse = pl.reciprocal(pivot, approx=True)
                head_row = {j: from_row(heads[0][j], i) for j in range(i + 1, SUB)}
                row = [from_row(v, i) for v in grp[g0]]
                for g in range(g0, groups):
                    head = heads[g - g0]
                    factor = head[i] * inverse
                    if g == g0:
                        factor = jnp.where(sub > i, factor, 0.0)
                    for j in range(i + 1, SUB):
                        head[j] = head[j] - factor * head_row[j]
                    grp[g] = [v - factor * r for v, r in zip(grp[g], row)]
        for g in range(groups):
            scale = refine_rsqrt(pivots[g])
            for v, t in zip(grp[g], cols):
                v = v * scale
                if t < tiles:
                    v = jnp.where(lane + LANES * t >= sub + (top + SUB * g), v, 0.0)
                work[rows_of(g), lanes_of(t)] = v
        for t in range(t0):
            work[top : top + PANEL, lanes_of(t)] = jnp.zeros((PANEL, LANES), jnp.float32)
        below = top + PANEL
        if below < n:
            lo, hi = LANES * t0, n + LANES * (t0 + 1)
            first = below // LANES * LANES
            update = lax.dot_general(
                work[top:below, first:n],
                work[top:below, lo:hi],
                (((0,), (0,)), ((), ())),
                precision=HIGHEST,
                preferred_element_type=jnp.float32,
            )
            work[below:, lo:hi] = work[below:, lo:hi] - update[below - first :, :]
    upper_ref[...] = work[:, :n]
    inverse_ref[...] = work[:, n:]


def cholesky(packed):
    n = RANK
    return pl.pallas_call(
        cholesky_kernel,
        out_shape=[f32(n, n)] * 2,
        scratch_shapes=[pltpu.VMEM((n, 2 * n), jnp.float32)],
        compiler_params=pltpu.CompilerParams(vmem_limit_bytes=VMEM_LIMIT),
        cost_estimate=pl.CostEstimate(flops=2 * n * n * n, bytes_accessed=12 * n * n, transcendentals=n),
        name="cholesky256",
    )(packed)


def core_kernel(place_ref, below, upper, inverse, own_h, own_l, even_h, even_l, odd_h, odd_l, *rest):
    factor_ref, out_ref, weights = rest

    @pl.when(pl.program_id(0) == 0)
    def _():
        left = upper[...]
        right = rows_dot(inverse[...], below[...], HIGHEST)
        squares = jnp.sum(left * left, axis=1, keepdims=True) + jnp.sum(right * right, axis=1, keepdims=True)
        length = jnp.sqrt(squares)
        left, right = left / length, right / length
        factor_ref[...] = jnp.concatenate([left, right], axis=1).T
        low = place_ref[0] < 4
        own = jnp.where(low, left, right)
        other = jnp.where(low, right, left)
        n = RANK // 4
        first = jnp.concatenate([other[:, :n], other[:, 2 * n : 3 * n]], axis=1)
        second = jnp.concatenate([other[:, n : 2 * n], other[:, 3 * n :]], axis=1)
        first_even = (place_ref[0] & 1) == 0
        even = jnp.where(first_even, first, second)
        odd = jnp.where(first_even, second, first)
        high, small = split(jnp.concatenate([own, even, odd], axis=1))
        weights[...] = jnp.concatenate([high, small, high], axis=1)

    w = weights[...]
    for t in range(own_h.shape[0]):
        high = [r[t] for r in (own_h, even_h, odd_h)]
        small = [r[t] for r in (own_l, even_l, odd_l)]
        both = jnp.dot(w, jnp.concatenate(high + high + small, axis=0), preferred_element_type=jnp.float32)
        out_ref[:, 0, 2 * t, :] = both[:, :LANES]
        out_ref[:, 0, 2 * t + 1, :] = both[:, LANES:]


def core_and_factor(place, kept, streamed, ny, nz, fields):
    size = sum(x.shape[1] for x in streamed) // 2
    return pl.pallas_call(
        core_kernel,
        grid=(ny,),
        in_specs=[pl.BlockSpec(memory_space=pltpu.SMEM)]
        + [whole(x.shape) for x in kept]
        + [stepped(x.shape, ny) for x in streamed],
        out_specs=[whole((size, RANK)), pl.BlockSpec((RANK, 1, nz, fields), lambda i: (0, i, 0, 0))],
        out_shape=[f32(size, RANK), f32(RANK, ny, nz, fields)],
        scratch_shapes=[pltpu.VMEM((RANK, 3 * size), jnp.bfloat16)],
        compiler_params=pltpu.CompilerParams(vmem_limit_bytes=VMEM_LIMIT),
        cost_estimate=pl.CostEstimate(
            flops=6 * size * RANK * ny * nz * fields,
            bytes_accessed=4 * (size + RANK) * ny * nz * fields,
            transcendentals=0,
        ),
        name="core",
    )(place, *kept, *streamed)


def tie(x, *deps):
    return lax.optimization_barrier((x,) + deps)[0]


def block_for(snapshot, device, nz):
    rows, ny, _, fields = snapshot.shape
    cut = lax.dynamic_slice_in_dim(snapshot, device * nz, nz, axis=2)
    return cut.transpose(1, 2, 0, 3).reshape(ny * nz, rows, fields)


def on_device_blocks(snapshot, wide, narrow):
    ny, nz = snapshot.shape[1], snapshot.shape[2] // wide
    here = lax.axis_index("wide")
    place = here.astype(jnp.int32).reshape(1)
    first = block_for(snapshot, here ^ 6, nz)
    snapshot = tie(snapshot, first)
    got = {}
    send = lambda k, *deps: over("wide", wide, k)(tie(block_for(snapshot, here ^ k, nz), *deps))
    got[6] = over("wide", wide, 6)(first)
    got[4], got[7], got[2] = send(4), send(7), send(2)
    got[5] = send(5, got[6])
    got[3] = send(3, got[2])
    got[1] = send(1, got[6])
    got[0] = block_for(snapshot, here, nz)
    own_gram, *own = gram_of_own(place, [got[k] for k in range(4)], ny)
    cross_even, gram_even, *even = gram_of_even(place, got[4], got[6], own, ny)
    corner, below, *odd = gram_of_odd(place, [own_gram, cross_even, gram_even], got[5], got[7], own, even, ny)
    corner = sum_over_all(corner, wide, narrow)
    below = sum_over_all(below, wide, narrow)
    upper, inverse = cholesky(corner)
    factor, core = core_and_factor(
        place, [below, upper, inverse], [*own, *even, *odd], ny, nz, snapshot.shape[3]
    )
    return core, factor


def on_device_any(snapshot):
    regrouped = lax.all_to_all(snapshot, "wide", split_axis=2, concat_axis=0, tiled=True)
    rows_all = regrouped.shape[0]
    unfold = regrouped.reshape(rows_all, -1)
    gram = lax.dot_general(
        unfold, unfold[:RANK], (((1,), (1,)), ((), ())), precision=HIGHEST, preferred_element_type=jnp.float32
    )
    gram = lax.psum(lax.psum(gram, "narrow"), "wide")
    lower = jnp.linalg.cholesky(gram[:RANK])
    upper = jnp.concatenate(
        [lower.T, lax.linalg.triangular_solve(lower, gram[RANK:].T, left_side=True, lower=True)], axis=1
    )
    lengths = jnp.sqrt(jnp.sum(upper * upper, axis=1))
    factor = (upper / lengths[:, None]).T
    core = jnp.dot(factor.T, unfold, precision=HIGHEST, preferred_element_type=jnp.float32)
    return core.reshape((RANK,) + regrouped.shape[1:]), factor


def solution(mesh):
    wide, narrow = mesh.shape["wide"], mesh.shape["narrow"]
    if wide == FAST_WIDE:
        on_device = functools.partial(on_device_blocks, wide=wide, narrow=narrow)
    else:
        on_device = on_device_any
    return jax.shard_map(
        on_device,
        mesh=mesh,
        in_specs=(P("wide", "narrow", None, None),),
        out_specs=(P(None, "narrow", "wide", None), P()),
        check_vma=False,
    )
```

time: 255 us -> 245 us (0.961)
  waiting for transfers between devices: 181 us -> 164 us
  starting transfers between devices: 23.3 us -> 31.6 us
  Pallas kernels: 33.2 us -> 28.9 us
  local copies, waits for them, and re-layouts: 15.3 us -> 19 us
    ppermute x6, waiting for transfers between devices: 146 us -> 140 us  [on_device_blocks(): over('wide', wide, k)(tie(block_for(snapshot, here ^ k, nz), *deps))]
    ppermute x3 -> x6, waiting for transfers between devices: 11.4 us -> 6.09 us  [sum_over_all(): x = x + over('wide', wide, 1 << b)(x)]
    ppermute x2 -> x4, starting transfers between devices: 6.82 us -> 11.6 us  [sum_over_all(): got = over('narrow', narrow, d)(x)]
    ppermute x3 -> x6, starting transfers between devices: 2.35 us -> 5.38 us  [sum_over_all(): x = x + over('wide', wide, 1 << b)(x)]
    ppermute x2 -> x4, waiting for transfers between devices: 3.78 us -> 0.76 us  [sum_over_all(): got = over('narrow', narrow, d)(x)]
    pallas_call x1, Pallas kernels: 9.73 us -> 7.15 us  [core_and_factor(): pl.pallas_call(core_kernel, grid=(ny,), in_specs=[pl.BlockSpec(memory_spa...]
    pallas_call x3 -> x4, Pallas kernels: 23.4 us -> 21.7 us  [the longest x3 13.4 us: call(): pl.pallas_call(kernel, grid=(steps,), in_specs=[pl.BlockSpec(memory_space...]
  transfers between devices with their start and end apart: 14 -> 21, of which waited for: 12 -> 13; matrix products, arithmetic and copies ran while one was open for 5% -> 7% of each run, Pallas kernels for 2% -> 8%
where the time goes in v3:
time: 245 us; the launch traced here: 244 us
  waiting for transfers between devices  164 us (67%)
  starting transfers between devices  31.6 us (13%)
  Pallas kernels  28.9 us (12%)
  local copies, waits for them, and re-layouts  19 us (8%)
    ppermute x6, waiting for transfers between devices, on_device_blocks(): over('wide', wide, k)(tie(block_for(snapshot, here ^ k, nz), *deps))  140 us
    transpose x10, local copies, waits for them, and re-layouts, block_for(): return cut.transpose(1, 2, 0, 3).reshape(ny * nz, rows, fields)  17.8 us
    ppermute x1, waiting for transfers between devices, on_device_blocks(): got[6] = over('wide', wide, 6)(first)  13.6 us
    pallas_call x3, Pallas kernels, call(): pl.pallas_call(kernel, grid=(steps,), in_specs=[pl.BlockSpec(memory_space...  13.4 us
    ppermute x4, starting transfers between devices, sum_over_all(): got = over('narrow', narrow, d)(x)  11.6 us
    pallas_call x1, Pallas kernels, cholesky(): pl.pallas_call(cholesky_kernel, out_shape=[f32(n, n)] * 2, scratch_shapes...  8.36 us
    pallas_call x1, Pallas kernels, core_and_factor(): pl.pallas_call(core_kernel, grid=(ny,), in_specs=[pl.BlockSpec(memory_spa...  7.15 us
    ppermute x6, starting transfers between devices, on_device_blocks(): over('wide', wide, k)(tie(block_for(snapshot, here ^ k, nz), *deps))  6.79 us
  transfers between devices with their start and end apart: 21, of which 13 were waited for; matrix products, arithmetic and copies ran while one was open for 7% of the time, Pallas kernels for 8%

profile of v3, /device:TPU:1, one launch (start us, length us, event | category | flops | bytes accessed | tf_op | source)
XLA Modules:
  0.0 244.3 jit_solution(16241739640348266655)
XLA Ops:
  0.6 1.3 dynamic-slice_bitcast_fusion.7
  2.6 4.2 %collective-permute-start = (f32[32,64,128]{2,1,0:T(8,128)S(1)}, f32[32,64,128]{2,1,0:T(8,128)S(1)}, u32[]{:S(2)}, u32[]{:S(2)}) collective-permute-start(f32[32,64,128]{2,1,0:T(8,128)S(1)} %bitcast.26), channel_id=1, source_target_pairs={{0,24},{4,28},{8,16},{12,20},{16,8},{20,12},{24,0},{28,4},{1,25},{... | collective-permute-start | bytes 3145736 | tf_op jit(solution)/shard_map/ppermute | solution.py:372
  6.8 5.4 %dynamic-slice_bitcast_fusion = (f32[4,8,64,128]{3,1,0,2:T(8,128)S(1)}, f32[4,8,64,128]{3,1,0,2:T(8,128)S(1)}, f32[4,8,64,128]{3,1,0,2:T(8,128)S(1)}, f32[4,8,64...) fusion(f32[64,4,64,128]{3,2,1,0:T(8,128)} %param.1, ...), kind=kLoop, calls=%fused_computation | loop fusion | bytes 14680092 | tf_op jit(solution)/shard_map/transpose | solution.py:361
  12.9 1.6 copy.7
  14.5 1.7 copy.5
  16.2 13.6 %collective-permute-done.far = f32[32,64,128]{2,1,0:T(8,128)S(1)} collective-permute-done((f32[32,64,128]{2,1,0:T(8,128)S(1)}, f32[32,64,128]{2,1,0:T(8,128)S(1)}, u32[]{:S(2)}, u32[]{:S(2)}) %collective-permute-start) | collective-permute-done | bytes 1048608 | tf_op jit(solution)/shard_map/ppermute | solution.py:372
  30.8 22.3 %collective-permute-done.2.refs_2_ = f32[32,64,128]{2,1,0:T(8,128)S(1)} collective-permute-done((f32[32,64,128]{2,1,0:T(8,128)S(1)}, f32[32,64,128]{2,1,0:T(8,128)S(1)}, u32[]{:S(2)}, u32[]{:S(2)}) %collective-permute-start.2) | collective-permute-done | bytes 1048608 | tf_op jit(solution)/shard_map/ppermute | solution.py:371
  54.3 1.6 copy.8
  55.9 3.2 %collective-permute-start.4 = (f32[32,64,128]{2,1,0:T(8,128)}, f32[32,64,128]{2,1,0:T(8,128)}, u32[]{:S(2)}, u32[]{:S(2)}) collective-permute-start(f32[32,64,128]{2,1,0:T(8,128)} %bitcast.12), channel_id=1, source_target_pairs={{0,16},{4,20},{8,24},{12,28},{16,0},{20,4},{24,8},{28,12},{1,17},{... | collective-permute-start | bytes 3145736 | tf_op jit(solution)/shard_map/ppermute | solution.py:371
  59.1 1.6 copy.10
  60.7 1.6 copy.9
  63.5 1.8 copy.4
  65.4 34.0 %collective-permute-done.3.refs_3_ = f32[32,64,128]{2,1,0:T(8,128)} collective-permute-done((f32[32,64,128]{2,1,0:T(8,128)}, f32[32,64,128]{2,1,0:T(8,128)}, u32[]{:S(2)}, u32[]{:S(2)}) %collective-permute-start.3) | collective-permute-done | bytes 1048608 | tf_op jit(solution)/shard_map/ppermute | solution.py:371
  100.6 4.7 %own_gram.1 = (f32[256,256]{1,0:T(8,128)S(1)}, bf16[16,256,256]{2,1,0:T(8,128)(2,1)S(1)}, bf16[16,256,256]{2,1,0:T(8,128)(2,1)S(1)}) custom-call(s32[1]{0:T(128)} %bitcast.place_ref, f32[32,64,128]{2,1,0:T(8,128)S(1)} %bitcast.25, f32[32,64,128]{2,1,0:T(8,128)} %collective-permute-done.1.refs_1_, f32[32,64,128]{2,1,0:T(8,128)S(1)} %copy-done.1, ...), custom_call_target="tpu_custom_call" | custom-call | flops 2147483648 | bytes 8388608 | tf_op jit(solution)/shard_map/own_gram/pallas_call | solution.py:137
  105.3 43.9 %collective-permute-done.4.near = f32[32,64,128]{2,1,0:T(8,128)} collective-permute-done((f32[32,64,128]{2,1,0:T(8,128)}, f32[32,64,128]{2,1,0:T(8,128)}, u32[]{:S(2)}, u32[]{:S(2)}) %collective-permute-start.4) | collective-permute-done | bytes 1048608 | tf_op jit(solution)/shard_map/ppermute | solution.py:371
  149.2 5.2 %even_gram.1 = (f32[128,256]{1,0:T(8,128)S(1)}, f32[128,128]{1,0:T(8,128)S(1)}, bf16[16,128,256]{2,1,0:T(8,128)(2,1)S(1)}, bf16[16,128,256]{2,1,0:T(8,128)(2,1)S(1)}) custom-call(s32[1]{0:T(128)} %bitcast.place_ref, f32[32,64,128]{2,1,0:T(8,128)} %collective-permute-done.4.near, f32[32,64,128]{2,1,0:T(8,128)S(1)} %collective-permute-done.far, ...), custom_call_target="tpu_custom_call" | custom-call | flops 1610612736 | bytes 12582912 | tf_op jit(solution)/shard_map/even_gram/pallas_call | solution.py:137
  154.5 39.5 %collective-permute-done.5.near = f32[32,64,128]{2,1,0:T(8,128)S(1)} collective-permute-done((f32[32,64,128]{2,1,0:T(8,128)}, f32[32,64,128]{2,1,0:T(8,128)S(1)}, u32[]{:S(2)}, u32[]{:S(2)}) %collective-permute-start.5) | collective-permute-done | bytes 1048608 | tf_op jit(solution)/shard_map/ppermute | solution.py:371
  194.0 3.4 %odd_gram.1 = (f32[384,128]{1,0:T(8,128)S(1)}, f32[256,256]{1,0:T(8,128)S(1)}, bf16[16,128,256]{2,1,0:T(8,128)(2,1)S(1)}, bf16[16,128,256]{2,1,0:T(8,128)(2,1)S(1)}) custom-call(s32[1]{0:T(128)} %bitcast.place_ref, f32[256,256]{1,0:T(8,128)S(1)} %get-tuple-element.24.own_gram, f32[128,256]{1,0:T(8,128)S(1)} %get-tuple-element.27.cross_even, ...), custom_call_target="tpu_custom_call" | custom-call | flops 2147483648 | bytes 16777216 | tf_op jit(solution)/shard_map/odd_gram/pallas_call | solution.py:137
  197.4 1.9 collective-permute-start.14
  200.3 1.3 collective-permute-start.15
  203.3 1.5 collective-permute-done.8
  204.8 1.3 collective-permute-start.9
  206.4 2.7 %collective-permute-done.16 = f32[96,128]{1,0:T(8,128)S(1)} collective-permute-done((f32[96,128]{1,0:T(8,128)S(1)}, f32[96,128]{1,0:T(8,128)S(1)}, u32[]{:S(2)}, u32[]{:S(2)}) %collective-permute-start.16) | collective-permute-done | bytes 49184 | tf_op jit(solution)/shard_map/ppermute | solution.py:203
  209.2 1.5 collective-permute-start.10
  210.7 1.4 collective-permute-done.17
  212.8 1.8 collective-permute-start.11
  214.6 1.8 collective-permute-done.18
  216.4 1.6 collective-permute-start.19
  219.4 6.8 %collective-permute-start.20 = (f32[192,128]{1,0:T(8,128)S(1)}, f32[192,128]{1,0:T(8,128)S(1)}, u32[]{:S(2)}, u32[]{:S(2)}) collective-permute-start(f32[192,128]{1,0:T(8,128)S(1)} %maximum_select_fusion.3), channel_id=1, source_target_pairs={{0,1},{1,0},{2,3},{3,2},{4,5},{5,4},{6,7},{7,6},{8,9},{9,8},{10,11... | collective-permute-start | bytes 294920 | tf_op jit(solution)/shard_map/ppermute | solution.py:206
  226.2 2.5 %collective-permute-start.13 = (f32[128,256]{1,0:T(8,128)S(1)}, f32[128,256]{1,0:T(8,128)S(1)}, u32[]{:S(2)}, u32[]{:S(2)}) collective-permute-start(f32[128,256]{1,0:T(8,128)S(1)} %maximum_select_fusion.2), channel_id=1, source_target_pairs={{0,1},{1,0},{2,3},{3,2},{4,5},{5,4},{6,7},{7,6},{8,9},{9,8},{10,11... | collective-permute-start | bytes 393224 | tf_op jit(solution)/shard_map/ppermute | solution.py:206
  228.8 8.4 %cholesky256.1 = (f32[256,256]{1,0:T(8,128)S(1)}, f32[256,256]{1,0:T(8,128)S(1)}) custom-call(f32[384,128]{1,0:T(8,128)S(1)} %maximum_select_fusion.1.gram_ref), custom_call_target="tpu_custom_call" | custom-call | flops 33554432 | bytes 786432 | tf_op jit(solution)/shard_map/cholesky256/pallas_call | solution.py:291
  237.2 7.2 %core.1 = (f32[512,256]{1,0:T(8,128)}, f32[256,4,8,128]{3,2,1,0:T(8,128)}) custom-call(s32[1]{0:T(128)} %bitcast.place_ref, f32[256,256]{1,0:T(8,128)S(1)} %maximum_select_fusion.below, f32[256,256]{1,0:T(8,128)S(1)} %get-tuple-element.34.upper, f32[256,256]{1,0:T(8,128)S(1)} %get-tuple-element.35.inverse, ...), custom_call_target="tpu_custom_call" | custom-call | flops 3221225472 | bytes 12582912 | tf_op jit(solution)/shard_map/core/pallas_call | solution.py:335
  (47 shorter events, 11.3 us)
Async XLA Ops:
  2.6 27.2 %collective-permute-start = (f32[32,64,128]{2,1,0:T(8,128)S(1)}, f32[32,64,128]{2,1,0:T(8,128)S(1)}, u32[]{:S(2)}, u32[]{:S(2)}) collective-permute-start(f32[32,64,128]{2,1,0:T(8,128)S(1)} %bitcast.26), channel_id=1, source_target_pairs={{0,24},{4,28},{8,16},{12,20},{16,8},{20,12},{24,0},{28,4},{1,25},{... | collective-permute-start | bytes 3145736 | tf_op jit(solution)/shard_map/ppermute | solution.py:372
  12.8 40.3 %collective-permute-start.2 = (f32[32,64,128]{2,1,0:T(8,128)S(1)}, f32[32,64,128]{2,1,0:T(8,128)S(1)}, u32[]{:S(2)}, u32[]{:S(2)}) collective-permute-start(f32[32,64,128]{2,1,0:T(8,128)S(1)} %bitcast.27), channel_id=1, source_target_pairs={{0,8},{4,12},{8,0},{12,4},{16,24},{20,28},{24,16},{28,20},{1,9},{5... | collective-permute-start | bytes 3145736 | tf_op jit(solution)/shard_map/ppermute | solution.py:371
  29.8 35.6 %collective-permute-start.1 = (f32[32,64,128]{2,1,0:T(8,128)}, f32[32,64,128]{2,1,0:T(8,128)}, u32[]{:S(2)}, u32[]{:S(2)}) collective-permute-start(f32[32,64,128]{2,1,0:T(8,128)} %bitcast.6), channel_id=1, source_target_pairs={{0,4},{4,0},{8,12},{12,8},{16,20},{20,16},{24,28},{28,24},{1,5},{5... | collective-permute-start | bytes 3145736 | tf_op jit(solution)/shard_map/ppermute | solution.py:371
  53.1 9.2 %copy-start = (f32[32,64,128]{2,1,0:T(8,128)}, f32[32,64,128]{2,1,0:T(8,128)S(1)}, u32[]{:S(2)}) copy-start(f32[32,64,128]{2,1,0:T(8,128)S(1)} %collective-permute-done.2.refs_2_) | copy-start | bytes 3145732
  53.1 46.3 %collective-permute-start.3 = (f32[32,64,128]{2,1,0:T(8,128)}, f32[32,64,128]{2,1,0:T(8,128)}, u32[]{:S(2)}, u32[]{:S(2)}) collective-permute-start(f32[32,64,128]{2,1,0:T(8,128)} %bitcast.10), channel_id=1, source_target_pairs={{0,12},{4,8},{8,4},{12,0},{16,28},{20,24},{24,20},{28,16},{1,13},{... | collective-permute-start | bytes 3145736 | tf_op jit(solution)/shard_map/ppermute | solution.py:371
  55.9 93.3 %collective-permute-start.4 = (f32[32,64,128]{2,1,0:T(8,128)}, f32[32,64,128]{2,1,0:T(8,128)}, u32[]{:S(2)}, u32[]{:S(2)}) collective-permute-start(f32[32,64,128]{2,1,0:T(8,128)} %bitcast.12), channel_id=1, source_target_pairs={{0,16},{4,20},{8,24},{12,28},{16,0},{20,4},{24,8},{28,12},{1,17},{... | collective-permute-start | bytes 3145736 | tf_op jit(solution)/shard_map/ppermute | solution.py:371
  60.7 93.8 %collective-permute-start.6 = (f32[32,64,128]{2,1,0:T(8,128)}, f32[32,64,128]{2,1,0:T(8,128)S(1)}, u32[]{:S(2)}, u32[]{:S(2)}) collective-permute-start(f32[32,64,128]{2,1,0:T(8,128)} %bitcast.16), channel_id=1, source_target_pairs={{0,28},{4,24},{8,20},{12,16},{16,12},{20,8},{24,4},{28,0},{1,29},{... | collective-permute-start | bytes 3145736 | tf_op jit(solution)/shard_map/ppermute | solution.py:371
  62.3 131.7 %collective-permute-start.5 = (f32[32,64,128]{2,1,0:T(8,128)}, f32[32,64,128]{2,1,0:T(8,128)S(1)}, u32[]{:S(2)}, u32[]{:S(2)}) collective-permute-start(f32[32,64,128]{2,1,0:T(8,128)} %bitcast.14), channel_id=1, source_target_pairs={{0,20},{4,16},{8,28},{12,24},{16,4},{20,0},{24,12},{28,8},{1,21},{... | collective-permute-start | bytes 3145736 | tf_op jit(solution)/shard_map/ppermute | solution.py:371
  99.4 1.2 copy-start.1
  197.4 2.8 %collective-permute-start.14 = (f32[192,128]{1,0:T(8,128)S(1)}, f32[192,128]{1,0:T(8,128)S(1)}, u32[]{:S(2)}, u32[]{:S(2)}) collective-permute-start(f32[192,128]{1,0:T(8,128)S(1)} %slice_select_fusion.1), channel_id=1, source_target_pairs={{0,1},{1,0},{2,3},{3,2},{4,5},{5,4},{6,7},{7,6},{8,9},{9,8},{10,11... | collective-permute-start | bytes 294920 | tf_op jit(solution)/shard_map/ppermute | solution.py:201
  199.3 2.3 collective-permute-start.7
  200.3 3.0 %collective-permute-start.15 = (f32[96,128]{1,0:T(8,128)S(1)}, f32[96,128]{1,0:T(8,128)S(1)}, u32[]{:S(2)}, u32[]{:S(2)}) collective-permute-start(f32[96,128]{1,0:T(8,128)S(1)} %slice_select_fusion.3), channel_id=1, source_target_pairs={{0,2},{1,3},{2,0},{3,1},{4,6},{5,7},{6,4},{7,5},{8,10},{9,11},{10,... | collective-permute-start | bytes 147464 | tf_op jit(solution)/shard_map/ppermute | solution.py:201
  201.6 3.2 %collective-permute-start.8 = (f32[64,256]{1,0:T(8,128)S(1)}, f32[64,256]{1,0:T(8,128)S(1)}, u32[]{:S(2)}, u32[]{:S(2)}) collective-permute-start(f32[64,256]{1,0:T(8,128)S(1)} %slice_select_fusion.2), channel_id=1, source_target_pairs={{0,2},{1,3},{2,0},{3,1},{4,6},{5,7},{6,4},{7,5},{8,10},{9,11},{10,... | collective-permute-start | bytes 196616 | tf_op jit(solution)/shard_map/ppermute | solution.py:201
  204.8 4.3 %collective-permute-start.9 = (f32[64,256]{1,0:T(8,128)S(1)}, f32[64,256]{1,0:T(8,128)S(1)}, u32[]{:S(2)}, u32[]{:S(2)}) collective-permute-start(f32[64,256]{1,0:T(8,128)S(1)} %select_add_fusion.2), channel_id=1, source_target_pairs={{0,4},{4,0},{8,12},{12,8},{16,20},{20,16},{24,28},{28,24},{1,5},{5... | collective-permute-start | bytes 196616 | tf_op jit(solution)/shard_map/ppermute | solution.py:203
  206.1 2.9 %collective-permute-start.16 = (f32[96,128]{1,0:T(8,128)S(1)}, f32[96,128]{1,0:T(8,128)S(1)}, u32[]{:S(2)}, u32[]{:S(2)}) collective-permute-start(f32[96,128]{1,0:T(8,128)S(1)} %select_add_fusion.3), channel_id=1, source_target_pairs={{0,4},{4,0},{8,12},{12,8},{16,20},{20,16},{24,28},{28,24},{1,5},{5... | collective-permute-start | bytes 147464 | tf_op jit(solution)/shard_map/ppermute | solution.py:203
  209.1 3.0 %collective-permute-start.17 = (f32[96,128]{1,0:T(8,128)S(1)}, f32[96,128]{1,0:T(8,128)S(1)}, u32[]{:S(2)}, u32[]{:S(2)}) collective-permute-start(f32[96,128]{1,0:T(8,128)S(1)} %add.69), channel_id=1, source_target_pairs={{0,8},{4,12},{8,0},{12,4},{16,24},{20,28},{24,16},{28,20},{1,9},{5... | collective-permute-start | bytes 147464 | tf_op jit(solution)/shard_map/ppermute | solution.py:203
  209.2 3.6 %collective-permute-start.10 = (f32[64,256]{1,0:T(8,128)S(1)}, f32[64,256]{1,0:T(8,128)S(1)}, u32[]{:S(2)}, u32[]{:S(2)}) collective-permute-start(f32[64,256]{1,0:T(8,128)S(1)} %add.64), channel_id=1, source_target_pairs={{0,8},{4,12},{8,0},{12,4},{16,24},{20,28},{24,16},{28,20},{1,9},{5... | collective-permute-start | bytes 196616 | tf_op jit(solution)/shard_map/ppermute | solution.py:203
  212.1 4.3 %collective-permute-start.18 = (f32[96,128]{1,0:T(8,128)S(1)}, f32[96,128]{1,0:T(8,128)S(1)}, u32[]{:S(2)}, u32[]{:S(2)}) collective-permute-start(f32[96,128]{1,0:T(8,128)S(1)} %add.70), channel_id=1, source_target_pairs={{0,16},{4,20},{8,24},{12,28},{16,0},{20,4},{24,8},{28,12},{1,17},{... | collective-permute-start | bytes 147464 | tf_op jit(solution)/shard_map/ppermute | solution.py:203
  212.8 5.1 %collective-permute-start.11 = (f32[64,256]{1,0:T(8,128)S(1)}, f32[64,256]{1,0:T(8,128)S(1)}, u32[]{:S(2)}, u32[]{:S(2)}) collective-permute-start(f32[64,256]{1,0:T(8,128)S(1)} %add.65), channel_id=1, source_target_pairs={{0,16},{4,20},{8,24},{12,28},{16,0},{20,4},{24,8},{28,12},{1,17},{... | collective-permute-start | bytes 196616 | tf_op jit(solution)/shard_map/ppermute | solution.py:203
  216.4 3.0 %collective-permute-start.19 = (f32[96,128]{1,0:T(8,128)S(1)}, f32[96,128]{1,0:T(8,128)S(1)}, u32[]{:S(2)}, u32[]{:S(2)}) collective-permute-start(f32[96,128]{1,0:T(8,128)S(1)} %add.71), channel_id=1, source_target_pairs={{0,2},{1,3},{2,0},{3,1},{4,6},{5,7},{6,4},{7,5},{8,10},{9,11},{10,... | collective-permute-start | bytes 147464 | tf_op jit(solution)/shard_map/ppermute | solution.py:206
  217.9 8.3 %collective-permute-start.12 = (f32[64,256]{1,0:T(8,128)S(1)}, f32[64,256]{1,0:T(8,128)S(1)}, u32[]{:S(2)}, u32[]{:S(2)}) collective-permute-start(f32[64,256]{1,0:T(8,128)S(1)} %add.66), channel_id=1, source_target_pairs={{0,2},{1,3},{2,0},{3,1},{4,6},{5,7},{6,4},{7,5},{8,10},{9,11},{10,... | collective-permute-start | bytes 196616 | tf_op jit(solution)/shard_map/ppermute | solution.py:206
  219.4 9.3 %collective-permute-start.20 = (f32[192,128]{1,0:T(8,128)S(1)}, f32[192,128]{1,0:T(8,128)S(1)}, u32[]{:S(2)}, u32[]{:S(2)}) collective-permute-start(f32[192,128]{1,0:T(8,128)S(1)} %maximum_select_fusion.3), channel_id=1, source_target_pairs={{0,1},{1,0},{2,3},{3,2},{4,5},{5,4},{6,7},{7,6},{8,9},{9,8},{10,11... | collective-permute-start | bytes 294920 | tf_op jit(solution)/shard_map/ppermute | solution.py:206
  226.2 10.9 %collective-permute-start.13 = (f32[128,256]{1,0:T(8,128)S(1)}, f32[128,256]{1,0:T(8,128)S(1)}, u32[]{:S(2)}, u32[]{:S(2)}) collective-permute-start(f32[128,256]{1,0:T(8,128)S(1)} %maximum_select_fusion.2), channel_id=1, source_target_pairs={{0,1},{1,0},{2,3},{3,2},{4,5},{5,4},{6,7},{7,6},{8,9},{9,8},{10,11... | collective-permute-start | bytes 393224 | tf_op jit(solution)/shard_map/ppermute | solution.py:206

commit v4 on v3

--- a/solution.py
+++ b/solution.py
@@ -370,10 +370,10 @@
     got = {}
     send = lambda k, *deps: over("wide", wide, k)(tie(block_for(snapshot, here ^ k, nz), *deps))
     got[6] = over("wide", wide, 6)(first)
-    got[4], got[7], got[2] = send(4), send(7), send(2)
+    got[4], got[2], got[1] = send(4), send(2), send(1)
+    got[3] = send(3, got[6])
     got[5] = send(5, got[6])
-    got[3] = send(3, got[2])
-    got[1] = send(1, got[6])
+    got[7] = send(7, got[4])
     got[0] = block_for(snapshot, here, nz)
     own_gram, *own = gram_of_own(place, [got[k] for k in range(4)], ny)
     cross_even, gram_even, *even = gram_of_even(place, got[4], got[6], own, ny)

time: 245 us -> 240 us (0.980)
  waiting for transfers between devices: 164 us -> 117 us
  starting transfers between devices: 31.6 us -> 74.7 us
    ppermute x6, waiting for transfers between devices: 140 us -> 96.1 us  [on_device_blocks(): over('wide', wide, k)(tie(block_for(snapshot, here ^ k, nz), *deps))]
    ppermute x6, starting transfers between devices: 6.79 us -> 49.7 us  [on_device_blocks(): over('wide', wide, k)(tie(block_for(snapshot, here ^ k, nz), *deps))]
    ppermute x1, waiting for transfers between devices: 13.6 us -> 10.3 us  [on_device_blocks(): got[6] = over('wide', wide, 6)(first)]
  transfers between devices with their start and end apart: 21 -> 21, of which waited for: 13 -> 12; matrix products, arithmetic and copies ran while one was open for 7% -> 7% of each run, Pallas kernels for 8% -> 7%
where the time goes in v4:
time: 240 us
  waiting for transfers between devices  117 us (49%)
  starting transfers between devices  74.7 us (31%)
  Pallas kernels  29.3 us (12%)
  local copies, waits for them, and re-layouts  17.9 us (7%)
    ppermute x6, waiting for transfers between devices, on_device_blocks(): over('wide', wide, k)(tie(block_for(snapshot, here ^ k, nz), *deps))  96.1 us
    ppermute x6, starting transfers between devices, on_device_blocks(): over('wide', wide, k)(tie(block_for(snapshot, here ^ k, nz), *deps))  49.7 us
    transpose x10, local copies, waits for them, and re-layouts, block_for(): return cut.transpose(1, 2, 0, 3).reshape(ny * nz, rows, fields)  17.9 us
    pallas_call x3, Pallas kernels, call(): pl.pallas_call(kernel, grid=(steps,), in_specs=[pl.BlockSpec(memory_space...  13.8 us
    ppermute x4, starting transfers between devices, sum_over_all(): got = over('narrow', narrow, d)(x)  11.4 us
    ppermute x1, waiting for transfers between devices, on_device_blocks(): got[6] = over('wide', wide, 6)(first)  10.3 us
    pallas_call x1, Pallas kernels, cholesky(): pl.pallas_call(cholesky_kernel, out_shape=[f32(n, n)] * 2, scratch_shapes...  8.36 us
    pallas_call x1, Pallas kernels, core_and_factor(): pl.pallas_call(core_kernel, grid=(ny,), in_specs=[pl.BlockSpec(memory_spa...  7.15 us
  transfers between devices with their start and end apart: 21, of which 12 were waited for; matrix products, arithmetic and copies ran while one was open for 7% of the time, Pallas kernels for 7%

profile of v4, /device:TPU:1, one launch (start us, length us, event | category | flops | bytes accessed | tf_op | source)
XLA Modules:
  0.0 239.9 jit_solution(7601496961129993782)
XLA Ops:
  0.6 1.3 dynamic-slice_bitcast_fusion.7
  2.6 4.2 %collective-permute-start.2 = (f32[32,64,128]{2,1,0:T(8,128)S(1)}, f32[32,64,128]{2,1,0:T(8,128)S(1)}, u32[]{:S(2)}, u32[]{:S(2)}) collective-permute-start(f32[32,64,128]{2,1,0:T(8,128)S(1)} %bitcast.26), channel_id=1, source_target_pairs={{0,24},{4,28},{8,16},{12,20},{16,8},{20,12},{24,0},{28,4},{1,25},{... | collective-permute-start | bytes 3145736 | tf_op jit(solution)/shard_map/ppermute | solution.py:372
  6.8 5.4 %dynamic-slice_bitcast_fusion = (f32[4,8,64,128]{3,1,0,2:T(8,128)S(1)}, f32[4,8,64,128]{3,1,0,2:T(8,128)S(1)}, f32[4,8,64,128]{3,1,0,2:T(8,128)S(1)}, f32[4,8,64...) fusion(f32[64,4,64,128]{3,2,1,0:T(8,128)} %param.1, ...), kind=kLoop, calls=%fused_computation | loop fusion | bytes 14680092 | tf_op jit(solution)/shard_map/transpose | solution.py:361
  12.9 1.6 copy.5
  15.7 1.7 copy.6
  17.7 1.7 copy.7
  19.4 10.3 %collective-permute-done.2.far = f32[32,64,128]{2,1,0:T(8,128)S(1)} collective-permute-done((f32[32,64,128]{2,1,0:T(8,128)S(1)}, f32[32,64,128]{2,1,0:T(8,128)S(1)}, u32[]{:S(2)}, u32[]{:S(2)}) %collective-permute-start.2) | collective-permute-done | bytes 1048608 | tf_op jit(solution)/shard_map/ppermute | solution.py:372
  29.8 45.2 %collective-permute-start.3 = (f32[32,64,128]{2,1,0:T(8,128)}, f32[32,64,128]{2,1,0:T(8,128)}, u32[]{:S(2)}, u32[]{:S(2)}) collective-permute-start(f32[32,64,128]{2,1,0:T(8,128)} %bitcast.10), channel_id=1, source_target_pairs={{0,12},{4,8},{8,4},{12,0},{16,28},{20,24},{24,20},{28,16},{1,13},{... | collective-permute-start | bytes 3145736 | tf_op jit(solution)/shard_map/ppermute | solution.py:371
  74.9 1.6 copy.10
  76.5 1.6 copy.9
  78.1 18.0 %collective-permute-done.4.near = f32[32,64,128]{2,1,0:T(8,128)S(1)} collective-permute-done((f32[32,64,128]{2,1,0:T(8,128)S(1)}, f32[32,64,128]{2,1,0:T(8,128)S(1)}, u32[]{:S(2)}, u32[]{:S(2)}) %collective-permute-start.4) | collective-permute-done | bytes 1048608 | tf_op jit(solution)/shard_map/ppermute | solution.py:371
  96.1 2.9 %collective-permute-start.6 = (f32[32,64,128]{2,1,0:T(8,128)}, f32[32,64,128]{2,1,0:T(8,128)S(1)}, u32[]{:S(2)}, u32[]{:S(2)}) collective-permute-start(f32[32,64,128]{2,1,0:T(8,128)} %bitcast.16), channel_id=1, source_target_pairs={{0,28},{4,24},{8,20},{12,16},{16,12},{20,8},{24,4},{28,0},{1,29},{... | collective-permute-start | bytes 3145736 | tf_op jit(solution)/shard_map/ppermute | solution.py:371
  99.1 1.8 copy.4
  100.9 41.9 %collective-permute-done.3.refs_3_ = f32[32,64,128]{2,1,0:T(8,128)} collective-permute-done((f32[32,64,128]{2,1,0:T(8,128)}, f32[32,64,128]{2,1,0:T(8,128)}, u32[]{:S(2)}, u32[]{:S(2)}) %collective-permute-start.3) | collective-permute-done | bytes 1048608 | tf_op jit(solution)/shard_map/ppermute | solution.py:371
  142.8 4.9 %own_gram.1 = (f32[256,256]{1,0:T(8,128)S(1)}, bf16[16,256,256]{2,1,0:T(8,128)(2,1)S(1)}, bf16[16,256,256]{2,1,0:T(8,128)(2,1)S(1)}) custom-call(s32[1]{0:T(128)} %bitcast.place_ref, f32[32,64,128]{2,1,0:T(8,128)S(1)} %bitcast.25, f32[32,64,128]{2,1,0:T(8,128)} %collective-permute-done.refs_1_, f32[32,64,128]{2,1,0:T(8,128)} %collective-permute-done.1.refs_2_, ...), custom_call_target="tpu_custom_call" | custom-call | flops 2147483648 | bytes 8388608 | tf_op jit(solution)/shard_map/own_gram/pallas_call | solution.py:137
  147.7 4.3 %even_gram.1 = (f32[128,256]{1,0:T(8,128)S(1)}, f32[128,128]{1,0:T(8,128)S(1)}, bf16[16,128,256]{2,1,0:T(8,128)(2,1)S(1)}, bf16[16,128,256]{2,1,0:T(8,128)(2,1)S(1)}) custom-call(s32[1]{0:T(128)} %bitcast.place_ref, f32[32,64,128]{2,1,0:T(8,128)S(1)} %collective-permute-done.4.near, f32[32,64,128]{2,1,0:T(8,128)S(1)} %collective-permute-done.2.far, ...), custom_call_target="tpu_custom_call" | custom-call | flops 1610612736 | bytes 12582912 | tf_op jit(solution)/shard_map/even_gram/pallas_call | solution.py:137
  152.1 36.2 %collective-permute-done.5.near = f32[32,64,128]{2,1,0:T(8,128)} collective-permute-done((f32[32,64,128]{2,1,0:T(8,128)}, f32[32,64,128]{2,1,0:T(8,128)}, u32[]{:S(2)}, u32[]{:S(2)}) %collective-permute-start.5) | collective-permute-done | bytes 1048608 | tf_op jit(solution)/shard_map/ppermute | solution.py:371
  188.2 4.6 %odd_gram.1 = (f32[384,128]{1,0:T(8,128)S(1)}, f32[256,256]{1,0:T(8,128)S(1)}, bf16[16,128,256]{2,1,0:T(8,128)(2,1)S(1)}, bf16[16,128,256]{2,1,0:T(8,128)(2,1)S(1)}) custom-call(s32[1]{0:T(128)} %bitcast.place_ref, f32[256,256]{1,0:T(8,128)S(1)} %get-tuple-element.23.own_gram, f32[128,256]{1,0:T(8,128)S(1)} %get-tuple-element.26.cross_even, ...), custom_call_target="tpu_custom_call" | custom-call | flops 2147483648 | bytes 16777216 | tf_op jit(solution)/shard_map/odd_gram/pallas_call | solution.py:137
  192.8 2.0 collective-permute-start.14
  195.8 1.3 collective-permute-start.15
  198.9 1.5 collective-permute-done.8
  200.4 1.3 collective-permute-start.9
  201.9 2.7 %collective-permute-done.16 = f32[96,128]{1,0:T(8,128)S(1)} collective-permute-done((f32[96,128]{1,0:T(8,128)S(1)}, f32[96,128]{1,0:T(8,128)S(1)}, u32[]{:S(2)}, u32[]{:S(2)}) %collective-permute-start.16) | collective-permute-done | bytes 49184 | tf_op jit(solution)/shard_map/ppermute | solution.py:203
  204.7 1.5 collective-permute-start.10
  206.2 1.4 collective-permute-done.17
  208.3 1.8 collective-permute-start.11
  210.1 1.8 collective-permute-done.18
  212.0 1.5 collective-permute-start.19
  215.0 6.7 %collective-permute-start.20 = (f32[192,128]{1,0:T(8,128)S(1)}, f32[192,128]{1,0:T(8,128)S(1)}, u32[]{:S(2)}, u32[]{:S(2)}) collective-permute-start(f32[192,128]{1,0:T(8,128)S(1)} %maximum_select_fusion.3), channel_id=1, source_target_pairs={{0,1},{1,0},{2,3},{3,2},{4,5},{5,4},{6,7},{7,6},{8,9},{9,8},{10,11... | collective-permute-start | bytes 294920 | tf_op jit(solution)/shard_map/ppermute | solution.py:206
  221.7 2.6 %collective-permute-start.13 = (f32[128,256]{1,0:T(8,128)S(1)}, f32[128,256]{1,0:T(8,128)S(1)}, u32[]{:S(2)}, u32[]{:S(2)}) collective-permute-start(f32[128,256]{1,0:T(8,128)S(1)} %maximum_select_fusion.2), channel_id=1, source_target_pairs={{0,1},{1,0},{2,3},{3,2},{4,5},{5,4},{6,7},{7,6},{8,9},{9,8},{10,11... | collective-permute-start | bytes 393224 | tf_op jit(solution)/shard_map/ppermute | solution.py:206
  224.3 8.4 %cholesky256.1 = (f32[256,256]{1,0:T(8,128)S(1)}, f32[256,256]{1,0:T(8,128)S(1)}) custom-call(f32[384,128]{1,0:T(8,128)S(1)} %maximum_select_fusion.1.gram_ref), custom_call_target="tpu_custom_call" | custom-call | flops 33554432 | bytes 786432 | tf_op jit(solution)/shard_map/cholesky256/pallas_call | solution.py:291
  232.7 7.2 %core.1 = (f32[512,256]{1,0:T(8,128)}, f32[256,4,8,128]{3,2,1,0:T(8,128)}) custom-call(s32[1]{0:T(128)} %bitcast.place_ref, f32[256,256]{1,0:T(8,128)S(1)} %maximum_select_fusion.below, f32[256,256]{1,0:T(8,128)S(1)} %get-tuple-element.34.upper, f32[256,256]{1,0:T(8,128)S(1)} %get-tuple-element.35.inverse, ...), custom_call_target="tpu_custom_call" | custom-call | flops 3221225472 | bytes 12582912 | tf_op jit(solution)/shard_map/core/pallas_call | solution.py:335
  (43 shorter events, 8.2 us)
Async XLA Ops:
  2.6 27.2 %collective-permute-start.2 = (f32[32,64,128]{2,1,0:T(8,128)S(1)}, f32[32,64,128]{2,1,0:T(8,128)S(1)}, u32[]{:S(2)}, u32[]{:S(2)}) collective-permute-start(f32[32,64,128]{2,1,0:T(8,128)S(1)} %bitcast.26), channel_id=1, source_target_pairs={{0,24},{4,28},{8,16},{12,20},{16,8},{20,12},{24,0},{28,4},{1,25},{... | collective-permute-start | bytes 3145736 | tf_op jit(solution)/shard_map/ppermute | solution.py:372
  12.8 83.3 %collective-permute-start.4 = (f32[32,64,128]{2,1,0:T(8,128)S(1)}, f32[32,64,128]{2,1,0:T(8,128)S(1)}, u32[]{:S(2)}, u32[]{:S(2)}) collective-permute-start(f32[32,64,128]{2,1,0:T(8,128)S(1)} %bitcast.27), channel_id=1, source_target_pairs={{0,16},{4,20},{8,24},{12,28},{16,0},{20,4},{24,8},{28,12},{1,17},{... | collective-permute-start | bytes 3145736 | tf_op jit(solution)/shard_map/ppermute | solution.py:371
  14.5 86.4 %collective-permute-start = (f32[32,64,128]{2,1,0:T(8,128)}, f32[32,64,128]{2,1,0:T(8,128)}, u32[]{:S(2)}, u32[]{:S(2)}) collective-permute-start(f32[32,64,128]{2,1,0:T(8,128)} %bitcast.6), channel_id=1, source_target_pairs={{0,4},{4,0},{8,12},{12,8},{16,20},{20,16},{24,28},{28,24},{1,5},{5... | collective-permute-start | bytes 3145736 | tf_op jit(solution)/shard_map/ppermute | solution.py:371
  17.4 83.5 %collective-permute-start.1 = (f32[32,64,128]{2,1,0:T(8,128)}, f32[32,64,128]{2,1,0:T(8,128)}, u32[]{:S(2)}, u32[]{:S(2)}) collective-permute-start(f32[32,64,128]{2,1,0:T(8,128)} %bitcast.8), channel_id=1, source_target_pairs={{0,8},{4,12},{8,0},{12,4},{16,24},{20,28},{24,16},{28,20},{1,9},{5... | collective-permute-start | bytes 3145736 | tf_op jit(solution)/shard_map/ppermute | solution.py:371
  29.8 113.1 %collective-permute-start.3 = (f32[32,64,128]{2,1,0:T(8,128)}, f32[32,64,128]{2,1,0:T(8,128)}, u32[]{:S(2)}, u32[]{:S(2)}) collective-permute-start(f32[32,64,128]{2,1,0:T(8,128)} %bitcast.10), channel_id=1, source_target_pairs={{0,12},{4,8},{8,4},{12,0},{16,28},{20,24},{24,20},{28,16},{1,13},{... | collective-permute-start | bytes 3145736 | tf_op jit(solution)/shard_map/ppermute | solution.py:371
  96.1 55.9 %collective-permute-start.6 = (f32[32,64,128]{2,1,0:T(8,128)}, f32[32,64,128]{2,1,0:T(8,128)S(1)}, u32[]{:S(2)}, u32[]{:S(2)}) collective-permute-start(f32[32,64,128]{2,1,0:T(8,128)} %bitcast.16), channel_id=1, source_target_pairs={{0,28},{4,24},{8,20},{12,16},{16,12},{20,8},{24,4},{28,0},{1,29},{... | collective-permute-start | bytes 3145736 | tf_op jit(solution)/shard_map/ppermute | solution.py:371
  99.1 89.1 %collective-permute-start.5 = (f32[32,64,128]{2,1,0:T(8,128)}, f32[32,64,128]{2,1,0:T(8,128)}, u32[]{:S(2)}, u32[]{:S(2)}) collective-permute-start(f32[32,64,128]{2,1,0:T(8,128)} %bitcast.14), channel_id=1, source_target_pairs={{0,20},{4,16},{8,28},{12,24},{16,4},{20,0},{24,12},{28,8},{1,21},{... | collective-permute-start | bytes 3145736 | tf_op jit(solution)/shard_map/ppermute | solution.py:371
  192.8 3.0 %collective-permute-start.14 = (f32[192,128]{1,0:T(8,128)S(1)}, f32[192,128]{1,0:T(8,128)S(1)}, u32[]{:S(2)}, u32[]{:S(2)}) collective-permute-start(f32[192,128]{1,0:T(8,128)S(1)} %slice_select_fusion.1), channel_id=1, source_target_pairs={{0,1},{1,0},{2,3},{3,2},{4,5},{5,4},{6,7},{7,6},{8,9},{9,8},{10,11... | collective-permute-start | bytes 294920 | tf_op jit(solution)/shard_map/ppermute | solution.py:201
  194.9 2.3 collective-permute-start.7
  195.8 3.0 %collective-permute-start.15 = (f32[96,128]{1,0:T(8,128)S(1)}, f32[96,128]{1,0:T(8,128)S(1)}, u32[]{:S(2)}, u32[]{:S(2)}) collective-permute-start(f32[96,128]{1,0:T(8,128)S(1)} %slice_select_fusion.3), channel_id=1, source_target_pairs={{0,2},{1,3},{2,0},{3,1},{4,6},{5,7},{6,4},{7,5},{8,10},{9,11},{10,... | collective-permute-start | bytes 147464 | tf_op jit(solution)/shard_map/ppermute | solution.py:201
  197.2 3.2 %collective-permute-start.8 = (f32[64,256]{1,0:T(8,128)S(1)}, f32[64,256]{1,0:T(8,128)S(1)}, u32[]{:S(2)}, u32[]{:S(2)}) collective-permute-start(f32[64,256]{1,0:T(8,128)S(1)} %slice_select_fusion.2), channel_id=1, source_target_pairs={{0,2},{1,3},{2,0},{3,1},{4,6},{5,7},{6,4},{7,5},{8,10},{9,11},{10,... | collective-permute-start | bytes 196616 | tf_op jit(solution)/shard_map/ppermute | solution.py:201
  200.4 4.3 %collective-permute-start.9 = (f32[64,256]{1,0:T(8,128)S(1)}, f32[64,256]{1,0:T(8,128)S(1)}, u32[]{:S(2)}, u32[]{:S(2)}) collective-permute-start(f32[64,256]{1,0:T(8,128)S(1)} %select_add_fusion.2), channel_id=1, source_target_pairs={{0,4},{4,0},{8,12},{12,8},{16,20},{20,16},{24,28},{28,24},{1,5},{5... | collective-permute-start | bytes 196616 | tf_op jit(solution)/shard_map/ppermute | solution.py:203
  201.7 2.9 %collective-permute-start.16 = (f32[96,128]{1,0:T(8,128)S(1)}, f32[96,128]{1,0:T(8,128)S(1)}, u32[]{:S(2)}, u32[]{:S(2)}) collective-permute-start(f32[96,128]{1,0:T(8,128)S(1)} %select_add_fusion.3), channel_id=1, source_target_pairs={{0,4},{4,0},{8,12},{12,8},{16,20},{20,16},{24,28},{28,24},{1,5},{5... | collective-permute-start | bytes 147464 | tf_op jit(solution)/shard_map/ppermute | solution.py:203
  204.6 3.0 %collective-permute-start.17 = (f32[96,128]{1,0:T(8,128)S(1)}, f32[96,128]{1,0:T(8,128)S(1)}, u32[]{:S(2)}, u32[]{:S(2)}) collective-permute-start(f32[96,128]{1,0:T(8,128)S(1)} %add.69), channel_id=1, source_target_pairs={{0,8},{4,12},{8,0},{12,4},{16,24},{20,28},{24,16},{28,20},{1,9},{5... | collective-permute-start | bytes 147464 | tf_op jit(solution)/shard_map/ppermute | solution.py:203
  204.7 3.6 %collective-permute-start.10 = (f32[64,256]{1,0:T(8,128)S(1)}, f32[64,256]{1,0:T(8,128)S(1)}, u32[]{:S(2)}, u32[]{:S(2)}) collective-permute-start(f32[64,256]{1,0:T(8,128)S(1)} %add.64), channel_id=1, source_target_pairs={{0,8},{4,12},{8,0},{12,4},{16,24},{20,28},{24,16},{28,20},{1,9},{5... | collective-permute-start | bytes 196616 | tf_op jit(solution)/shard_map/ppermute | solution.py:203
  207.6 4.3 %collective-permute-start.18 = (f32[96,128]{1,0:T(8,128)S(1)}, f32[96,128]{1,0:T(8,128)S(1)}, u32[]{:S(2)}, u32[]{:S(2)}) collective-permute-start(f32[96,128]{1,0:T(8,128)S(1)} %add.70), channel_id=1, source_target_pairs={{0,16},{4,20},{8,24},{12,28},{16,0},{20,4},{24,8},{28,12},{1,17},{... | collective-permute-start | bytes 147464 | tf_op jit(solution)/shard_map/ppermute | solution.py:203
  208.3 5.1 %collective-permute-start.11 = (f32[64,256]{1,0:T(8,128)S(1)}, f32[64,256]{1,0:T(8,128)S(1)}, u32[]{:S(2)}, u32[]{:S(2)}) collective-permute-start(f32[64,256]{1,0:T(8,128)S(1)} %add.65), channel_id=1, source_target_pairs={{0,16},{4,20},{8,24},{12,28},{16,0},{20,4},{24,8},{28,12},{1,17},{... | collective-permute-start | bytes 196616 | tf_op jit(solution)/shard_map/ppermute | solution.py:203
  212.0 3.0 %collective-permute-start.19 = (f32[96,128]{1,0:T(8,128)S(1)}, f32[96,128]{1,0:T(8,128)S(1)}, u32[]{:S(2)}, u32[]{:S(2)}) collective-permute-start(f32[96,128]{1,0:T(8,128)S(1)} %add.71), channel_id=1, source_target_pairs={{0,2},{1,3},{2,0},{3,1},{4,6},{5,7},{6,4},{7,5},{8,10},{9,11},{10,... | collective-permute-start | bytes 147464 | tf_op jit(solution)/shard_map/ppermute | solution.py:206
  213.5 8.2 %collective-permute-start.12 = (f32[64,256]{1,0:T(8,128)S(1)}, f32[64,256]{1,0:T(8,128)S(1)}, u32[]{:S(2)}, u32[]{:S(2)}) collective-permute-start(f32[64,256]{1,0:T(8,128)S(1)} %add.66), channel_id=1, source_target_pairs={{0,2},{1,3},{2,0},{3,1},{4,6},{5,7},{6,4},{7,5},{8,10},{9,11},{10,... | collective-permute-start | bytes 196616 | tf_op jit(solution)/shard_map/ppermute | solution.py:206
  215.0 9.3 %collective-permute-start.20 = (f32[192,128]{1,0:T(8,128)S(1)}, f32[192,128]{1,0:T(8,128)S(1)}, u32[]{:S(2)}, u32[]{:S(2)}) collective-permute-start(f32[192,128]{1,0:T(8,128)S(1)} %maximum_select_fusion.3), channel_id=1, source_target_pairs={{0,1},{1,0},{2,3},{3,2},{4,5},{5,4},{6,7},{7,6},{8,9},{9,8},{10,11... | collective-permute-start | bytes 294920 | tf_op jit(solution)/shard_map/ppermute | solution.py:206
  221.7 10.9 %collective-permute-start.13 = (f32[128,256]{1,0:T(8,128)S(1)}, f32[128,256]{1,0:T(8,128)S(1)}, u32[]{:S(2)}, u32[]{:S(2)}) collective-permute-start(f32[128,256]{1,0:T(8,128)S(1)} %maximum_select_fusion.2), channel_id=1, source_target_pairs={{0,1},{1,0},{2,3},{3,2},{4,5},{5,4},{6,7},{7,6},{8,9},{9,8},{10,11... | collective-permute-start | bytes 393224 | tf_op jit(solution)/shard_map/ppermute | solution.py:206

commit v5 on v4

--- a/solution.py
+++ b/solution.py
@@ -9,7 +9,9 @@
 
 RANK = 256
 LANES = 128
-FAST_WIDE = 8
+FAST_WIDE, FAST_NARROW = 8, 4
+LATE = 1
+LATE_STEPS = 2
 HIGHEST = lax.Precision.HIGHEST
 VMEM_LIMIT = 16 * 1024 * 1024
 
@@ -84,20 +86,32 @@
         add_to(gram_ref, product(x, x))
 
 
-def odd_kernel(
-    place_ref, own_gram, cross_even, gram_even, near, far, own_h, own_l, even_h, even_l,
+def add_odd(place_ref, near, far, own, even, odd, all_ref):
+    for t in range(near.shape[0] // 2):
+        x = split(two_cells(place_ref[0] // 2, (near, far), t))
+        write(odd, t, x)
+        both = jnp.concatenate(x, axis=0)
+        n = both.shape[0] // 2
+        high = rows_dot(jnp.concatenate([own[0][t], even[0][t], x[0]], axis=0), both)
+        low = rows_dot(jnp.concatenate([own[1][t], even[1][t], x[1]], axis=0), both)
+        add_to(all_ref, (high[:, :n] + high[:, n:]) + (low[:, :n] + low[:, n:]))
+
+
+def odd_kernel(place_ref, near, far, own_h, own_l, even_h, even_l, all_ref, odd_h, odd_l):
+    start_at_zero(all_ref)
+    add_odd(place_ref, near, far, (own_h, own_l), (even_h, even_l), (odd_h, odd_l), all_ref)
+
+
+def last_kernel(
+    place_ref, own_gram, cross_even, gram_even, all_odd, near, far, own_h, own_l, even_h, even_l, _, __,
     corner_ref, below_ref, odd_h, odd_l, all_ref,
 ):
-    start_at_zero(all_ref)
+    @pl.when(pl.program_id(0) == 0)
+    def _():
+        all_ref[...] = all_odd[...]
+
+    add_odd(place_ref, near, far, (own_h, own_l), (even_h, even_l), (odd_h, odd_l), all_ref)
     place = place_ref[0]
-    for t in range(near.shape[0] // 2):
-        x = split(two_cells(place // 2, (near, far), t))
-        write((odd_h, odd_l), t, x)
-        both = jnp.concatenate(x, axis=0)
-        n = both.shape[0] // 2
-        high = rows_dot(jnp.concatenate([own_h[t], even_h[t], x[0]], axis=0), both)
-        low = rows_dot(jnp.concatenate([own_l[t], even_l[t], x[1]], axis=0), both)
-        add_to(all_ref, (high[:, :n] + high[:, n:]) + (low[:, :n] + low[:, n:]))
 
     @pl.when(pl.program_id(0) == pl.num_programs(0) - 1)
     def _():
@@ -128,25 +142,33 @@
     return pl.BlockSpec(shape, lambda i: (0,) * len(shape))
 
 
-def stepped(shape, steps):
-    return pl.BlockSpec((shape[0] // steps,) + shape[1:], lambda i: (i,) + (0,) * (len(shape) - 1))
-
-
-def call(kernel, name, steps, place, kept, streamed, kept_out, streamed_out, scratch=(), flops=0):
-    moved = sum(4 * x.size for x in streamed) + sum(2 * s.size for s in streamed_out)
+def parts_of(x, size, first=0):
+    return pl.BlockSpec((size,) + x.shape[1:], lambda i: (i + first,) + (0,) * (len(x.shape) - 1))
+
+
+def call(
+    kernel, name, steps, place, kept, blocks, split_blocks, kept_out, out, first=0, filled=(), scratch=(), flops=0
+):
+    pairs = blocks[0].shape[0] // 2 // steps
+    moved = sum(4 * x.size for x in blocks) + sum(2 * s.size for s in out)
     return pl.pallas_call(
         kernel,
         grid=(steps,),
         in_specs=[pl.BlockSpec(memory_space=pltpu.SMEM)]
         + [whole(x.shape) for x in kept]
-        + [stepped(x.shape, steps) for x in streamed],
-        out_specs=[whole(s.shape) for s in kept_out] + [stepped(s.shape, steps) for s in streamed_out],
-        out_shape=list(kept_out) + list(streamed_out),
+        + [parts_of(x, 2 * pairs) for x in blocks]
+        + [parts_of(x, pairs, first) for x in split_blocks]
+        + [pl.BlockSpec(memory_space=pl.ANY) for _ in filled],
+        out_specs=[whole(s.shape) for s in kept_out] + [parts_of(s, pairs, first) for s in out],
+        out_shape=list(kept_out) + list(out),
         scratch_shapes=list(scratch),
+        input_output_aliases={
+            1 + len(kept) + len(blocks) + len(split_blocks) + i: len(kept_out) + i for i in range(len(filled))
+        },
         compiler_params=pltpu.CompilerParams(vmem_limit_bytes=VMEM_LIMIT),
         cost_estimate=pl.CostEstimate(flops=flops, bytes_accessed=moved, transcendentals=0),
         name=name,
-    )(place, *kept, *streamed)
+    )(place, *kept, *blocks, *split_blocks, *filled)
 
 
 def f32(*shape):
@@ -161,7 +183,7 @@
     cells, rows, fields = blocks[0].shape
     n = rows * len(blocks)
     return call(
-        own_kernel, "own_gram", steps, place, [], blocks, [f32(n, n)], halves(cells, n, fields),
+        own_kernel, "own_gram", steps, place, [], blocks, [], [f32(n, n)], halves(cells, n, fields),
         flops=8 * n * n * cells * fields,
     )
 
@@ -170,42 +192,57 @@
     cells, rows, fields = near.shape
     n = 2 * rows
     return call(
-        even_kernel, "even_gram", steps, place, [], [near, far, *own],
+        even_kernel, "even_gram", steps, place, [], [near, far], own,
         [f32(n, 2 * n), f32(n, n)], halves(cells, n, fields), flops=24 * n * n * cells * fields,
     )
 
 
-def gram_of_odd(place, kept, near, far, own, even, steps):
+def gram_of_odd(place, near, far, own, even, steps):
     cells, rows, fields = near.shape
     n = 2 * rows
     return call(
-        odd_kernel, "odd_gram", steps, place, kept, [near, far, *own, *even],
-        [f32(3 * LANES, LANES), f32(RANK, RANK)], halves(cells, n, fields),
-        [pltpu.VMEM((4 * n, n), jnp.float32)],
-        flops=32 * n * n * cells * fields,
-    )
-
-
-def over(axis, n, distance):
+        odd_kernel, "odd_gram", steps, place, [], [near, far], [*own, *even],
+        [f32(4 * n, n)], halves(2 * own[0].shape[0], n, fields), flops=32 * n * n * cells * fields,
+    )
+
+
+def gram_of_last(place, kept, near, far, own, even, odd, steps):
+    cells, rows, fields = near.shape
+    n = 2 * rows
+    pairs = cells // 2 // steps
+    return call(
+        last_kernel, "last_gram", steps, place, kept, [near, far], [*own, *even],
+        [f32(3 * LANES, LANES), f32(RANK, RANK)], halves(2 * own[0].shape[0], n, fields), own[0].shape[0] // pairs - steps, odd,
+        [pltpu.VMEM((4 * n, n), jnp.float32)], flops=32 * n * n * cells * fields,
+    )
+
+
+def over(step):
+    axis, n, distance = step
     return functools.partial(lax.ppermute, axis_name=axis, perm=[(i, i ^ distance) for i in range(n)])
 
 
-def sum_over_all(x, wide, narrow):
-    place = lax.axis_index("narrow")
-    distances = [1 << b for b in range(narrow.bit_length() - 1)]
-    for d in distances:
-        side = (place & d) != 0
+def sum_over_all(x, halved, doubled):
+    sides = [(lax.axis_index(axis) & distance) != 0 for axis, _, distance in halved]
+    for step, side in zip(halved, sides):
         n = x.shape[0] // 2
         keep = jnp.where(side, x[n:], x[:n])
         send = jnp.where(side, x[:n], x[n:])
-        x = keep + over("narrow", narrow, d)(send)
-    for b in range(wide.bit_length() - 1):
-        x = x + over("wide", wide, 1 << b)(x)
-    for d in reversed(distances):
-        side = (place & d) != 0
-        got = over("narrow", narrow, d)(x)
+        x = keep + over(step)(send)
+    for step in doubled:
+        x = x + over(step)(x)
+    for step, side in reversed(list(zip(halved, sides))):
+        got = over(step)(x)
         x = jnp.where(side, jnp.concatenate([got, x]), jnp.concatenate([x, got]))
     return x
+
+
+def sum_both(corner, below, wide, narrow):
+    core, y = ("narrow", narrow, 1), ("narrow", narrow, 2)
+    x, z_near, z_far = [("wide", wide, 1 << b) for b in range(3)]
+    corner = sum_over_all(corner, [core, y], [z_far, x, z_near])
+    below = sum_over_all(below, [core, x], [y, z_near, z_far])
+    return corner, below
 
 
 PANEL = 64
@@ -337,7 +374,7 @@
         grid=(ny,),
         in_specs=[pl.BlockSpec(memory_space=pltpu.SMEM)]
         + [whole(x.shape) for x in kept]
-        + [stepped(x.shape, ny) for x in streamed],
+        + [parts_of(x, nz // 2) for x in streamed],
         out_specs=[whole((size, RANK)), pl.BlockSpec((RANK, 1, nz, fields), lambda i: (0, i, 0, 0))],
         out_shape=[f32(size, RANK), f32(RANK, ny, nz, fields)],
         scratch_shapes=[pltpu.VMEM((RANK, 3 * size), jnp.bfloat16)],
@@ -368,18 +405,25 @@
     first = block_for(snapshot, here ^ 6, nz)
     snapshot = tie(snapshot, first)
     got = {}
-    send = lambda k, *deps: over("wide", wide, k)(tie(block_for(snapshot, here ^ k, nz), *deps))
-    got[6] = over("wide", wide, 6)(first)
+    send = lambda k, *deps: over(("wide", wide, k))(tie(block_for(snapshot, here ^ k, nz), *deps))
+    got[6] = over(("wide", wide, 6))(first)
     got[4], got[2], got[1] = send(4), send(2), send(1)
     got[3] = send(3, got[6])
-    got[5] = send(5, got[6])
-    got[7] = send(7, got[4])
+    split_at = (ny - LATE) * nz
+    blocks, late = {}, {}
+    for k, after in ((5, 6), (7, 4)):
+        block = tie(block_for(snapshot, here ^ k, nz), got[after])
+        got[k] = over(("wide", wide, k))(block[:split_at])
+        blocks[k] = block[split_at:]
+    late[5] = over(("wide", wide, 5))(tie(blocks[5], got[7]))
+    late[7] = over(("wide", wide, 7))(tie(blocks[7], got[7]))
     got[0] = block_for(snapshot, here, nz)
     own_gram, *own = gram_of_own(place, [got[k] for k in range(4)], ny)
     cross_even, gram_even, *even = gram_of_even(place, got[4], got[6], own, ny)
-    corner, below, *odd = gram_of_odd(place, [own_gram, cross_even, gram_even], got[5], got[7], own, even, ny)
-    corner = sum_over_all(corner, wide, narrow)
-    below = sum_over_all(below, wide, narrow)
+    all_odd, *odd = gram_of_odd(place, got[5], got[7], own, even, ny - LATE)
+    kept = [own_gram, cross_even, gram_even, all_odd]
+    corner, below, *odd = gram_of_last(place, kept, late[5], late[7], own, even, odd, LATE * LATE_STEPS)
+    corner, below = sum_both(corner, below, wide, narrow)
     upper, inverse = cholesky(corner)
     factor, core = core_and_factor(
         place, [below, upper, inverse], [*own, *even, *odd], ny, nz, snapshot.shape[3]
@@ -407,7 +451,7 @@
 
 def solution(mesh):
     wide, narrow = mesh.shape["wide"], mesh.shape["narrow"]
-    if wide == FAST_WIDE:
+    if (wide, narrow) == (FAST_WIDE, FAST_NARROW):
         on_device = functools.partial(on_device_blocks, wide=wide, narrow=narrow)
     else:
         on_device = on_device_any

time: 240 us -> 235 us (0.979)
  waiting for transfers between devices: 117 us -> 65.1 us
  starting transfers between devices: 74.7 us -> 118 us
  local copies, waits for them, and re-layouts: 17.9 us -> 20.9 us
    ppermute x21 -> x23, waiting for transfers between devices: 117 us -> 65.1 us  [the longest x2 26.7 us: on_device_blocks(): got[k] = over(('wide', wide, k))(block[:split_at])]
    ppermute x21 -> x23, starting transfers between devices: 74.7 us -> 118 us  [the longest x4 46.8 us: on_device_blocks(): over(('wide', wide, k))(tie(block_for(snapshot, here ^ k, nz), *deps))]
    slice x0 -> x4, local copies, waits for them, and re-layouts: none -> 3.94 us  [the longest x2 2 us: on_device_blocks(): got[k] = over(('wide', wide, k))(block[:split_at])]
    pallas_call x3 -> x4, Pallas kernels: 13.8 us -> 14.2 us  [call(): pl.pallas_call(kernel, grid=(steps,), in_specs=[pl.BlockSpec(memory_space...]
  transfers between devices with their start and end apart: 21 -> 23, of which waited for: 12 -> 11; matrix products, arithmetic and copies ran while one was open for 7% -> 8% of each run, Pallas kernels for 7% -> 9%
where the time goes in v5:
time: 235 us
  starting transfers between devices  118 us (50%)
  waiting for transfers between devices  65.1 us (28%)
  Pallas kernels  29.7 us (13%)
  local copies, waits for them, and re-layouts  20.9 us (9%)
    ppermute x4, starting transfers between devices, on_device_blocks(): over(('wide', wide, k))(tie(block_for(snapshot, here ^ k, nz), *deps))  46.8 us
    ppermute x1, starting transfers between devices, on_device_blocks(): late[5] = over(('wide', wide, 5))(tie(blocks[5], got[7]))  33.4 us
    ppermute x2, waiting for transfers between devices, on_device_blocks(): got[k] = over(('wide', wide, k))(block[:split_at])  26.7 us
    ppermute x4, waiting for transfers between devices, on_device_blocks(): over(('wide', wide, k))(tie(block_for(snapshot, here ^ k, nz), *deps))  20.6 us
    transpose x10, local copies, waits for them, and re-layouts, block_for(): return cut.transpose(1, 2, 0, 3).reshape(ny * nz, rows, fields)  15.8 us
    pallas_call x4, Pallas kernels, call(): pl.pallas_call(kernel, grid=(steps,), in_specs=[pl.BlockSpec(memory_space...  14.2 us
    ppermute x6, starting transfers between devices, sum_over_all(): x = x + over(step)(x)  12.4 us
    ppermute x4, starting transfers between devices, sum_over_all(): got = over(step)(x)  10.6 us
  transfers between devices with their start and end apart: 23, of which 11 were waited for; matrix products, arithmetic and copies ran while one was open for 8% of the time, Pallas kernels for 9%

profile of v5, /device:TPU:1, one launch (start us, length us, event | category | flops | bytes accessed | tf_op | source)
XLA Modules:
  0.0 234.8 jit_solution(10656341424377760701)
XLA Ops:
  0.6 1.3 dynamic-slice_bitcast_fusion.7
  2.6 4.2 %collective-permute-start.2 = (f32[32,64,128]{2,1,0:T(8,128)S(1)}, f32[32,64,128]{2,1,0:T(8,128)S(1)}, u32[]{:S(2)}, u32[]{:S(2)}) collective-permute-start(f32[32,64,128]{2,1,0:T(8,128)S(1)} %bitcast.30), channel_id=1, source_target_pairs={{0,24},{4,28},{8,16},{12,20},{16,8},{20,12},{24,0},{28,4},{1,25},{... | collective-permute-start | bytes 3145736 | tf_op jit(solution)/shard_map/ppermute | solution.py:409
  6.8 5.4 %dynamic-slice_bitcast_fusion = (f32[4,8,64,128]{3,1,0,2:T(8,128)S(1)}, f32[4,8,64,128]{3,1,0,2:T(8,128)S(1)}, f32[4,8,64,128]{3,1,0,2:T(8,128)S(1)}, f32[4,8,64...) fusion(f32[64,4,64,128]{3,2,1,0:T(8,128)} %param.1, ...), kind=kLoop, calls=%fused_computation | loop fusion | bytes 14680092 | tf_op jit(solution)/shard_map/transpose | solution.py:398
  12.9 1.6 copy.7
  15.7 1.6 copy.8
  17.7 1.6 copy.9
  19.3 10.5 %collective-permute-done.2.far = f32[32,64,128]{2,1,0:T(8,128)S(1)} collective-permute-done((f32[32,64,128]{2,1,0:T(8,128)S(1)}, f32[32,64,128]{2,1,0:T(8,128)S(1)}, u32[]{:S(2)}, u32[]{:S(2)}) %collective-permute-start.2) | collective-permute-done | bytes 1048608 | tf_op jit(solution)/shard_map/ppermute | solution.py:409
  29.8 45.2 %collective-permute-start.3 = (f32[32,64,128]{2,1,0:T(8,128)}, f32[32,64,128]{2,1,0:T(8,128)}, u32[]{:S(2)}, u32[]{:S(2)}) collective-permute-start(f32[32,64,128]{2,1,0:T(8,128)} %bitcast.10), channel_id=1, source_target_pairs={{0,12},{4,8},{8,4},{12,0},{16,28},{20,24},{24,20},{28,16},{1,13},{... | collective-permute-start | bytes 3145736 | tf_op jit(solution)/shard_map/ppermute | solution.py:408
  75.6 20.6 %collective-permute-done.4.near = f32[32,64,128]{2,1,0:T(8,128)S(1)} collective-permute-done((f32[32,64,128]{2,1,0:T(8,128)S(1)}, f32[32,64,128]{2,1,0:T(8,128)S(1)}, u32[]{:S(2)}, u32[]{:S(2)}) %collective-permute-start.4) | collective-permute-done | bytes 1048608 | tf_op jit(solution)/shard_map/ppermute | solution.py:408
  97.1 2.9 %collective-permute-start.6 = (f32[24,64,128]{2,1,0:T(8,128)}, f32[24,64,128]{2,1,0:T(8,128)S(1)}, u32[]{:S(2)}, u32[]{:S(2)}) collective-permute-start(f32[24,64,128]{2,1,0:T(8,128)} %slice.45), channel_id=1, source_target_pairs={{0,28},{4,24},{8,20},{12,16},{16,12},{20,8},{24,4},{28,0},{1,29},{... | collective-permute-start | bytes 2359304 | tf_op jit(solution)/shard_map/ppermute | solution.py:416
  102.8 1.8 copy.6
  106.6 11.2 %collective-permute-done.6.far = f32[24,64,128]{2,1,0:T(8,128)S(1)} collective-permute-done((f32[24,64,128]{2,1,0:T(8,128)}, f32[24,64,128]{2,1,0:T(8,128)S(1)}, u32[]{:S(2)}, u32[]{:S(2)}) %collective-permute-start.6) | collective-permute-done | bytes 786464 | tf_op jit(solution)/shard_map/ppermute | solution.py:416
  117.7 33.4 %collective-permute-start.7 = (f32[8,64,128]{2,1,0:T(8,128)S(1)}, f32[8,64,128]{2,1,0:T(8,128)S(1)}, u32[]{:S(2)}, u32[]{:S(2)}) collective-permute-start(f32[8,64,128]{2,1,0:T(8,128)S(1)} %slice.46), channel_id=1, source_target_pairs={{0,20},{4,16},{8,28},{12,24},{16,4},{20,0},{24,12},{28,8},{1,21},{... | collective-permute-start | bytes 786440 | tf_op jit(solution)/shard_map/ppermute | solution.py:418
  152.0 5.1 %own_gram.1 = (f32[256,256]{1,0:T(8,128)S(1)}, bf16[16,256,256]{2,1,0:T(8,128)(2,1)S(1)}, bf16[16,256,256]{2,1,0:T(8,128)(2,1)S(1)}) custom-call(s32[1]{0:T(128)} %bitcast.place_ref, f32[32,64,128]{2,1,0:T(8,128)S(1)} %bitcast.25, f32[32,64,128]{2,1,0:T(8,128)} %collective-permute-done.refs_1_, f32[32,64,128]{2,1,0:T(8,128)} %collective-permute-done.1.refs_2_, ...), custom_call_target="tpu_custom_call" | custom-call | flops 2147483648 | bytes 8388608 | tf_op jit(solution)/shard_map/own_gram/pallas_call | solution.py:154
  157.1 4.3 %even_gram.1 = (f32[128,256]{1,0:T(8,128)S(1)}, f32[128,128]{1,0:T(8,128)S(1)}, bf16[16,128,256]{2,1,0:T(8,128)(2,1)S(1)}, bf16[16,128,256]{2,1,0:T(8,128)(2,1)S(1)}) custom-call(s32[1]{0:T(128)} %bitcast.place_ref, f32[32,64,128]{2,1,0:T(8,128)S(1)} %collective-permute-done.4.near, f32[32,64,128]{2,1,0:T(8,128)S(1)} %collective-permute-done.2.far, ...), custom_call_target="tpu_custom_call" | custom-call | flops 1610612736 | bytes 4194304 | tf_op jit(solution)/shard_map/even_gram/pallas_call | solution.py:154
  161.4 15.5 %collective-permute-done.5.near = f32[24,64,128]{2,1,0:T(8,128)} collective-permute-done((f32[24,64,128]{2,1,0:T(8,128)}, f32[24,64,128]{2,1,0:T(8,128)}, u32[]{:S(2)}, u32[]{:S(2)}) %collective-permute-start.5) | collective-permute-done | bytes 786464 | tf_op jit(solution)/shard_map/ppermute | solution.py:416
  176.9 3.5 %odd_gram.1 = (f32[512,128]{1,0:T(8,128)S(1)}, bf16[16,128,256]{2,1,0:T(8,128)(2,1)S(1)}, bf16[16,128,256]{2,1,0:T(8,128)(2,1)S(1)}) custom-call(s32[1]{0:T(128)} %bitcast.place_ref, f32[24,64,128]{2,1,0:T(8,128)} %collective-permute-done.5.near, f32[24,64,128]{2,1,0:T(8,128)S(1)} %collective-permute-done.6.far, ...), custom_call_target="tpu_custom_call" | custom-call | flops 1610612736 | bytes 3670016 | tf_op jit(solution)/shard_map/odd_gram/pallas_call | solution.py:154
  180.4 2.1 collective-permute-done.7.near
  182.5 1.3 last_gram.1
  183.8 4.1 %collective-permute-start.16 = (f32[192,128]{1,0:T(8,128)S(1)}, f32[192,128]{1,0:T(8,128)S(1)}, u32[]{:S(2)}, u32[]{:S(2)}) collective-permute-start(f32[192,128]{1,0:T(8,128)S(1)} %slice_select_fusion.1), channel_id=1, source_target_pairs={{0,1},{1,0},{2,3},{3,2},{4,5},{5,4},{6,7},{7,6},{8,9},{9,8},{10,11... | collective-permute-start | bytes 294920 | tf_op jit(solution)/shard_map/ppermute | solution.py:231
  188.9 1.3 collective-permute-start.17
  192.0 1.5 collective-permute-done.10
  194.3 4.8 %collective-permute-start.18 = (f32[96,128]{1,0:T(8,128)S(1)}, f32[96,128]{1,0:T(8,128)S(1)}, u32[]{:S(2)}, u32[]{:S(2)}) collective-permute-start(f32[96,128]{1,0:T(8,128)S(1)} %select_add_fusion.3), channel_id=1, source_target_pairs={{0,16},{4,20},{8,24},{12,28},{16,0},{20,4},{24,8},{28,12},{1,17},{... | collective-permute-start | bytes 147464 | tf_op jit(solution)/shard_map/ppermute | solution.py:233
  199.1 1.5 collective-permute-done.18
  201.8 1.6 collective-permute-start.12
  203.5 1.7 collective-permute-start.20
  205.3 2.3 collective-permute-start.13
  209.3 1.7 collective-permute-start.14
  211.1 5.8 %collective-permute-start.22 = (f32[192,128]{1,0:T(8,128)S(1)}, f32[192,128]{1,0:T(8,128)S(1)}, u32[]{:S(2)}, u32[]{:S(2)}) collective-permute-start(f32[192,128]{1,0:T(8,128)S(1)} %maximum_select_fusion.3), channel_id=1, source_target_pairs={{0,1},{1,0},{2,3},{3,2},{4,5},{5,4},{6,7},{7,6},{8,9},{9,8},{10,11... | collective-permute-start | bytes 294920 | tf_op jit(solution)/shard_map/ppermute | solution.py:235
  216.9 2.2 collective-permute-start.15
  219.2 8.4 %cholesky256.1 = (f32[256,256]{1,0:T(8,128)S(1)}, f32[256,256]{1,0:T(8,128)S(1)}) custom-call(f32[384,128]{1,0:T(8,128)S(1)} %maximum_select_fusion.1.gram_ref), custom_call_target="tpu_custom_call" | custom-call | flops 33554432 | bytes 786432 | tf_op jit(solution)/shard_map/cholesky256/pallas_call | solution.py:328
  227.6 7.2 %core.1 = (f32[512,256]{1,0:T(8,128)}, f32[256,4,8,128]{3,2,1,0:T(8,128)}) custom-call(s32[1]{0:T(128)} %bitcast.place_ref, f32[256,256]{1,0:T(8,128)S(1)} %maximum_select_fusion.below, f32[256,256]{1,0:T(8,128)S(1)} %get-tuple-element.44.upper, f32[256,256]{1,0:T(8,128)S(1)} %get-tuple-element.45.inverse, ...), custom_call_target="tpu_custom_call" | custom-call | flops 3221225472 | bytes 12582912 | tf_op jit(solution)/shard_map/core/pallas_call | solution.py:372
  (56 shorter events, 16.7 us)
Async XLA Ops:
  2.6 27.2 %collective-permute-start.2 = (f32[32,64,128]{2,1,0:T(8,128)S(1)}, f32[32,64,128]{2,1,0:T(8,128)S(1)}, u32[]{:S(2)}, u32[]{:S(2)}) collective-permute-start(f32[32,64,128]{2,1,0:T(8,128)S(1)} %bitcast.30), channel_id=1, source_target_pairs={{0,24},{4,28},{8,16},{12,20},{16,8},{20,12},{24,0},{28,4},{1,25},{... | collective-permute-start | bytes 3145736 | tf_op jit(solution)/shard_map/ppermute | solution.py:409
  12.8 83.3 %collective-permute-start.4 = (f32[32,64,128]{2,1,0:T(8,128)S(1)}, f32[32,64,128]{2,1,0:T(8,128)S(1)}, u32[]{:S(2)}, u32[]{:S(2)}) collective-permute-start(f32[32,64,128]{2,1,0:T(8,128)S(1)} %bitcast.31), channel_id=1, source_target_pairs={{0,16},{4,20},{8,24},{12,28},{16,0},{20,4},{24,8},{28,12},{1,17},{... | collective-permute-start | bytes 3145736 | tf_op jit(solution)/shard_map/ppermute | solution.py:408
  14.5 136.6 %collective-permute-start = (f32[32,64,128]{2,1,0:T(8,128)}, f32[32,64,128]{2,1,0:T(8,128)}, u32[]{:S(2)}, u32[]{:S(2)}) collective-permute-start(f32[32,64,128]{2,1,0:T(8,128)} %bitcast.6), channel_id=1, source_target_pairs={{0,4},{4,0},{8,12},{12,8},{16,20},{20,16},{24,28},{28,24},{1,5},{5... | collective-permute-start | bytes 3145736 | tf_op jit(solution)/shard_map/ppermute | solution.py:408
  17.3 134.7 %collective-permute-start.1 = (f32[32,64,128]{2,1,0:T(8,128)}, f32[32,64,128]{2,1,0:T(8,128)}, u32[]{:S(2)}, u32[]{:S(2)}) collective-permute-start(f32[32,64,128]{2,1,0:T(8,128)} %bitcast.8), channel_id=1, source_target_pairs={{0,8},{4,12},{8,0},{12,4},{16,24},{20,28},{24,16},{28,20},{1,9},{5... | collective-permute-start | bytes 3145736 | tf_op jit(solution)/shard_map/ppermute | solution.py:408
  29.8 122.3 %collective-permute-start.3 = (f32[32,64,128]{2,1,0:T(8,128)}, f32[32,64,128]{2,1,0:T(8,128)}, u32[]{:S(2)}, u32[]{:S(2)}) collective-permute-start(f32[32,64,128]{2,1,0:T(8,128)} %bitcast.10), channel_id=1, source_target_pairs={{0,12},{4,8},{8,4},{12,0},{16,28},{20,24},{24,20},{28,16},{1,13},{... | collective-permute-start | bytes 3145736 | tf_op jit(solution)/shard_map/ppermute | solution.py:408
  75.6 25.1 %copy-start = (f32[4,8,64,128]{3,2,1,0:T(8,128)}, f32[4,8,64,128]{3,2,1,0:T(8,128)S(1)}, u32[]{:S(2)}) copy-start(f32[4,8,64,128]{3,2,1,0:T(8,128)S(1)} %copy.12) | copy-start | bytes 3145732
  97.1 20.6 %collective-permute-start.6 = (f32[24,64,128]{2,1,0:T(8,128)}, f32[24,64,128]{2,1,0:T(8,128)S(1)}, u32[]{:S(2)}, u32[]{:S(2)}) collective-permute-start(f32[24,64,128]{2,1,0:T(8,128)} %slice.45), channel_id=1, source_target_pairs={{0,28},{4,24},{8,20},{12,16},{16,12},{20,8},{24,4},{28,0},{1,29},{... | collective-permute-start | bytes 2359304 | tf_op jit(solution)/shard_map/ppermute | solution.py:416
  100.7 1.1 copy-start.1
  102.8 74.2 %collective-permute-start.5 = (f32[24,64,128]{2,1,0:T(8,128)}, f32[24,64,128]{2,1,0:T(8,128)}, u32[]{:S(2)}, u32[]{:S(2)}) collective-permute-start(f32[24,64,128]{2,1,0:T(8,128)} %slice.44), channel_id=1, source_target_pairs={{0,20},{4,16},{8,28},{12,24},{16,4},{20,0},{24,12},{28,8},{1,21},{... | collective-permute-start | bytes 2359304 | tf_op jit(solution)/shard_map/ppermute | solution.py:416
  117.7 64.7 %collective-permute-start.7 = (f32[8,64,128]{2,1,0:T(8,128)S(1)}, f32[8,64,128]{2,1,0:T(8,128)S(1)}, u32[]{:S(2)}, u32[]{:S(2)}) collective-permute-start(f32[8,64,128]{2,1,0:T(8,128)S(1)} %slice.46), channel_id=1, source_target_pairs={{0,20},{4,16},{8,28},{12,24},{16,4},{20,0},{24,12},{28,8},{1,21},{... | collective-permute-start | bytes 786440 | tf_op jit(solution)/shard_map/ppermute | solution.py:418
  151.1 31.4 %collective-permute-start.8 = (f32[8,64,128]{2,1,0:T(8,128)S(1)}, f32[8,64,128]{2,1,0:T(8,128)S(1)}, u32[]{:S(2)}, u32[]{:S(2)}) collective-permute-start(f32[8,64,128]{2,1,0:T(8,128)S(1)} %slice.47), channel_id=1, source_target_pairs={{0,28},{4,24},{8,20},{12,16},{16,12},{20,8},{24,4},{28,0},{1,29},{... | collective-permute-start | bytes 786440 | tf_op jit(solution)/shard_map/ppermute | solution.py:419
  183.8 5.1 %collective-permute-start.16 = (f32[192,128]{1,0:T(8,128)S(1)}, f32[192,128]{1,0:T(8,128)S(1)}, u32[]{:S(2)}, u32[]{:S(2)}) collective-permute-start(f32[192,128]{1,0:T(8,128)S(1)} %slice_select_fusion.1), channel_id=1, source_target_pairs={{0,1},{1,0},{2,3},{3,2},{4,5},{5,4},{6,7},{7,6},{8,9},{9,8},{10,11... | collective-permute-start | bytes 294920 | tf_op jit(solution)/shard_map/ppermute | solution.py:231
  188.0 2.3 collective-permute-start.9
  188.9 3.0 %collective-permute-start.17 = (f32[96,128]{1,0:T(8,128)S(1)}, f32[96,128]{1,0:T(8,128)S(1)}, u32[]{:S(2)}, u32[]{:S(2)}) collective-permute-start(f32[96,128]{1,0:T(8,128)S(1)} %slice_select_fusion.3), channel_id=1, source_target_pairs={{0,2},{1,3},{2,0},{3,1},{4,6},{5,7},{6,4},{7,5},{8,10},{9,11},{10,... | collective-permute-start | bytes 147464 | tf_op jit(solution)/shard_map/ppermute | solution.py:231
  190.3 3.2 %collective-permute-start.10 = (f32[64,256]{1,0:T(8,128)S(1)}, f32[64,256]{1,0:T(8,128)S(1)}, u32[]{:S(2)}, u32[]{:S(2)}) collective-permute-start(f32[64,256]{1,0:T(8,128)S(1)} %slice_select_fusion.2), channel_id=1, source_target_pairs={{0,4},{4,0},{8,12},{12,8},{16,20},{20,16},{24,28},{28,24},{1,5},{5... | collective-permute-start | bytes 196616 | tf_op jit(solution)/shard_map/ppermute | solution.py:231
  193.5 8.3 %collective-permute-start.11 = (f32[64,256]{1,0:T(8,128)S(1)}, f32[64,256]{1,0:T(8,128)S(1)}, u32[]{:S(2)}, u32[]{:S(2)}) collective-permute-start(f32[64,256]{1,0:T(8,128)S(1)} %select_add_fusion.2), channel_id=1, source_target_pairs={{0,2},{1,3},{2,0},{3,1},{4,6},{5,7},{6,4},{7,5},{8,10},{9,11},{10,... | collective-permute-start | bytes 196616 | tf_op jit(solution)/shard_map/ppermute | solution.py:233
  194.3 6.3 %collective-permute-start.18 = (f32[96,128]{1,0:T(8,128)S(1)}, f32[96,128]{1,0:T(8,128)S(1)}, u32[]{:S(2)}, u32[]{:S(2)}) collective-permute-start(f32[96,128]{1,0:T(8,128)S(1)} %select_add_fusion.3), channel_id=1, source_target_pairs={{0,16},{4,20},{8,24},{12,28},{16,0},{20,4},{24,8},{28,12},{1,17},{... | collective-permute-start | bytes 147464 | tf_op jit(solution)/shard_map/ppermute | solution.py:233
  200.5 3.0 %collective-permute-start.19 = (f32[96,128]{1,0:T(8,128)S(1)}, f32[96,128]{1,0:T(8,128)S(1)}, u32[]{:S(2)}, u32[]{:S(2)}) collective-permute-start(f32[96,128]{1,0:T(8,128)S(1)} %add.69), channel_id=1, source_target_pairs={{0,4},{4,0},{8,12},{12,8},{16,20},{20,16},{24,28},{28,24},{1,5},{5... | collective-permute-start | bytes 147464 | tf_op jit(solution)/shard_map/ppermute | solution.py:233
  201.8 3.4 %collective-permute-start.12 = (f32[64,256]{1,0:T(8,128)S(1)}, f32[64,256]{1,0:T(8,128)S(1)}, u32[]{:S(2)}, u32[]{:S(2)}) collective-permute-start(f32[64,256]{1,0:T(8,128)S(1)} %add.64), channel_id=1, source_target_pairs={{0,8},{4,12},{8,0},{12,4},{16,24},{20,28},{24,16},{28,20},{1,9},{5... | collective-permute-start | bytes 196616 | tf_op jit(solution)/shard_map/ppermute | solution.py:233
  203.5 4.0 %collective-permute-start.20 = (f32[96,128]{1,0:T(8,128)S(1)}, f32[96,128]{1,0:T(8,128)S(1)}, u32[]{:S(2)}, u32[]{:S(2)}) collective-permute-start(f32[96,128]{1,0:T(8,128)S(1)} %add.70), channel_id=1, source_target_pairs={{0,8},{4,12},{8,0},{12,4},{16,24},{20,28},{24,16},{28,20},{1,9},{5... | collective-permute-start | bytes 147464 | tf_op jit(solution)/shard_map/ppermute | solution.py:233
  205.3 4.1 %collective-permute-start.13 = (f32[64,256]{1,0:T(8,128)S(1)}, f32[64,256]{1,0:T(8,128)S(1)}, u32[]{:S(2)}, u32[]{:S(2)}) collective-permute-start(f32[64,256]{1,0:T(8,128)S(1)} %add.65), channel_id=1, source_target_pairs={{0,16},{4,20},{8,24},{12,28},{16,0},{20,4},{24,8},{28,12},{1,17},{... | collective-permute-start | bytes 196616 | tf_op jit(solution)/shard_map/ppermute | solution.py:233
  207.6 3.5 %collective-permute-start.21 = (f32[96,128]{1,0:T(8,128)S(1)}, f32[96,128]{1,0:T(8,128)S(1)}, u32[]{:S(2)}, u32[]{:S(2)}) collective-permute-start(f32[96,128]{1,0:T(8,128)S(1)} %add.71), channel_id=1, source_target_pairs={{0,2},{1,3},{2,0},{3,1},{4,6},{5,7},{6,4},{7,5},{8,10},{9,11},{10,... | collective-permute-start | bytes 147464 | tf_op jit(solution)/shard_map/ppermute | solution.py:235
  209.3 7.6 %collective-permute-start.14 = (f32[64,256]{1,0:T(8,128)S(1)}, f32[64,256]{1,0:T(8,128)S(1)}, u32[]{:S(2)}, u32[]{:S(2)}) collective-permute-start(f32[64,256]{1,0:T(8,128)S(1)} %add.66), channel_id=1, source_target_pairs={{0,4},{4,0},{8,12},{12,8},{16,20},{20,16},{24,28},{28,24},{1,5},{5... | collective-permute-start | bytes 196616 | tf_op jit(solution)/shard_map/ppermute | solution.py:235
  211.1 8.1 %collective-permute-start.22 = (f32[192,128]{1,0:T(8,128)S(1)}, f32[192,128]{1,0:T(8,128)S(1)}, u32[]{:S(2)}, u32[]{:S(2)}) collective-permute-start(f32[192,128]{1,0:T(8,128)S(1)} %maximum_select_fusion.3), channel_id=1, source_target_pairs={{0,1},{1,0},{2,3},{3,2},{4,5},{5,4},{6,7},{7,6},{8,9},{9,8},{10,11... | collective-permute-start | bytes 294920 | tf_op jit(solution)/shard_map/ppermute | solution.py:235
  216.9 10.6 %collective-permute-start.15 = (f32[128,256]{1,0:T(8,128)S(1)}, f32[128,256]{1,0:T(8,128)S(1)}, u32[]{:S(2)}, u32[]{:S(2)}) collective-permute-start(f32[128,256]{1,0:T(8,128)S(1)} %maximum_select_fusion.2), channel_id=1, source_target_pairs={{0,1},{1,0},{2,3},{3,2},{4,5},{5,4},{6,7},{7,6},{8,9},{9,8},{10,11... | collective-permute-start | bytes 393224 | tf_op jit(solution)/shard_map/ppermute | solution.py:235

commit v6 on v5

--- a/solution.py
+++ b/solution.py
@@ -16,9 +16,14 @@
 VMEM_LIMIT = 16 * 1024 * 1024
 
 
+def split_off(x):
+    high = x.astype(jnp.bfloat16)
+    return high, x - high.astype(jnp.float32)
+
+
 def split(x):
-    high = x.astype(jnp.bfloat16)
-    return high, (x - high.astype(jnp.float32)).astype(jnp.bfloat16)
+    high, rest = split_off(x)
+    return high, rest.astype(jnp.bfloat16)
 
 
 def by_device(place, blocks):
@@ -240,8 +245,8 @@
 def sum_both(corner, below, wide, narrow):
     core, y = ("narrow", narrow, 1), ("narrow", narrow, 2)
     x, z_near, z_far = [("wide", wide, 1 << b) for b in range(3)]
-    corner = sum_over_all(corner, [core, y], [z_far, x, z_near])
-    below = sum_over_all(below, [core, x], [y, z_near, z_far])
+    corner = sum_over_all(corner, [core, y], [z_near, x, z_far])
+    below = sum_over_all(below, [core, x], [y, z_far, z_near])
     return corner, below
 
 
@@ -260,6 +265,18 @@
 
 def from_lane(v, c):
     return jnp.broadcast_to(v[:, c : c + 1], (SUB, LANES))
+
+
+def full_product(a, b):
+    def terms(x):
+        high, rest = split_off(x)
+        middle, rest = split_off(rest)
+        return high, middle, rest.astype(jnp.bfloat16)
+
+    (ah, am, al), (bh, bm, bl) = terms(a), terms(b)
+    left = jnp.concatenate([ah, ah, am, ah, am, al], axis=0)
+    right = jnp.concatenate([bh, bm, bh, bl, bm, bh], axis=0)
+    return lax.dot_general(left, right, (((0,), (0,)), ((), ())), preferred_element_type=jnp.float32)
 
 
 def cholesky_kernel(gram_ref, upper_ref, inverse_ref, work):
@@ -311,13 +328,7 @@
         if below < n:
             lo, hi = LANES * t0, n + LANES * (t0 + 1)
             first = below // LANES * LANES
-            update = lax.dot_general(
-                work[top:below, first:n],
-                work[top:below, lo:hi],
-                (((0,), (0,)), ((), ())),
-                precision=HIGHEST,
-                preferred_element_type=jnp.float32,
-            )
+            update = full_product(work[top:below, first:n], work[top:below, lo:hi])
             work[below:, lo:hi] = work[below:, lo:hi] - update[below - first :, :]
     upper_ref[...] = work[:, :n]
     inverse_ref[...] = work[:, n:]
@@ -330,7 +341,7 @@
         out_shape=[f32(n, n)] * 2,
         scratch_shapes=[pltpu.VMEM((n, 2 * n), jnp.float32)],
         compiler_params=pltpu.CompilerParams(vmem_limit_bytes=VMEM_LIMIT),
-        cost_estimate=pl.CostEstimate(flops=2 * n * n * n, bytes_accessed=12 * n * n, transcendentals=n),
+        cost_estimate=pl.CostEstimate(flops=64 * n * n * n, bytes_accessed=12 * n * n, transcendentals=n),
         name="cholesky256",
     )(packed)
 

time: 235 us -> 234 us (level)
  transfers between devices with their start and end apart: 23 -> 23, of which waited for: 11 -> 12; matrix products, arithmetic and copies ran while one was open for 8% -> 8% of each run, Pallas kernels for 9% -> 9%
where the time goes in v6:
time: 234 us; the launch traced here: 233 us
  starting transfers between devices  116 us (50%)
  waiting for transfers between devices  66.2 us (28%)
  Pallas kernels  29.1 us (12%)
  local copies, waits for them, and re-layouts  20.9 us (9%)
    ppermute x4, starting transfers between devices, on_device_blocks(): over(('wide', wide, k))(tie(block_for(snapshot, here ^ k, nz), *deps))  46.8 us
    ppermute x1, starting transfers between devices, on_device_blocks(): late[5] = over(('wide', wide, 5))(tie(blocks[5], got[7]))  33.4 us
    ppermute x2, waiting for transfers between devices, on_device_blocks(): got[k] = over(('wide', wide, k))(block[:split_at])  26.7 us
    ppermute x4, waiting for transfers between devices, on_device_blocks(): over(('wide', wide, k))(tie(block_for(snapshot, here ^ k, nz), *deps))  20.6 us
    transpose x10, local copies, waits for them, and re-layouts, block_for(): return cut.transpose(1, 2, 0, 3).reshape(ny * nz, rows, fields)  15.8 us
    pallas_call x4, Pallas kernels, call(): pl.pallas_call(kernel, grid=(steps,), in_specs=[pl.BlockSpec(memory_space...  14.2 us
    ppermute x6, starting transfers between devices, sum_over_all(): x = x + over(step)(x)  11.6 us
    ppermute x1, waiting for transfers between devices, on_device_blocks(): got[6] = over(('wide', wide, 6))(first)  10.5 us
  transfers between devices with their start and end apart: 23, of which 12 were waited for; matrix products, arithmetic and copies ran while one was open for 8% of the time, Pallas kernels for 9%

profile of v6, /device:TPU:1, one launch (start us, length us, event | category | flops | bytes accessed | tf_op | source)
XLA Modules:
  0.0 233.2 jit_solution(16246235196346168802)
XLA Ops:
  0.6 1.3 dynamic-slice_bitcast_fusion.7
  2.6 4.2 %collective-permute-start.2 = (f32[32,64,128]{2,1,0:T(8,128)S(1)}, f32[32,64,128]{2,1,0:T(8,128)S(1)}, u32[]{:S(2)}, u32[]{:S(2)}) collective-permute-start(f32[32,64,128]{2,1,0:T(8,128)S(1)} %bitcast.30), channel_id=1, source_target_pairs={{0,24},{4,28},{8,16},{12,20},{16,8},{20,12},{24,0},{28,4},{1,25},{... | collective-permute-start | bytes 3145736 | tf_op jit(solution)/shard_map/ppermute | solution.py:420
  6.8 5.4 %dynamic-slice_bitcast_fusion = (f32[4,8,64,128]{3,1,0,2:T(8,128)S(1)}, f32[4,8,64,128]{3,1,0,2:T(8,128)S(1)}, f32[4,8,64,128]{3,1,0,2:T(8,128)S(1)}, f32[4,8,64...) fusion(f32[64,4,64,128]{3,2,1,0:T(8,128)} %param.1, ...), kind=kLoop, calls=%fused_computation | loop fusion | bytes 14680092 | tf_op jit(solution)/shard_map/transpose | solution.py:409
  12.9 1.6 copy.7
  15.7 1.6 copy.8
  17.7 1.6 copy.9
  19.3 10.5 %collective-permute-done.2.far = f32[32,64,128]{2,1,0:T(8,128)S(1)} collective-permute-done((f32[32,64,128]{2,1,0:T(8,128)S(1)}, f32[32,64,128]{2,1,0:T(8,128)S(1)}, u32[]{:S(2)}, u32[]{:S(2)}) %collective-permute-start.2) | collective-permute-done | bytes 1048608 | tf_op jit(solution)/shard_map/ppermute | solution.py:420
  29.8 45.2 %collective-permute-start.3 = (f32[32,64,128]{2,1,0:T(8,128)}, f32[32,64,128]{2,1,0:T(8,128)}, u32[]{:S(2)}, u32[]{:S(2)}) collective-permute-start(f32[32,64,128]{2,1,0:T(8,128)} %bitcast.10), channel_id=1, source_target_pairs={{0,12},{4,8},{8,4},{12,0},{16,28},{20,24},{24,20},{28,16},{1,13},{... | collective-permute-start | bytes 3145736 | tf_op jit(solution)/shard_map/ppermute | solution.py:419
  75.6 20.6 %collective-permute-done.4.near = f32[32,64,128]{2,1,0:T(8,128)S(1)} collective-permute-done((f32[32,64,128]{2,1,0:T(8,128)S(1)}, f32[32,64,128]{2,1,0:T(8,128)S(1)}, u32[]{:S(2)}, u32[]{:S(2)}) %collective-permute-start.4) | collective-permute-done | bytes 1048608 | tf_op jit(solution)/shard_map/ppermute | solution.py:419
  97.1 2.9 %collective-permute-start.6 = (f32[24,64,128]{2,1,0:T(8,128)}, f32[24,64,128]{2,1,0:T(8,128)S(1)}, u32[]{:S(2)}, u32[]{:S(2)}) collective-permute-start(f32[24,64,128]{2,1,0:T(8,128)} %slice.45), channel_id=1, source_target_pairs={{0,28},{4,24},{8,20},{12,16},{16,12},{20,8},{24,4},{28,0},{1,29},{... | collective-permute-start | bytes 2359304 | tf_op jit(solution)/shard_map/ppermute | solution.py:427
  102.8 1.8 copy.6
  106.6 11.2 %collective-permute-done.6.far = f32[24,64,128]{2,1,0:T(8,128)S(1)} collective-permute-done((f32[24,64,128]{2,1,0:T(8,128)}, f32[24,64,128]{2,1,0:T(8,128)S(1)}, u32[]{:S(2)}, u32[]{:S(2)}) %collective-permute-start.6) | collective-permute-done | bytes 786464 | tf_op jit(solution)/shard_map/ppermute | solution.py:427
  117.7 33.4 %collective-permute-start.7 = (f32[8,64,128]{2,1,0:T(8,128)S(1)}, f32[8,64,128]{2,1,0:T(8,128)S(1)}, u32[]{:S(2)}, u32[]{:S(2)}) collective-permute-start(f32[8,64,128]{2,1,0:T(8,128)S(1)} %slice.46), channel_id=1, source_target_pairs={{0,20},{4,16},{8,28},{12,24},{16,4},{20,0},{24,12},{28,8},{1,21},{... | collective-permute-start | bytes 786440 | tf_op jit(solution)/shard_map/ppermute | solution.py:429
  152.0 5.1 %own_gram.1 = (f32[256,256]{1,0:T(8,128)S(1)}, bf16[16,256,256]{2,1,0:T(8,128)(2,1)S(1)}, bf16[16,256,256]{2,1,0:T(8,128)(2,1)S(1)}) custom-call(s32[1]{0:T(128)} %bitcast.place_ref, f32[32,64,128]{2,1,0:T(8,128)S(1)} %bitcast.25, f32[32,64,128]{2,1,0:T(8,128)} %collective-permute-done.refs_1_, f32[32,64,128]{2,1,0:T(8,128)} %collective-permute-done.1.refs_2_, ...), custom_call_target="tpu_custom_call" | custom-call | flops 2147483648 | bytes 8388608 | tf_op jit(solution)/shard_map/own_gram/pallas_call | solution.py:159
  157.1 4.3 %even_gram.1 = (f32[128,256]{1,0:T(8,128)S(1)}, f32[128,128]{1,0:T(8,128)S(1)}, bf16[16,128,256]{2,1,0:T(8,128)(2,1)S(1)}, bf16[16,128,256]{2,1,0:T(8,128)(2,1)S(1)}) custom-call(s32[1]{0:T(128)} %bitcast.place_ref, f32[32,64,128]{2,1,0:T(8,128)S(1)} %collective-permute-done.4.near, f32[32,64,128]{2,1,0:T(8,128)S(1)} %collective-permute-done.2.far, ...), custom_call_target="tpu_custom_call" | custom-call | flops 1610612736 | bytes 4194304 | tf_op jit(solution)/shard_map/even_gram/pallas_call | solution.py:159
  161.4 15.5 %collective-permute-done.5.near = f32[24,64,128]{2,1,0:T(8,128)} collective-permute-done((f32[24,64,128]{2,1,0:T(8,128)}, f32[24,64,128]{2,1,0:T(8,128)}, u32[]{:S(2)}, u32[]{:S(2)}) %collective-permute-start.5) | collective-permute-done | bytes 786464 | tf_op jit(solution)/shard_map/ppermute | solution.py:427
  176.9 3.5 %odd_gram.1 = (f32[512,128]{1,0:T(8,128)S(1)}, bf16[16,128,256]{2,1,0:T(8,128)(2,1)S(1)}, bf16[16,128,256]{2,1,0:T(8,128)(2,1)S(1)}) custom-call(s32[1]{0:T(128)} %bitcast.place_ref, f32[24,64,128]{2,1,0:T(8,128)} %collective-permute-done.5.near, f32[24,64,128]{2,1,0:T(8,128)S(1)} %collective-permute-done.6.far, ...), custom_call_target="tpu_custom_call" | custom-call | flops 1610612736 | bytes 3670016 | tf_op jit(solution)/shard_map/odd_gram/pallas_call | solution.py:159
  180.4 2.1 collective-permute-done.7.near
  182.5 1.3 last_gram.1
  183.8 4.1 %collective-permute-start.16 = (f32[192,128]{1,0:T(8,128)S(1)}, f32[192,128]{1,0:T(8,128)S(1)}, u32[]{:S(2)}, u32[]{:S(2)}) collective-permute-start(f32[192,128]{1,0:T(8,128)S(1)} %slice_select_fusion.1), channel_id=1, source_target_pairs={{0,1},{1,0},{2,3},{3,2},{4,5},{5,4},{6,7},{7,6},{8,9},{9,8},{10,11... | collective-permute-start | bytes 294920 | tf_op jit(solution)/shard_map/ppermute | solution.py:236
  188.9 1.3 collective-permute-start.17
  190.3 1.3 collective-permute-start.10
  192.0 1.5 collective-permute-done.10
  194.3 4.1 %collective-permute-start.18 = (f32[96,128]{1,0:T(8,128)S(1)}, f32[96,128]{1,0:T(8,128)S(1)}, u32[]{:S(2)}, u32[]{:S(2)}) collective-permute-start(f32[96,128]{1,0:T(8,128)S(1)} %select_add_fusion.3), channel_id=1, source_target_pairs={{0,8},{4,12},{8,0},{12,4},{16,24},{20,28},{24,16},{28,20},{1,9},{5... | collective-permute-start | bytes 147464 | tf_op jit(solution)/shard_map/ppermute | solution.py:238
  198.3 1.5 collective-permute-done.18
  201.0 2.4 %collective-permute-start.12 = (f32[64,256]{1,0:T(8,128)S(1)}, f32[64,256]{1,0:T(8,128)S(1)}, u32[]{:S(2)}, u32[]{:S(2)}) collective-permute-start(f32[64,256]{1,0:T(8,128)S(1)} %add.64), channel_id=1, source_target_pairs={{0,16},{4,20},{8,24},{12,28},{16,0},{20,4},{24,8},{28,12},{1,17},{... | collective-permute-start | bytes 196616 | tf_op jit(solution)/shard_map/ppermute | solution.py:238
  203.4 1.7 collective-permute-start.20
  205.1 1.5 collective-permute-start.13
  210.3 5.7 %collective-permute-start.22 = (f32[192,128]{1,0:T(8,128)S(1)}, f32[192,128]{1,0:T(8,128)S(1)}, u32[]{:S(2)}, u32[]{:S(2)}) collective-permute-start(f32[192,128]{1,0:T(8,128)S(1)} %maximum_select_fusion.3), channel_id=1, source_target_pairs={{0,1},{1,0},{2,3},{3,2},{4,5},{5,4},{6,7},{7,6},{8,9},{9,8},{10,11... | collective-permute-start | bytes 294920 | tf_op jit(solution)/shard_map/ppermute | solution.py:240
  216.0 2.2 collective-permute-start.15
  218.2 7.8 %cholesky256.1 = (f32[256,256]{1,0:T(8,128)S(1)}, f32[256,256]{1,0:T(8,128)S(1)}) custom-call(f32[384,128]{1,0:T(8,128)S(1)} %maximum_select_fusion.1.gram_ref), custom_call_target="tpu_custom_call" | custom-call | flops 1073741824 | bytes 786432 | tf_op jit(solution)/shard_map/cholesky256/pallas_call | solution.py:339
  226.0 7.2 %core.1 = (f32[512,256]{1,0:T(8,128)}, f32[256,4,8,128]{3,2,1,0:T(8,128)}) custom-call(s32[1]{0:T(128)} %bitcast.place_ref, f32[256,256]{1,0:T(8,128)S(1)} %maximum_select_fusion.below, f32[256,256]{1,0:T(8,128)S(1)} %get-tuple-element.44.upper, f32[256,256]{1,0:T(8,128)S(1)} %get-tuple-element.45.inverse, ...), custom_call_target="tpu_custom_call" | custom-call | flops 3221225472 | bytes 12582912 | tf_op jit(solution)/shard_map/core/pallas_call | solution.py:383
  (56 shorter events, 17.1 us)
Async XLA Ops:
  2.6 27.2 %collective-permute-start.2 = (f32[32,64,128]{2,1,0:T(8,128)S(1)}, f32[32,64,128]{2,1,0:T(8,128)S(1)}, u32[]{:S(2)}, u32[]{:S(2)}) collective-permute-start(f32[32,64,128]{2,1,0:T(8,128)S(1)} %bitcast.30), channel_id=1, source_target_pairs={{0,24},{4,28},{8,16},{12,20},{16,8},{20,12},{24,0},{28,4},{1,25},{... | collective-permute-start | bytes 3145736 | tf_op jit(solution)/shard_map/ppermute | solution.py:420
  12.8 83.3 %collective-permute-start.4 = (f32[32,64,128]{2,1,0:T(8,128)S(1)}, f32[32,64,128]{2,1,0:T(8,128)S(1)}, u32[]{:S(2)}, u32[]{:S(2)}) collective-permute-start(f32[32,64,128]{2,1,0:T(8,128)S(1)} %bitcast.31), channel_id=1, source_target_pairs={{0,16},{4,20},{8,24},{12,28},{16,0},{20,4},{24,8},{28,12},{1,17},{... | collective-permute-start | bytes 3145736 | tf_op jit(solution)/shard_map/ppermute | solution.py:419
  14.5 136.6 %collective-permute-start = (f32[32,64,128]{2,1,0:T(8,128)}, f32[32,64,128]{2,1,0:T(8,128)}, u32[]{:S(2)}, u32[]{:S(2)}) collective-permute-start(f32[32,64,128]{2,1,0:T(8,128)} %bitcast.6), channel_id=1, source_target_pairs={{0,4},{4,0},{8,12},{12,8},{16,20},{20,16},{24,28},{28,24},{1,5},{5... | collective-permute-start | bytes 3145736 | tf_op jit(solution)/shard_map/ppermute | solution.py:419
  17.3 134.7 %collective-permute-start.1 = (f32[32,64,128]{2,1,0:T(8,128)}, f32[32,64,128]{2,1,0:T(8,128)}, u32[]{:S(2)}, u32[]{:S(2)}) collective-permute-start(f32[32,64,128]{2,1,0:T(8,128)} %bitcast.8), channel_id=1, source_target_pairs={{0,8},{4,12},{8,0},{12,4},{16,24},{20,28},{24,16},{28,20},{1,9},{5... | collective-permute-start | bytes 3145736 | tf_op jit(solution)/shard_map/ppermute | solution.py:419
  29.8 122.3 %collective-permute-start.3 = (f32[32,64,128]{2,1,0:T(8,128)}, f32[32,64,128]{2,1,0:T(8,128)}, u32[]{:S(2)}, u32[]{:S(2)}) collective-permute-start(f32[32,64,128]{2,1,0:T(8,128)} %bitcast.10), channel_id=1, source_target_pairs={{0,12},{4,8},{8,4},{12,0},{16,28},{20,24},{24,20},{28,16},{1,13},{... | collective-permute-start | bytes 3145736 | tf_op jit(solution)/shard_map/ppermute | solution.py:419
  75.6 25.1 %copy-start = (f32[4,8,64,128]{3,2,1,0:T(8,128)}, f32[4,8,64,128]{3,2,1,0:T(8,128)S(1)}, u32[]{:S(2)}) copy-start(f32[4,8,64,128]{3,2,1,0:T(8,128)S(1)} %copy.12) | copy-start | bytes 3145732
  97.1 20.6 %collective-permute-start.6 = (f32[24,64,128]{2,1,0:T(8,128)}, f32[24,64,128]{2,1,0:T(8,128)S(1)}, u32[]{:S(2)}, u32[]{:S(2)}) collective-permute-start(f32[24,64,128]{2,1,0:T(8,128)} %slice.45), channel_id=1, source_target_pairs={{0,28},{4,24},{8,20},{12,16},{16,12},{20,8},{24,4},{28,0},{1,29},{... | collective-permute-start | bytes 2359304 | tf_op jit(solution)/shard_map/ppermute | solution.py:427
  100.7 1.1 copy-start.1
  102.8 74.2 %collective-permute-start.5 = (f32[24,64,128]{2,1,0:T(8,128)}, f32[24,64,128]{2,1,0:T(8,128)}, u32[]{:S(2)}, u32[]{:S(2)}) collective-permute-start(f32[24,64,128]{2,1,0:T(8,128)} %slice.44), channel_id=1, source_target_pairs={{0,20},{4,16},{8,28},{12,24},{16,4},{20,0},{24,12},{28,8},{1,21},{... | collective-permute-start | bytes 2359304 | tf_op jit(solution)/shard_map/ppermute | solution.py:427
  117.7 64.7 %collective-permute-start.7 = (f32[8,64,128]{2,1,0:T(8,128)S(1)}, f32[8,64,128]{2,1,0:T(8,128)S(1)}, u32[]{:S(2)}, u32[]{:S(2)}) collective-permute-start(f32[8,64,128]{2,1,0:T(8,128)S(1)} %slice.46), channel_id=1, source_target_pairs={{0,20},{4,16},{8,28},{12,24},{16,4},{20,0},{24,12},{28,8},{1,21},{... | collective-permute-start | bytes 786440 | tf_op jit(solution)/shard_map/ppermute | solution.py:429
  151.1 31.4 %collective-permute-start.8 = (f32[8,64,128]{2,1,0:T(8,128)S(1)}, f32[8,64,128]{2,1,0:T(8,128)S(1)}, u32[]{:S(2)}, u32[]{:S(2)}) collective-permute-start(f32[8,64,128]{2,1,0:T(8,128)S(1)} %slice.47), channel_id=1, source_target_pairs={{0,28},{4,24},{8,20},{12,16},{16,12},{20,8},{24,4},{28,0},{1,29},{... | collective-permute-start | bytes 786440 | tf_op jit(solution)/shard_map/ppermute | solution.py:430
  183.8 5.1 %collective-permute-start.16 = (f32[192,128]{1,0:T(8,128)S(1)}, f32[192,128]{1,0:T(8,128)S(1)}, u32[]{:S(2)}, u32[]{:S(2)}) collective-permute-start(f32[192,128]{1,0:T(8,128)S(1)} %slice_select_fusion.1), channel_id=1, source_target_pairs={{0,1},{1,0},{2,3},{3,2},{4,5},{5,4},{6,7},{7,6},{8,9},{9,8},{10,11... | collective-permute-start | bytes 294920 | tf_op jit(solution)/shard_map/ppermute | solution.py:236
  188.0 2.3 collective-permute-start.9
  188.9 3.0 %collective-permute-start.17 = (f32[96,128]{1,0:T(8,128)S(1)}, f32[96,128]{1,0:T(8,128)S(1)}, u32[]{:S(2)}, u32[]{:S(2)}) collective-permute-start(f32[96,128]{1,0:T(8,128)S(1)} %slice_select_fusion.3), channel_id=1, source_target_pairs={{0,2},{1,3},{2,0},{3,1},{4,6},{5,7},{6,4},{7,5},{8,10},{9,11},{10,... | collective-permute-start | bytes 147464 | tf_op jit(solution)/shard_map/ppermute | solution.py:236
  190.3 3.2 %collective-permute-start.10 = (f32[64,256]{1,0:T(8,128)S(1)}, f32[64,256]{1,0:T(8,128)S(1)}, u32[]{:S(2)}, u32[]{:S(2)}) collective-permute-start(f32[64,256]{1,0:T(8,128)S(1)} %slice_select_fusion.2), channel_id=1, source_target_pairs={{0,4},{4,0},{8,12},{12,8},{16,20},{20,16},{24,28},{28,24},{1,5},{5... | collective-permute-start | bytes 196616 | tf_op jit(solution)/shard_map/ppermute | solution.py:236
  193.5 7.5 %collective-permute-start.11 = (f32[64,256]{1,0:T(8,128)S(1)}, f32[64,256]{1,0:T(8,128)S(1)}, u32[]{:S(2)}, u32[]{:S(2)}) collective-permute-start(f32[64,256]{1,0:T(8,128)S(1)} %select_add_fusion.2), channel_id=1, source_target_pairs={{0,2},{1,3},{2,0},{3,1},{4,6},{5,7},{6,4},{7,5},{8,10},{9,11},{10,... | collective-permute-start | bytes 196616 | tf_op jit(solution)/shard_map/ppermute | solution.py:238
  194.3 5.5 %collective-permute-start.18 = (f32[96,128]{1,0:T(8,128)S(1)}, f32[96,128]{1,0:T(8,128)S(1)}, u32[]{:S(2)}, u32[]{:S(2)}) collective-permute-start(f32[96,128]{1,0:T(8,128)S(1)} %select_add_fusion.3), channel_id=1, source_target_pairs={{0,8},{4,12},{8,0},{12,4},{16,24},{20,28},{24,16},{28,20},{1,9},{5... | collective-permute-start | bytes 147464 | tf_op jit(solution)/shard_map/ppermute | solution.py:238
  199.8 3.6 %collective-permute-start.19 = (f32[96,128]{1,0:T(8,128)S(1)}, f32[96,128]{1,0:T(8,128)S(1)}, u32[]{:S(2)}, u32[]{:S(2)}) collective-permute-start(f32[96,128]{1,0:T(8,128)S(1)} %add.69), channel_id=1, source_target_pairs={{0,4},{4,0},{8,12},{12,8},{16,20},{20,16},{24,28},{28,24},{1,5},{5... | collective-permute-start | bytes 147464 | tf_op jit(solution)/shard_map/ppermute | solution.py:238
  201.0 4.1 %collective-permute-start.12 = (f32[64,256]{1,0:T(8,128)S(1)}, f32[64,256]{1,0:T(8,128)S(1)}, u32[]{:S(2)}, u32[]{:S(2)}) collective-permute-start(f32[64,256]{1,0:T(8,128)S(1)} %add.64), channel_id=1, source_target_pairs={{0,16},{4,20},{8,24},{12,28},{16,0},{20,4},{24,8},{28,12},{1,17},{... | collective-permute-start | bytes 196616 | tf_op jit(solution)/shard_map/ppermute | solution.py:238
  203.4 3.9 %collective-permute-start.20 = (f32[96,128]{1,0:T(8,128)S(1)}, f32[96,128]{1,0:T(8,128)S(1)}, u32[]{:S(2)}, u32[]{:S(2)}) collective-permute-start(f32[96,128]{1,0:T(8,128)S(1)} %add.70), channel_id=1, source_target_pairs={{0,16},{4,20},{8,24},{12,28},{16,0},{20,4},{24,8},{28,12},{1,17},{... | collective-permute-start | bytes 147464 | tf_op jit(solution)/shard_map/ppermute | solution.py:238
  205.1 3.9 %collective-permute-start.13 = (f32[64,256]{1,0:T(8,128)S(1)}, f32[64,256]{1,0:T(8,128)S(1)}, u32[]{:S(2)}, u32[]{:S(2)}) collective-permute-start(f32[64,256]{1,0:T(8,128)S(1)} %add.65), channel_id=1, source_target_pairs={{0,8},{4,12},{8,0},{12,4},{16,24},{20,28},{24,16},{28,20},{1,9},{5... | collective-permute-start | bytes 196616 | tf_op jit(solution)/shard_map/ppermute | solution.py:238
  207.3 3.0 %collective-permute-start.21 = (f32[96,128]{1,0:T(8,128)S(1)}, f32[96,128]{1,0:T(8,128)S(1)}, u32[]{:S(2)}, u32[]{:S(2)}) collective-permute-start(f32[96,128]{1,0:T(8,128)S(1)} %add.71), channel_id=1, source_target_pairs={{0,2},{1,3},{2,0},{3,1},{4,6},{5,7},{6,4},{7,5},{8,10},{9,11},{10,... | collective-permute-start | bytes 147464 | tf_op jit(solution)/shard_map/ppermute | solution.py:240
  209.0 7.0 %collective-permute-start.14 = (f32[64,256]{1,0:T(8,128)S(1)}, f32[64,256]{1,0:T(8,128)S(1)}, u32[]{:S(2)}, u32[]{:S(2)}) collective-permute-start(f32[64,256]{1,0:T(8,128)S(1)} %add.66), channel_id=1, source_target_pairs={{0,4},{4,0},{8,12},{12,8},{16,20},{20,16},{24,28},{28,24},{1,5},{5... | collective-permute-start | bytes 196616 | tf_op jit(solution)/shard_map/ppermute | solution.py:240
  210.3 7.9 %collective-permute-start.22 = (f32[192,128]{1,0:T(8,128)S(1)}, f32[192,128]{1,0:T(8,128)S(1)}, u32[]{:S(2)}, u32[]{:S(2)}) collective-permute-start(f32[192,128]{1,0:T(8,128)S(1)} %maximum_select_fusion.3), channel_id=1, source_target_pairs={{0,1},{1,0},{2,3},{3,2},{4,5},{5,4},{6,7},{7,6},{8,9},{9,8},{10,11... | collective-permute-start | bytes 294920 | tf_op jit(solution)/shard_map/ppermute | solution.py:240
  216.0 10.0 %collective-permute-start.15 = (f32[128,256]{1,0:T(8,128)S(1)}, f32[128,256]{1,0:T(8,128)S(1)}, u32[]{:S(2)}, u32[]{:S(2)}) collective-permute-start(f32[128,256]{1,0:T(8,128)S(1)} %maximum_select_fusion.2), channel_id=1, source_target_pairs={{0,1},{1,0},{2,3},{3,2},{4,5},{5,4},{6,7},{7,6},{8,9},{9,8},{10,11... | collective-permute-start | bytes 393224 | tf_op jit(solution)/shard_map/ppermute | solution.py:240

commit v7 on v6

--- a/solution.py
+++ b/solution.py
@@ -370,12 +370,13 @@
         weights[...] = jnp.concatenate([high, small, high], axis=1)
 
     w = weights[...]
+    cells = []
     for t in range(own_h.shape[0]):
         high = [r[t] for r in (own_h, even_h, odd_h)]
         small = [r[t] for r in (own_l, even_l, odd_l)]
         both = jnp.dot(w, jnp.concatenate(high + high + small, axis=0), preferred_element_type=jnp.float32)
-        out_ref[:, 0, 2 * t, :] = both[:, :LANES]
-        out_ref[:, 0, 2 * t + 1, :] = both[:, LANES:]
+        cells += [both[:, :LANES], both[:, LANES:]]
+    out_ref[:, 0, :, :] = jnp.swapaxes(jnp.stack(cells, axis=0), 0, 1)
 
 
 def core_and_factor(place, kept, streamed, ny, nz, fields):

time: 234 us -> 232 us (level)
  no operation moved by 1% of the time
where the time goes in v7:
time: 232 us
  starting transfers between devices  116 us (50%)
  waiting for transfers between devices  66.2 us (29%)
  Pallas kernels  28 us (12%)
  local copies, waits for them, and re-layouts  20.9 us (9%)
    ppermute x4, starting transfers between devices, on_device_blocks(): over(('wide', wide, k))(tie(block_for(snapshot, here ^ k, nz), *deps))  46.8 us
    ppermute x1, starting transfers between devices, on_device_blocks(): late[5] = over(('wide', wide, 5))(tie(blocks[5], got[7]))  33.4 us
    ppermute x2, waiting for transfers between devices, on_device_blocks(): got[k] = over(('wide', wide, k))(block[:split_at])  26.7 us
    ppermute x4, waiting for transfers between devices, on_device_blocks(): over(('wide', wide, k))(tie(block_for(snapshot, here ^ k, nz), *deps))  20.6 us
    transpose x10, local copies, waits for them, and re-layouts, block_for(): return cut.transpose(1, 2, 0, 3).reshape(ny * nz, rows, fields)  15.8 us
    pallas_call x4, Pallas kernels, call(): pl.pallas_call(kernel, grid=(steps,), in_specs=[pl.BlockSpec(memory_space...  14.2 us
    ppermute x6, starting transfers between devices, sum_over_all(): x = x + over(step)(x)  11.6 us
    ppermute x1, waiting for transfers between devices, on_device_blocks(): got[6] = over(('wide', wide, 6))(first)  10.5 us
  transfers between devices with their start and end apart: 23, of which 12 were waited for; matrix products, arithmetic and copies ran while one was open for 8% of the time, Pallas kernels for 9%

profile of v7, /device:TPU:1, one launch (start us, length us, event | category | flops | bytes accessed | tf_op | source)
XLA Modules:
  0.0 232.1 jit_solution(16929534194123261386)
XLA Ops:
  0.6 1.3 dynamic-slice_bitcast_fusion.7
  2.6 4.2 %collective-permute-start.2 = (f32[32,64,128]{2,1,0:T(8,128)S(1)}, f32[32,64,128]{2,1,0:T(8,128)S(1)}, u32[]{:S(2)}, u32[]{:S(2)}) collective-permute-start(f32[32,64,128]{2,1,0:T(8,128)S(1)} %bitcast.30), channel_id=1, source_target_pairs={{0,24},{4,28},{8,16},{12,20},{16,8},{20,12},{24,0},{28,4},{1,25},{... | collective-permute-start | bytes 3145736 | tf_op jit(solution)/shard_map/ppermute | solution.py:421
  6.8 5.4 %dynamic-slice_bitcast_fusion = (f32[4,8,64,128]{3,1,0,2:T(8,128)S(1)}, f32[4,8,64,128]{3,1,0,2:T(8,128)S(1)}, f32[4,8,64,128]{3,1,0,2:T(8,128)S(1)}, f32[4,8,64...) fusion(f32[64,4,64,128]{3,2,1,0:T(8,128)} %param.1, ...), kind=kLoop, calls=%fused_computation | loop fusion | bytes 14680092 | tf_op jit(solution)/shard_map/transpose | solution.py:410
  12.9 1.6 copy.7
  15.7 1.6 copy.8
  17.7 1.6 copy.9
  19.3 10.5 %collective-permute-done.2.far = f32[32,64,128]{2,1,0:T(8,128)S(1)} collective-permute-done((f32[32,64,128]{2,1,0:T(8,128)S(1)}, f32[32,64,128]{2,1,0:T(8,128)S(1)}, u32[]{:S(2)}, u32[]{:S(2)}) %collective-permute-start.2) | collective-permute-done | bytes 1048608 | tf_op jit(solution)/shard_map/ppermute | solution.py:421
  29.8 45.2 %collective-permute-start.3 = (f32[32,64,128]{2,1,0:T(8,128)}, f32[32,64,128]{2,1,0:T(8,128)}, u32[]{:S(2)}, u32[]{:S(2)}) collective-permute-start(f32[32,64,128]{2,1,0:T(8,128)} %bitcast.10), channel_id=1, source_target_pairs={{0,12},{4,8},{8,4},{12,0},{16,28},{20,24},{24,20},{28,16},{1,13},{... | collective-permute-start | bytes 3145736 | tf_op jit(solution)/shard_map/ppermute | solution.py:420
  75.6 20.6 %collective-permute-done.4.near = f32[32,64,128]{2,1,0:T(8,128)S(1)} collective-permute-done((f32[32,64,128]{2,1,0:T(8,128)S(1)}, f32[32,64,128]{2,1,0:T(8,128)S(1)}, u32[]{:S(2)}, u32[]{:S(2)}) %collective-permute-start.4) | collective-permute-done | bytes 1048608 | tf_op jit(solution)/shard_map/ppermute | solution.py:420
  97.1 2.9 %collective-permute-start.6 = (f32[24,64,128]{2,1,0:T(8,128)}, f32[24,64,128]{2,1,0:T(8,128)S(1)}, u32[]{:S(2)}, u32[]{:S(2)}) collective-permute-start(f32[24,64,128]{2,1,0:T(8,128)} %slice.45), channel_id=1, source_target_pairs={{0,28},{4,24},{8,20},{12,16},{16,12},{20,8},{24,4},{28,0},{1,29},{... | collective-permute-start | bytes 2359304 | tf_op jit(solution)/shard_map/ppermute | solution.py:428
  102.8 1.8 copy.6
  106.6 11.2 %collective-permute-done.6.far = f32[24,64,128]{2,1,0:T(8,128)S(1)} collective-permute-done((f32[24,64,128]{2,1,0:T(8,128)}, f32[24,64,128]{2,1,0:T(8,128)S(1)}, u32[]{:S(2)}, u32[]{:S(2)}) %collective-permute-start.6) | collective-permute-done | bytes 786464 | tf_op jit(solution)/shard_map/ppermute | solution.py:428
  117.7 33.4 %collective-permute-start.7 = (f32[8,64,128]{2,1,0:T(8,128)S(1)}, f32[8,64,128]{2,1,0:T(8,128)S(1)}, u32[]{:S(2)}, u32[]{:S(2)}) collective-permute-start(f32[8,64,128]{2,1,0:T(8,128)S(1)} %slice.46), channel_id=1, source_target_pairs={{0,20},{4,16},{8,28},{12,24},{16,4},{20,0},{24,12},{28,8},{1,21},{... | collective-permute-start | bytes 786440 | tf_op jit(solution)/shard_map/ppermute | solution.py:430
  152.0 5.1 %own_gram.1 = (f32[256,256]{1,0:T(8,128)S(1)}, bf16[16,256,256]{2,1,0:T(8,128)(2,1)S(1)}, bf16[16,256,256]{2,1,0:T(8,128)(2,1)S(1)}) custom-call(s32[1]{0:T(128)} %bitcast.place_ref, f32[32,64,128]{2,1,0:T(8,128)S(1)} %bitcast.25, f32[32,64,128]{2,1,0:T(8,128)} %collective-permute-done.refs_1_, f32[32,64,128]{2,1,0:T(8,128)} %collective-permute-done.1.refs_2_, ...), custom_call_target="tpu_custom_call" | custom-call | flops 2147483648 | bytes 8388608 | tf_op jit(solution)/shard_map/own_gram/pallas_call | solution.py:159
  157.1 4.3 %even_gram.1 = (f32[128,256]{1,0:T(8,128)S(1)}, f32[128,128]{1,0:T(8,128)S(1)}, bf16[16,128,256]{2,1,0:T(8,128)(2,1)S(1)}, bf16[16,128,256]{2,1,0:T(8,128)(2,1)S(1)}) custom-call(s32[1]{0:T(128)} %bitcast.place_ref, f32[32,64,128]{2,1,0:T(8,128)S(1)} %collective-permute-done.4.near, f32[32,64,128]{2,1,0:T(8,128)S(1)} %collective-permute-done.2.far, ...), custom_call_target="tpu_custom_call" | custom-call | flops 1610612736 | bytes 4194304 | tf_op jit(solution)/shard_map/even_gram/pallas_call | solution.py:159
  161.4 15.5 %collective-permute-done.5.near = f32[24,64,128]{2,1,0:T(8,128)} collective-permute-done((f32[24,64,128]{2,1,0:T(8,128)}, f32[24,64,128]{2,1,0:T(8,128)}, u32[]{:S(2)}, u32[]{:S(2)}) %collective-permute-start.5) | collective-permute-done | bytes 786464 | tf_op jit(solution)/shard_map/ppermute | solution.py:428
  176.9 3.5 %odd_gram.1 = (f32[512,128]{1,0:T(8,128)S(1)}, bf16[16,128,256]{2,1,0:T(8,128)(2,1)S(1)}, bf16[16,128,256]{2,1,0:T(8,128)(2,1)S(1)}) custom-call(s32[1]{0:T(128)} %bitcast.place_ref, f32[24,64,128]{2,1,0:T(8,128)} %collective-permute-done.5.near, f32[24,64,128]{2,1,0:T(8,128)S(1)} %collective-permute-done.6.far, ...), custom_call_target="tpu_custom_call" | custom-call | flops 1610612736 | bytes 3670016 | tf_op jit(solution)/shard_map/odd_gram/pallas_call | solution.py:159
  180.4 2.1 collective-permute-done.7.near
  182.5 1.3 last_gram.1
  183.8 4.1 %collective-permute-start.16 = (f32[192,128]{1,0:T(8,128)S(1)}, f32[192,128]{1,0:T(8,128)S(1)}, u32[]{:S(2)}, u32[]{:S(2)}) collective-permute-start(f32[192,128]{1,0:T(8,128)S(1)} %slice_select_fusion.1), channel_id=1, source_target_pairs={{0,1},{1,0},{2,3},{3,2},{4,5},{5,4},{6,7},{7,6},{8,9},{9,8},{10,11... | collective-permute-start | bytes 294920 | tf_op jit(solution)/shard_map/ppermute | solution.py:236
  188.9 1.3 collective-permute-start.17
  190.3 1.3 collective-permute-start.10
  192.0 1.5 collective-permute-done.10
  194.3 4.1 %collective-permute-start.18 = (f32[96,128]{1,0:T(8,128)S(1)}, f32[96,128]{1,0:T(8,128)S(1)}, u32[]{:S(2)}, u32[]{:S(2)}) collective-permute-start(f32[96,128]{1,0:T(8,128)S(1)} %select_add_fusion.3), channel_id=1, source_target_pairs={{0,8},{4,12},{8,0},{12,4},{16,24},{20,28},{24,16},{28,20},{1,9},{5... | collective-permute-start | bytes 147464 | tf_op jit(solution)/shard_map/ppermute | solution.py:238
  198.3 1.5 collective-permute-done.18
  201.0 2.4 %collective-permute-start.12 = (f32[64,256]{1,0:T(8,128)S(1)}, f32[64,256]{1,0:T(8,128)S(1)}, u32[]{:S(2)}, u32[]{:S(2)}) collective-permute-start(f32[64,256]{1,0:T(8,128)S(1)} %add.64), channel_id=1, source_target_pairs={{0,16},{4,20},{8,24},{12,28},{16,0},{20,4},{24,8},{28,12},{1,17},{... | collective-permute-start | bytes 196616 | tf_op jit(solution)/shard_map/ppermute | solution.py:238
  203.4 1.7 collective-permute-start.20
  205.1 1.5 collective-permute-start.13
  210.3 5.7 %collective-permute-start.22 = (f32[192,128]{1,0:T(8,128)S(1)}, f32[192,128]{1,0:T(8,128)S(1)}, u32[]{:S(2)}, u32[]{:S(2)}) collective-permute-start(f32[192,128]{1,0:T(8,128)S(1)} %maximum_select_fusion.3), channel_id=1, source_target_pairs={{0,1},{1,0},{2,3},{3,2},{4,5},{5,4},{6,7},{7,6},{8,9},{9,8},{10,11... | collective-permute-start | bytes 294920 | tf_op jit(solution)/shard_map/ppermute | solution.py:240
  216.0 2.2 collective-permute-start.15
  218.2 7.8 %cholesky256.1 = (f32[256,256]{1,0:T(8,128)S(1)}, f32[256,256]{1,0:T(8,128)S(1)}) custom-call(f32[384,128]{1,0:T(8,128)S(1)} %maximum_select_fusion.1.gram_ref), custom_call_target="tpu_custom_call" | custom-call | flops 1073741824 | bytes 786432 | tf_op jit(solution)/shard_map/cholesky256/pallas_call | solution.py:339
  226.0 6.0 %core.1 = (f32[512,256]{1,0:T(8,128)}, f32[256,4,8,128]{3,2,1,0:T(8,128)}) custom-call(s32[1]{0:T(128)} %bitcast.place_ref, f32[256,256]{1,0:T(8,128)S(1)} %maximum_select_fusion.below, f32[256,256]{1,0:T(8,128)S(1)} %get-tuple-element.44.upper, f32[256,256]{1,0:T(8,128)S(1)} %get-tuple-element.45.inverse, ...), custom_call_target="tpu_custom_call" | custom-call | flops 3221225472 | bytes 12582912 | tf_op jit(solution)/shard_map/core/pallas_call | solution.py:384
  (56 shorter events, 17.1 us)
Async XLA Ops:
  2.6 27.2 %collective-permute-start.2 = (f32[32,64,128]{2,1,0:T(8,128)S(1)}, f32[32,64,128]{2,1,0:T(8,128)S(1)}, u32[]{:S(2)}, u32[]{:S(2)}) collective-permute-start(f32[32,64,128]{2,1,0:T(8,128)S(1)} %bitcast.30), channel_id=1, source_target_pairs={{0,24},{4,28},{8,16},{12,20},{16,8},{20,12},{24,0},{28,4},{1,25},{... | collective-permute-start | bytes 3145736 | tf_op jit(solution)/shard_map/ppermute | solution.py:421
  12.8 83.3 %collective-permute-start.4 = (f32[32,64,128]{2,1,0:T(8,128)S(1)}, f32[32,64,128]{2,1,0:T(8,128)S(1)}, u32[]{:S(2)}, u32[]{:S(2)}) collective-permute-start(f32[32,64,128]{2,1,0:T(8,128)S(1)} %bitcast.31), channel_id=1, source_target_pairs={{0,16},{4,20},{8,24},{12,28},{16,0},{20,4},{24,8},{28,12},{1,17},{... | collective-permute-start | bytes 3145736 | tf_op jit(solution)/shard_map/ppermute | solution.py:420
  14.5 136.6 %collective-permute-start = (f32[32,64,128]{2,1,0:T(8,128)}, f32[32,64,128]{2,1,0:T(8,128)}, u32[]{:S(2)}, u32[]{:S(2)}) collective-permute-start(f32[32,64,128]{2,1,0:T(8,128)} %bitcast.6), channel_id=1, source_target_pairs={{0,4},{4,0},{8,12},{12,8},{16,20},{20,16},{24,28},{28,24},{1,5},{5... | collective-permute-start | bytes 3145736 | tf_op jit(solution)/shard_map/ppermute | solution.py:420
  17.3 134.7 %collective-permute-start.1 = (f32[32,64,128]{2,1,0:T(8,128)}, f32[32,64,128]{2,1,0:T(8,128)}, u32[]{:S(2)}, u32[]{:S(2)}) collective-permute-start(f32[32,64,128]{2,1,0:T(8,128)} %bitcast.8), channel_id=1, source_target_pairs={{0,8},{4,12},{8,0},{12,4},{16,24},{20,28},{24,16},{28,20},{1,9},{5... | collective-permute-start | bytes 3145736 | tf_op jit(solution)/shard_map/ppermute | solution.py:420
  29.8 122.3 %collective-permute-start.3 = (f32[32,64,128]{2,1,0:T(8,128)}, f32[32,64,128]{2,1,0:T(8,128)}, u32[]{:S(2)}, u32[]{:S(2)}) collective-permute-start(f32[32,64,128]{2,1,0:T(8,128)} %bitcast.10), channel_id=1, source_target_pairs={{0,12},{4,8},{8,4},{12,0},{16,28},{20,24},{24,20},{28,16},{1,13},{... | collective-permute-start | bytes 3145736 | tf_op jit(solution)/shard_map/ppermute | solution.py:420
  75.6 25.1 %copy-start = (f32[4,8,64,128]{3,2,1,0:T(8,128)}, f32[4,8,64,128]{3,2,1,0:T(8,128)S(1)}, u32[]{:S(2)}) copy-start(f32[4,8,64,128]{3,2,1,0:T(8,128)S(1)} %copy.12) | copy-start | bytes 3145732
  97.1 20.6 %collective-permute-start.6 = (f32[24,64,128]{2,1,0:T(8,128)}, f32[24,64,128]{2,1,0:T(8,128)S(1)}, u32[]{:S(2)}, u32[]{:S(2)}) collective-permute-start(f32[24,64,128]{2,1,0:T(8,128)} %slice.45), channel_id=1, source_target_pairs={{0,28},{4,24},{8,20},{12,16},{16,12},{20,8},{24,4},{28,0},{1,29},{... | collective-permute-start | bytes 2359304 | tf_op jit(solution)/shard_map/ppermute | solution.py:428
  100.7 1.1 copy-start.1
  102.8 74.2 %collective-permute-start.5 = (f32[24,64,128]{2,1,0:T(8,128)}, f32[24,64,128]{2,1,0:T(8,128)}, u32[]{:S(2)}, u32[]{:S(2)}) collective-permute-start(f32[24,64,128]{2,1,0:T(8,128)} %slice.44), channel_id=1, source_target_pairs={{0,20},{4,16},{8,28},{12,24},{16,4},{20,0},{24,12},{28,8},{1,21},{... | collective-permute-start | bytes 2359304 | tf_op jit(solution)/shard_map/ppermute | solution.py:428
  117.7 64.7 %collective-permute-start.7 = (f32[8,64,128]{2,1,0:T(8,128)S(1)}, f32[8,64,128]{2,1,0:T(8,128)S(1)}, u32[]{:S(2)}, u32[]{:S(2)}) collective-permute-start(f32[8,64,128]{2,1,0:T(8,128)S(1)} %slice.46), channel_id=1, source_target_pairs={{0,20},{4,16},{8,28},{12,24},{16,4},{20,0},{24,12},{28,8},{1,21},{... | collective-permute-start | bytes 786440 | tf_op jit(solution)/shard_map/ppermute | solution.py:430
  151.1 31.4 %collective-permute-start.8 = (f32[8,64,128]{2,1,0:T(8,128)S(1)}, f32[8,64,128]{2,1,0:T(8,128)S(1)}, u32[]{:S(2)}, u32[]{:S(2)}) collective-permute-start(f32[8,64,128]{2,1,0:T(8,128)S(1)} %slice.47), channel_id=1, source_target_pairs={{0,28},{4,24},{8,20},{12,16},{16,12},{20,8},{24,4},{28,0},{1,29},{... | collective-permute-start | bytes 786440 | tf_op jit(solution)/shard_map/ppermute | solution.py:431
  183.8 5.1 %collective-permute-start.16 = (f32[192,128]{1,0:T(8,128)S(1)}, f32[192,128]{1,0:T(8,128)S(1)}, u32[]{:S(2)}, u32[]{:S(2)}) collective-permute-start(f32[192,128]{1,0:T(8,128)S(1)} %slice_select_fusion.1), channel_id=1, source_target_pairs={{0,1},{1,0},{2,3},{3,2},{4,5},{5,4},{6,7},{7,6},{8,9},{9,8},{10,11... | collective-permute-start | bytes 294920 | tf_op jit(solution)/shard_map/ppermute | solution.py:236
  188.0 2.3 collective-permute-start.9
  188.9 3.0 %collective-permute-start.17 = (f32[96,128]{1,0:T(8,128)S(1)}, f32[96,128]{1,0:T(8,128)S(1)}, u32[]{:S(2)}, u32[]{:S(2)}) collective-permute-start(f32[96,128]{1,0:T(8,128)S(1)} %slice_select_fusion.3), channel_id=1, source_target_pairs={{0,2},{1,3},{2,0},{3,1},{4,6},{5,7},{6,4},{7,5},{8,10},{9,11},{10,... | collective-permute-start | bytes 147464 | tf_op jit(solution)/shard_map/ppermute | solution.py:236
  190.3 3.2 %collective-permute-start.10 = (f32[64,256]{1,0:T(8,128)S(1)}, f32[64,256]{1,0:T(8,128)S(1)}, u32[]{:S(2)}, u32[]{:S(2)}) collective-permute-start(f32[64,256]{1,0:T(8,128)S(1)} %slice_select_fusion.2), channel_id=1, source_target_pairs={{0,4},{4,0},{8,12},{12,8},{16,20},{20,16},{24,28},{28,24},{1,5},{5... | collective-permute-start | bytes 196616 | tf_op jit(solution)/shard_map/ppermute | solution.py:236
  193.5 7.5 %collective-permute-start.11 = (f32[64,256]{1,0:T(8,128)S(1)}, f32[64,256]{1,0:T(8,128)S(1)}, u32[]{:S(2)}, u32[]{:S(2)}) collective-permute-start(f32[64,256]{1,0:T(8,128)S(1)} %select_add_fusion.2), channel_id=1, source_target_pairs={{0,2},{1,3},{2,0},{3,1},{4,6},{5,7},{6,4},{7,5},{8,10},{9,11},{10,... | collective-permute-start | bytes 196616 | tf_op jit(solution)/shard_map/ppermute | solution.py:238
  194.3 5.5 %collective-permute-start.18 = (f32[96,128]{1,0:T(8,128)S(1)}, f32[96,128]{1,0:T(8,128)S(1)}, u32[]{:S(2)}, u32[]{:S(2)}) collective-permute-start(f32[96,128]{1,0:T(8,128)S(1)} %select_add_fusion.3), channel_id=1, source_target_pairs={{0,8},{4,12},{8,0},{12,4},{16,24},{20,28},{24,16},{28,20},{1,9},{5... | collective-permute-start | bytes 147464 | tf_op jit(solution)/shard_map/ppermute | solution.py:238
  199.8 3.6 %collective-permute-start.19 = (f32[96,128]{1,0:T(8,128)S(1)}, f32[96,128]{1,0:T(8,128)S(1)}, u32[]{:S(2)}, u32[]{:S(2)}) collective-permute-start(f32[96,128]{1,0:T(8,128)S(1)} %add.69), channel_id=1, source_target_pairs={{0,4},{4,0},{8,12},{12,8},{16,20},{20,16},{24,28},{28,24},{1,5},{5... | collective-permute-start | bytes 147464 | tf_op jit(solution)/shard_map/ppermute | solution.py:238
  201.0 4.1 %collective-permute-start.12 = (f32[64,256]{1,0:T(8,128)S(1)}, f32[64,256]{1,0:T(8,128)S(1)}, u32[]{:S(2)}, u32[]{:S(2)}) collective-permute-start(f32[64,256]{1,0:T(8,128)S(1)} %add.64), channel_id=1, source_target_pairs={{0,16},{4,20},{8,24},{12,28},{16,0},{20,4},{24,8},{28,12},{1,17},{... | collective-permute-start | bytes 196616 | tf_op jit(solution)/shard_map/ppermute | solution.py:238
  203.4 3.9 %collective-permute-start.20 = (f32[96,128]{1,0:T(8,128)S(1)}, f32[96,128]{1,0:T(8,128)S(1)}, u32[]{:S(2)}, u32[]{:S(2)}) collective-permute-start(f32[96,128]{1,0:T(8,128)S(1)} %add.70), channel_id=1, source_target_pairs={{0,16},{4,20},{8,24},{12,28},{16,0},{20,4},{24,8},{28,12},{1,17},{... | collective-permute-start | bytes 147464 | tf_op jit(solution)/shard_map/ppermute | solution.py:238
  205.1 3.9 %collective-permute-start.13 = (f32[64,256]{1,0:T(8,128)S(1)}, f32[64,256]{1,0:T(8,128)S(1)}, u32[]{:S(2)}, u32[]{:S(2)}) collective-permute-start(f32[64,256]{1,0:T(8,128)S(1)} %add.65), channel_id=1, source_target_pairs={{0,8},{4,12},{8,0},{12,4},{16,24},{20,28},{24,16},{28,20},{1,9},{5... | collective-permute-start | bytes 196616 | tf_op jit(solution)/shard_map/ppermute | solution.py:238
  207.3 3.0 %collective-permute-start.21 = (f32[96,128]{1,0:T(8,128)S(1)}, f32[96,128]{1,0:T(8,128)S(1)}, u32[]{:S(2)}, u32[]{:S(2)}) collective-permute-start(f32[96,128]{1,0:T(8,128)S(1)} %add.71), channel_id=1, source_target_pairs={{0,2},{1,3},{2,0},{3,1},{4,6},{5,7},{6,4},{7,5},{8,10},{9,11},{10,... | collective-permute-start | bytes 147464 | tf_op jit(solution)/shard_map/ppermute | solution.py:240
  209.0 7.0 %collective-permute-start.14 = (f32[64,256]{1,0:T(8,128)S(1)}, f32[64,256]{1,0:T(8,128)S(1)}, u32[]{:S(2)}, u32[]{:S(2)}) collective-permute-start(f32[64,256]{1,0:T(8,128)S(1)} %add.66), channel_id=1, source_target_pairs={{0,4},{4,0},{8,12},{12,8},{16,20},{20,16},{24,28},{28,24},{1,5},{5... | collective-permute-start | bytes 196616 | tf_op jit(solution)/shard_map/ppermute | solution.py:240
  210.3 7.9 %collective-permute-start.22 = (f32[192,128]{1,0:T(8,128)S(1)}, f32[192,128]{1,0:T(8,128)S(1)}, u32[]{:S(2)}, u32[]{:S(2)}) collective-permute-start(f32[192,128]{1,0:T(8,128)S(1)} %maximum_select_fusion.3), channel_id=1, source_target_pairs={{0,1},{1,0},{2,3},{3,2},{4,5},{5,4},{6,7},{7,6},{8,9},{9,8},{10,11... | collective-permute-start | bytes 294920 | tf_op jit(solution)/shard_map/ppermute | solution.py:240
  216.0 10.0 %collective-permute-start.15 = (f32[128,256]{1,0:T(8,128)S(1)}, f32[128,256]{1,0:T(8,128)S(1)}, u32[]{:S(2)}, u32[]{:S(2)}) collective-permute-start(f32[128,256]{1,0:T(8,128)S(1)} %maximum_select_fusion.2), channel_id=1, source_target_pairs={{0,1},{1,0},{2,3},{3,2},{4,5},{5,4},{6,7},{7,6},{8,9},{9,8},{10,11... | collective-permute-start | bytes 393224 | tf_op jit(solution)/shard_map/ppermute | solution.py:240

commit v8 on v7

--- a/solution.py
+++ b/solution.py
@@ -11,7 +11,7 @@
 LANES = 128
 FAST_WIDE, FAST_NARROW = 8, 4
 LATE = 1
-LATE_STEPS = 2
+LATE_STEPS = 1
 HIGHEST = lax.Precision.HIGHEST
 VMEM_LIMIT = 16 * 1024 * 1024
 
@@ -279,7 +279,7 @@
     return lax.dot_general(left, right, (((0,), (0,)), ((), ())), preferred_element_type=jnp.float32)
 
 
-def cholesky_kernel(gram_ref, upper_ref, inverse_ref, work):
+def cholesky_kernel(gram_ref, upper_ref, inverse_ref):
     n = upper_ref.shape[0]
     tiles = n // LANES
     groups = PANEL // SUB
@@ -287,16 +287,17 @@
     lane = lax.broadcasted_iota(jnp.int32, (SUB, LANES), 1)
     row_id = lax.broadcasted_iota(jnp.int32, (n, n), 0)
     col_id = lax.broadcasted_iota(jnp.int32, (n, n), 1)
-    work[:LANES, :LANES] = gram_ref[:LANES]
-    work[:LANES, LANES:n] = gram_ref[LANES : 2 * LANES]
-    work[LANES:, LANES:n] = gram_ref[2 * LANES :]
-    work[:, n:] = jnp.where(row_id == col_id, 1.0, 0.0)
+    upper_ref[:LANES, :LANES] = gram_ref[:LANES]
+    upper_ref[:LANES, LANES:] = gram_ref[LANES : 2 * LANES]
+    upper_ref[LANES:, LANES:] = gram_ref[2 * LANES :]
+    inverse_ref[...] = jnp.where(row_id == col_id, 1.0, 0.0)
     for top in range(0, n, PANEL):
         t0 = top // LANES
         cols = list(range(t0, tiles)) + [tiles + t for t in range(t0 + 1)]
         rows_of = lambda g: slice(top + SUB * g, top + SUB * (g + 1))
-        lanes_of = lambda t: slice(LANES * t, LANES * (t + 1))
-        grp = [[work[rows_of(g), lanes_of(t)] for t in cols] for g in range(groups)]
+        lanes_of = lambda t: slice(LANES * (t % tiles), LANES * (t % tiles + 1))
+        ref_of = lambda t: upper_ref if t < tiles else inverse_ref
+        grp = [[ref_of(t)[rows_of(g), lanes_of(t)] for t in cols] for g in range(groups)]
         pivots = [jnp.ones((SUB, LANES), jnp.float32) for _ in range(groups)]
         for g0 in range(groups):
             c0 = (top + SUB * g0) % LANES
@@ -321,17 +322,17 @@
                 v = v * scale
                 if t < tiles:
                     v = jnp.where(lane + LANES * t >= sub + (top + SUB * g), v, 0.0)
-                work[rows_of(g), lanes_of(t)] = v
+                ref_of(t)[rows_of(g), lanes_of(t)] = v
         for t in range(t0):
-            work[top : top + PANEL, lanes_of(t)] = jnp.zeros((PANEL, LANES), jnp.float32)
+            upper_ref[top : top + PANEL, lanes_of(t)] = jnp.zeros((PANEL, LANES), jnp.float32)
         below = top + PANEL
         if below < n:
-            lo, hi = LANES * t0, n + LANES * (t0 + 1)
+            lo, hi = LANES * t0, LANES * (t0 + 1)
             first = below // LANES * LANES
-            update = full_product(work[top:below, first:n], work[top:below, lo:hi])
-            work[below:, lo:hi] = work[below:, lo:hi] - update[below - first :, :]
-    upper_ref[...] = work[:, :n]
-    inverse_ref[...] = work[:, n:]
+            rows = jnp.concatenate([upper_ref[top:below, lo:], inverse_ref[top:below, :hi]], axis=1)
+            update = full_product(upper_ref[top:below, first:], rows)[below - first :]
+            upper_ref[below:, lo:] = upper_ref[below:, lo:] - update[:, : n - lo]
+            inverse_ref[below:, :hi] = inverse_ref[below:, :hi] - update[:, n - lo :]
 
 
 def cholesky(packed):
@@ -339,7 +340,6 @@
     return pl.pallas_call(
         cholesky_kernel,
         out_shape=[f32(n, n)] * 2,
-        scratch_shapes=[pltpu.VMEM((n, 2 * n), jnp.float32)],
         compiler_params=pltpu.CompilerParams(vmem_limit_bytes=VMEM_LIMIT),
         cost_estimate=pl.CostEstimate(flops=64 * n * n * n, bytes_accessed=12 * n * n, transcendentals=n),
         name="cholesky256",

time: 232 us -> 232 us (level)
  no operation moved by 1% of the time
where the time goes in v8:
time: 232 us
  starting transfers between devices  116 us (50%)
  waiting for transfers between devices  66.2 us (29%)
  Pallas kernels  27.6 us (12%)
  local copies, waits for them, and re-layouts  20.9 us (9%)
    ppermute x4, starting transfers between devices, on_device_blocks(): over(('wide', wide, k))(tie(block_for(snapshot, here ^ k, nz), *deps))  46.8 us
    ppermute x1, starting transfers between devices, on_device_blocks(): late[5] = over(('wide', wide, 5))(tie(blocks[5], got[7]))  33.4 us
    ppermute x2, waiting for transfers between devices, on_device_blocks(): got[k] = over(('wide', wide, k))(block[:split_at])  26.7 us
    ppermute x4, waiting for transfers between devices, on_device_blocks(): over(('wide', wide, k))(tie(block_for(snapshot, here ^ k, nz), *deps))  20.6 us
    transpose x10, local copies, waits for them, and re-layouts, block_for(): return cut.transpose(1, 2, 0, 3).reshape(ny * nz, rows, fields)  15.8 us
    pallas_call x4, Pallas kernels, call(): pl.pallas_call(kernel, grid=(steps,), in_specs=[pl.BlockSpec(memory_space...  13.8 us
    ppermute x6, starting transfers between devices, sum_over_all(): x = x + over(step)(x)  11.6 us
    ppermute x1, waiting for transfers between devices, on_device_blocks(): got[6] = over(('wide', wide, 6))(first)  10.5 us
  transfers between devices with their start and end apart: 23, of which 12 were waited for; matrix products, arithmetic and copies ran while one was open for 8% of the time, Pallas kernels for 9%

profile of v8, /device:TPU:1, one launch (start us, length us, event | category | flops | bytes accessed | tf_op | source)
XLA Modules:
  0.0 231.6 jit_solution(9359753339477951226)
XLA Ops:
  0.6 1.3 dynamic-slice_bitcast_fusion.7
  2.6 4.2 %collective-permute-start.2 = (f32[32,64,128]{2,1,0:T(8,128)S(1)}, f32[32,64,128]{2,1,0:T(8,128)S(1)}, u32[]{:S(2)}, u32[]{:S(2)}) collective-permute-start(f32[32,64,128]{2,1,0:T(8,128)S(1)} %bitcast.30), channel_id=1, source_target_pairs={{0,24},{4,28},{8,16},{12,20},{16,8},{20,12},{24,0},{28,4},{1,25},{... | collective-permute-start | bytes 3145736 | tf_op jit(solution)/shard_map/ppermute | solution.py:421
  6.8 5.4 %dynamic-slice_bitcast_fusion = (f32[4,8,64,128]{3,1,0,2:T(8,128)S(1)}, f32[4,8,64,128]{3,1,0,2:T(8,128)S(1)}, f32[4,8,64,128]{3,1,0,2:T(8,128)S(1)}, f32[4,8,64...) fusion(f32[64,4,64,128]{3,2,1,0:T(8,128)} %param.1, ...), kind=kLoop, calls=%fused_computation | loop fusion | bytes 14680092 | tf_op jit(solution)/shard_map/transpose | solution.py:410
  12.9 1.6 copy.7
  14.5 1.2 collective-permute-start
  15.7 1.6 copy.8
  17.7 1.6 copy.9
  19.3 10.5 %collective-permute-done.2.far = f32[32,64,128]{2,1,0:T(8,128)S(1)} collective-permute-done((f32[32,64,128]{2,1,0:T(8,128)S(1)}, f32[32,64,128]{2,1,0:T(8,128)S(1)}, u32[]{:S(2)}, u32[]{:S(2)}) %collective-permute-start.2) | collective-permute-done | bytes 1048608 | tf_op jit(solution)/shard_map/ppermute | solution.py:421
  29.8 45.2 %collective-permute-start.3 = (f32[32,64,128]{2,1,0:T(8,128)}, f32[32,64,128]{2,1,0:T(8,128)}, u32[]{:S(2)}, u32[]{:S(2)}) collective-permute-start(f32[32,64,128]{2,1,0:T(8,128)} %bitcast.10), channel_id=1, source_target_pairs={{0,12},{4,8},{8,4},{12,0},{16,28},{20,24},{24,20},{28,16},{1,13},{... | collective-permute-start | bytes 3145736 | tf_op jit(solution)/shard_map/ppermute | solution.py:420
  75.6 20.6 %collective-permute-done.4.near = f32[32,64,128]{2,1,0:T(8,128)S(1)} collective-permute-done((f32[32,64,128]{2,1,0:T(8,128)S(1)}, f32[32,64,128]{2,1,0:T(8,128)S(1)}, u32[]{:S(2)}, u32[]{:S(2)}) %collective-permute-start.4) | collective-permute-done | bytes 1048608 | tf_op jit(solution)/shard_map/ppermute | solution.py:420
  97.1 2.9 %collective-permute-start.6 = (f32[24,64,128]{2,1,0:T(8,128)}, f32[24,64,128]{2,1,0:T(8,128)S(1)}, u32[]{:S(2)}, u32[]{:S(2)}) collective-permute-start(f32[24,64,128]{2,1,0:T(8,128)} %slice.45), channel_id=1, source_target_pairs={{0,28},{4,24},{8,20},{12,16},{16,12},{20,8},{24,4},{28,0},{1,29},{... | collective-permute-start | bytes 2359304 | tf_op jit(solution)/shard_map/ppermute | solution.py:428
  102.8 1.8 copy.6
  106.6 11.2 %collective-permute-done.6.far = f32[24,64,128]{2,1,0:T(8,128)S(1)} collective-permute-done((f32[24,64,128]{2,1,0:T(8,128)}, f32[24,64,128]{2,1,0:T(8,128)S(1)}, u32[]{:S(2)}, u32[]{:S(2)}) %collective-permute-start.6) | collective-permute-done | bytes 786464 | tf_op jit(solution)/shard_map/ppermute | solution.py:428
  117.7 33.4 %collective-permute-start.7 = (f32[8,64,128]{2,1,0:T(8,128)S(1)}, f32[8,64,128]{2,1,0:T(8,128)S(1)}, u32[]{:S(2)}, u32[]{:S(2)}) collective-permute-start(f32[8,64,128]{2,1,0:T(8,128)S(1)} %slice.46), channel_id=1, source_target_pairs={{0,20},{4,16},{8,28},{12,24},{16,4},{20,0},{24,12},{28,8},{1,21},{... | collective-permute-start | bytes 786440 | tf_op jit(solution)/shard_map/ppermute | solution.py:430
  152.0 5.1 %own_gram.1 = (f32[256,256]{1,0:T(8,128)S(1)}, bf16[16,256,256]{2,1,0:T(8,128)(2,1)S(1)}, bf16[16,256,256]{2,1,0:T(8,128)(2,1)S(1)}) custom-call(s32[1]{0:T(128)} %bitcast.place_ref, f32[32,64,128]{2,1,0:T(8,128)S(1)} %bitcast.25, f32[32,64,128]{2,1,0:T(8,128)} %collective-permute-done.refs_1_, f32[32,64,128]{2,1,0:T(8,128)} %collective-permute-done.1.refs_2_, ...), custom_call_target="tpu_custom_call" | custom-call | flops 2147483648 | bytes 8388608 | tf_op jit(solution)/shard_map/own_gram/pallas_call | solution.py:159
  157.1 4.3 %even_gram.1 = (f32[128,256]{1,0:T(8,128)S(1)}, f32[128,128]{1,0:T(8,128)S(1)}, bf16[16,128,256]{2,1,0:T(8,128)(2,1)S(1)}, bf16[16,128,256]{2,1,0:T(8,128)(2,1)S(1)}) custom-call(s32[1]{0:T(128)} %bitcast.place_ref, f32[32,64,128]{2,1,0:T(8,128)S(1)} %collective-permute-done.4.near, f32[32,64,128]{2,1,0:T(8,128)S(1)} %collective-permute-done.2.far, ...), custom_call_target="tpu_custom_call" | custom-call | flops 1610612736 | bytes 4194304 | tf_op jit(solution)/shard_map/even_gram/pallas_call | solution.py:159
  161.4 15.5 %collective-permute-done.5.near = f32[24,64,128]{2,1,0:T(8,128)} collective-permute-done((f32[24,64,128]{2,1,0:T(8,128)}, f32[24,64,128]{2,1,0:T(8,128)}, u32[]{:S(2)}, u32[]{:S(2)}) %collective-permute-start.5) | collective-permute-done | bytes 786464 | tf_op jit(solution)/shard_map/ppermute | solution.py:428
  176.9 3.5 %odd_gram.1 = (f32[512,128]{1,0:T(8,128)S(1)}, bf16[16,128,256]{2,1,0:T(8,128)(2,1)S(1)}, bf16[16,128,256]{2,1,0:T(8,128)(2,1)S(1)}) custom-call(s32[1]{0:T(128)} %bitcast.place_ref, f32[24,64,128]{2,1,0:T(8,128)} %collective-permute-done.5.near, f32[24,64,128]{2,1,0:T(8,128)S(1)} %collective-permute-done.6.far, ...), custom_call_target="tpu_custom_call" | custom-call | flops 1610612736 | bytes 3670016 | tf_op jit(solution)/shard_map/odd_gram/pallas_call | solution.py:159
  180.4 2.1 collective-permute-done.7.near
  183.4 4.2 %collective-permute-start.16 = (f32[192,128]{1,0:T(8,128)S(1)}, f32[192,128]{1,0:T(8,128)S(1)}, u32[]{:S(2)}, u32[]{:S(2)}) collective-permute-start(f32[192,128]{1,0:T(8,128)S(1)} %slice_select_fusion.1), channel_id=1, source_target_pairs={{0,1},{1,0},{2,3},{3,2},{4,5},{5,4},{6,7},{7,6},{8,9},{9,8},{10,11... | collective-permute-start | bytes 294920 | tf_op jit(solution)/shard_map/ppermute | solution.py:236
  188.6 1.3 collective-permute-start.17
  189.9 1.3 collective-permute-start.10
  191.6 1.5 collective-permute-done.10
  193.9 4.0 %collective-permute-start.18 = (f32[96,128]{1,0:T(8,128)S(1)}, f32[96,128]{1,0:T(8,128)S(1)}, u32[]{:S(2)}, u32[]{:S(2)}) collective-permute-start(f32[96,128]{1,0:T(8,128)S(1)} %select_add_fusion.3), channel_id=1, source_target_pairs={{0,8},{4,12},{8,0},{12,4},{16,24},{20,28},{24,16},{28,20},{1,9},{5... | collective-permute-start | bytes 147464 | tf_op jit(solution)/shard_map/ppermute | solution.py:238
  197.9 1.5 collective-permute-done.18
  200.6 2.4 %collective-permute-start.12 = (f32[64,256]{1,0:T(8,128)S(1)}, f32[64,256]{1,0:T(8,128)S(1)}, u32[]{:S(2)}, u32[]{:S(2)}) collective-permute-start(f32[64,256]{1,0:T(8,128)S(1)} %add.64), channel_id=1, source_target_pairs={{0,16},{4,20},{8,24},{12,28},{16,0},{20,4},{24,8},{28,12},{1,17},{... | collective-permute-start | bytes 196616 | tf_op jit(solution)/shard_map/ppermute | solution.py:238
  203.0 1.7 collective-permute-start.20
  204.7 1.5 collective-permute-start.13
  209.9 5.7 %collective-permute-start.22 = (f32[192,128]{1,0:T(8,128)S(1)}, f32[192,128]{1,0:T(8,128)S(1)}, u32[]{:S(2)}, u32[]{:S(2)}) collective-permute-start(f32[192,128]{1,0:T(8,128)S(1)} %maximum_select_fusion.3), channel_id=1, source_target_pairs={{0,1},{1,0},{2,3},{3,2},{4,5},{5,4},{6,7},{7,6},{8,9},{9,8},{10,11... | collective-permute-start | bytes 294920 | tf_op jit(solution)/shard_map/ppermute | solution.py:240
  215.6 2.2 collective-permute-start.15
  217.8 7.8 %cholesky256.1 = (f32[256,256]{1,0:T(8,128)S(1)}, f32[256,256]{1,0:T(8,128)S(1)}) custom-call(f32[384,128]{1,0:T(8,128)S(1)} %maximum_select_fusion.1.gram_ref), custom_call_target="tpu_custom_call" | custom-call | flops 1073741824 | bytes 786432 | tf_op jit(solution)/shard_map/cholesky256/pallas_call | solution.py:340
  225.6 6.0 %core.1 = (f32[512,256]{1,0:T(8,128)}, f32[256,4,8,128]{3,2,1,0:T(8,128)}) custom-call(s32[1]{0:T(128)} %bitcast.place_ref, f32[256,256]{1,0:T(8,128)S(1)} %maximum_select_fusion.below, f32[256,256]{1,0:T(8,128)S(1)} %get-tuple-element.44.upper, f32[256,256]{1,0:T(8,128)S(1)} %get-tuple-element.45.inverse, ...), custom_call_target="tpu_custom_call" | custom-call | flops 3221225472 | bytes 12582912 | tf_op jit(solution)/shard_map/core/pallas_call | solution.py:384
  (56 shorter events, 16.9 us)
Async XLA Ops:
  2.6 27.2 %collective-permute-start.2 = (f32[32,64,128]{2,1,0:T(8,128)S(1)}, f32[32,64,128]{2,1,0:T(8,128)S(1)}, u32[]{:S(2)}, u32[]{:S(2)}) collective-permute-start(f32[32,64,128]{2,1,0:T(8,128)S(1)} %bitcast.30), channel_id=1, source_target_pairs={{0,24},{4,28},{8,16},{12,20},{16,8},{20,12},{24,0},{28,4},{1,25},{... | collective-permute-start | bytes 3145736 | tf_op jit(solution)/shard_map/ppermute | solution.py:421
  12.8 83.3 %collective-permute-start.4 = (f32[32,64,128]{2,1,0:T(8,128)S(1)}, f32[32,64,128]{2,1,0:T(8,128)S(1)}, u32[]{:S(2)}, u32[]{:S(2)}) collective-permute-start(f32[32,64,128]{2,1,0:T(8,128)S(1)} %bitcast.31), channel_id=1, source_target_pairs={{0,16},{4,20},{8,24},{12,28},{16,0},{20,4},{24,8},{28,12},{1,17},{... | collective-permute-start | bytes 3145736 | tf_op jit(solution)/shard_map/ppermute | solution.py:420
  14.5 136.6 %collective-permute-start = (f32[32,64,128]{2,1,0:T(8,128)}, f32[32,64,128]{2,1,0:T(8,128)}, u32[]{:S(2)}, u32[]{:S(2)}) collective-permute-start(f32[32,64,128]{2,1,0:T(8,128)} %bitcast.6), channel_id=1, source_target_pairs={{0,4},{4,0},{8,12},{12,8},{16,20},{20,16},{24,28},{28,24},{1,5},{5... | collective-permute-start | bytes 3145736 | tf_op jit(solution)/shard_map/ppermute | solution.py:420
  17.3 134.7 %collective-permute-start.1 = (f32[32,64,128]{2,1,0:T(8,128)}, f32[32,64,128]{2,1,0:T(8,128)}, u32[]{:S(2)}, u32[]{:S(2)}) collective-permute-start(f32[32,64,128]{2,1,0:T(8,128)} %bitcast.8), channel_id=1, source_target_pairs={{0,8},{4,12},{8,0},{12,4},{16,24},{20,28},{24,16},{28,20},{1,9},{5... | collective-permute-start | bytes 3145736 | tf_op jit(solution)/shard_map/ppermute | solution.py:420
  29.8 122.3 %collective-permute-start.3 = (f32[32,64,128]{2,1,0:T(8,128)}, f32[32,64,128]{2,1,0:T(8,128)}, u32[]{:S(2)}, u32[]{:S(2)}) collective-permute-start(f32[32,64,128]{2,1,0:T(8,128)} %bitcast.10), channel_id=1, source_target_pairs={{0,12},{4,8},{8,4},{12,0},{16,28},{20,24},{24,20},{28,16},{1,13},{... | collective-permute-start | bytes 3145736 | tf_op jit(solution)/shard_map/ppermute | solution.py:420
  75.6 25.1 %copy-start = (f32[4,8,64,128]{3,2,1,0:T(8,128)}, f32[4,8,64,128]{3,2,1,0:T(8,128)S(1)}, u32[]{:S(2)}) copy-start(f32[4,8,64,128]{3,2,1,0:T(8,128)S(1)} %copy.12) | copy-start | bytes 3145732
  97.1 20.6 %collective-permute-start.6 = (f32[24,64,128]{2,1,0:T(8,128)}, f32[24,64,128]{2,1,0:T(8,128)S(1)}, u32[]{:S(2)}, u32[]{:S(2)}) collective-permute-start(f32[24,64,128]{2,1,0:T(8,128)} %slice.45), channel_id=1, source_target_pairs={{0,28},{4,24},{8,20},{12,16},{16,12},{20,8},{24,4},{28,0},{1,29},{... | collective-permute-start | bytes 2359304 | tf_op jit(solution)/shard_map/ppermute | solution.py:428
  100.7 1.1 copy-start.1
  102.8 74.2 %collective-permute-start.5 = (f32[24,64,128]{2,1,0:T(8,128)}, f32[24,64,128]{2,1,0:T(8,128)}, u32[]{:S(2)}, u32[]{:S(2)}) collective-permute-start(f32[24,64,128]{2,1,0:T(8,128)} %slice.44), channel_id=1, source_target_pairs={{0,20},{4,16},{8,28},{12,24},{16,4},{20,0},{24,12},{28,8},{1,21},{... | collective-permute-start | bytes 2359304 | tf_op jit(solution)/shard_map/ppermute | solution.py:428
  117.7 64.7 %collective-permute-start.7 = (f32[8,64,128]{2,1,0:T(8,128)S(1)}, f32[8,64,128]{2,1,0:T(8,128)S(1)}, u32[]{:S(2)}, u32[]{:S(2)}) collective-permute-start(f32[8,64,128]{2,1,0:T(8,128)S(1)} %slice.46), channel_id=1, source_target_pairs={{0,20},{4,16},{8,28},{12,24},{16,4},{20,0},{24,12},{28,8},{1,21},{... | collective-permute-start | bytes 786440 | tf_op jit(solution)/shard_map/ppermute | solution.py:430
  151.1 31.4 %collective-permute-start.8 = (f32[8,64,128]{2,1,0:T(8,128)S(1)}, f32[8,64,128]{2,1,0:T(8,128)S(1)}, u32[]{:S(2)}, u32[]{:S(2)}) collective-permute-start(f32[8,64,128]{2,1,0:T(8,128)S(1)} %slice.47), channel_id=1, source_target_pairs={{0,28},{4,24},{8,20},{12,16},{16,12},{20,8},{24,4},{28,0},{1,29},{... | collective-permute-start | bytes 786440 | tf_op jit(solution)/shard_map/ppermute | solution.py:431
  183.4 5.1 %collective-permute-start.16 = (f32[192,128]{1,0:T(8,128)S(1)}, f32[192,128]{1,0:T(8,128)S(1)}, u32[]{:S(2)}, u32[]{:S(2)}) collective-permute-start(f32[192,128]{1,0:T(8,128)S(1)} %slice_select_fusion.1), channel_id=1, source_target_pairs={{0,1},{1,0},{2,3},{3,2},{4,5},{5,4},{6,7},{7,6},{8,9},{9,8},{10,11... | collective-permute-start | bytes 294920 | tf_op jit(solution)/shard_map/ppermute | solution.py:236
  187.6 2.3 collective-permute-start.9
  188.6 3.0 %collective-permute-start.17 = (f32[96,128]{1,0:T(8,128)S(1)}, f32[96,128]{1,0:T(8,128)S(1)}, u32[]{:S(2)}, u32[]{:S(2)}) collective-permute-start(f32[96,128]{1,0:T(8,128)S(1)} %slice_select_fusion.3), channel_id=1, source_target_pairs={{0,2},{1,3},{2,0},{3,1},{4,6},{5,7},{6,4},{7,5},{8,10},{9,11},{10,... | collective-permute-start | bytes 147464 | tf_op jit(solution)/shard_map/ppermute | solution.py:236
  189.9 3.2 %collective-permute-start.10 = (f32[64,256]{1,0:T(8,128)S(1)}, f32[64,256]{1,0:T(8,128)S(1)}, u32[]{:S(2)}, u32[]{:S(2)}) collective-permute-start(f32[64,256]{1,0:T(8,128)S(1)} %slice_select_fusion.2), channel_id=1, source_target_pairs={{0,4},{4,0},{8,12},{12,8},{16,20},{20,16},{24,28},{28,24},{1,5},{5... | collective-permute-start | bytes 196616 | tf_op jit(solution)/shard_map/ppermute | solution.py:236
  193.1 7.5 %collective-permute-start.11 = (f32[64,256]{1,0:T(8,128)S(1)}, f32[64,256]{1,0:T(8,128)S(1)}, u32[]{:S(2)}, u32[]{:S(2)}) collective-permute-start(f32[64,256]{1,0:T(8,128)S(1)} %select_add_fusion.2), channel_id=1, source_target_pairs={{0,2},{1,3},{2,0},{3,1},{4,6},{5,7},{6,4},{7,5},{8,10},{9,11},{10,... | collective-permute-start | bytes 196616 | tf_op jit(solution)/shard_map/ppermute | solution.py:238
  193.9 5.5 %collective-permute-start.18 = (f32[96,128]{1,0:T(8,128)S(1)}, f32[96,128]{1,0:T(8,128)S(1)}, u32[]{:S(2)}, u32[]{:S(2)}) collective-permute-start(f32[96,128]{1,0:T(8,128)S(1)} %select_add_fusion.3), channel_id=1, source_target_pairs={{0,8},{4,12},{8,0},{12,4},{16,24},{20,28},{24,16},{28,20},{1,9},{5... | collective-permute-start | bytes 147464 | tf_op jit(solution)/shard_map/ppermute | solution.py:238
  199.4 3.6 %collective-permute-start.19 = (f32[96,128]{1,0:T(8,128)S(1)}, f32[96,128]{1,0:T(8,128)S(1)}, u32[]{:S(2)}, u32[]{:S(2)}) collective-permute-start(f32[96,128]{1,0:T(8,128)S(1)} %add.69), channel_id=1, source_target_pairs={{0,4},{4,0},{8,12},{12,8},{16,20},{20,16},{24,28},{28,24},{1,5},{5... | collective-permute-start | bytes 147464 | tf_op jit(solution)/shard_map/ppermute | solution.py:238
  200.6 4.1 %collective-permute-start.12 = (f32[64,256]{1,0:T(8,128)S(1)}, f32[64,256]{1,0:T(8,128)S(1)}, u32[]{:S(2)}, u32[]{:S(2)}) collective-permute-start(f32[64,256]{1,0:T(8,128)S(1)} %add.64), channel_id=1, source_target_pairs={{0,16},{4,20},{8,24},{12,28},{16,0},{20,4},{24,8},{28,12},{1,17},{... | collective-permute-start | bytes 196616 | tf_op jit(solution)/shard_map/ppermute | solution.py:238
  203.0 3.9 %collective-permute-start.20 = (f32[96,128]{1,0:T(8,128)S(1)}, f32[96,128]{1,0:T(8,128)S(1)}, u32[]{:S(2)}, u32[]{:S(2)}) collective-permute-start(f32[96,128]{1,0:T(8,128)S(1)} %add.70), channel_id=1, source_target_pairs={{0,16},{4,20},{8,24},{12,28},{16,0},{20,4},{24,8},{28,12},{1,17},{... | collective-permute-start | bytes 147464 | tf_op jit(solution)/shard_map/ppermute | solution.py:238
  204.7 3.9 %collective-permute-start.13 = (f32[64,256]{1,0:T(8,128)S(1)}, f32[64,256]{1,0:T(8,128)S(1)}, u32[]{:S(2)}, u32[]{:S(2)}) collective-permute-start(f32[64,256]{1,0:T(8,128)S(1)} %add.65), channel_id=1, source_target_pairs={{0,8},{4,12},{8,0},{12,4},{16,24},{20,28},{24,16},{28,20},{1,9},{5... | collective-permute-start | bytes 196616 | tf_op jit(solution)/shard_map/ppermute | solution.py:238
  206.9 3.0 %collective-permute-start.21 = (f32[96,128]{1,0:T(8,128)S(1)}, f32[96,128]{1,0:T(8,128)S(1)}, u32[]{:S(2)}, u32[]{:S(2)}) collective-permute-start(f32[96,128]{1,0:T(8,128)S(1)} %add.71), channel_id=1, source_target_pairs={{0,2},{1,3},{2,0},{3,1},{4,6},{5,7},{6,4},{7,5},{8,10},{9,11},{10,... | collective-permute-start | bytes 147464 | tf_op jit(solution)/shard_map/ppermute | solution.py:240
  208.6 7.0 %collective-permute-start.14 = (f32[64,256]{1,0:T(8,128)S(1)}, f32[64,256]{1,0:T(8,128)S(1)}, u32[]{:S(2)}, u32[]{:S(2)}) collective-permute-start(f32[64,256]{1,0:T(8,128)S(1)} %add.66), channel_id=1, source_target_pairs={{0,4},{4,0},{8,12},{12,8},{16,20},{20,16},{24,28},{28,24},{1,5},{5... | collective-permute-start | bytes 196616 | tf_op jit(solution)/shard_map/ppermute | solution.py:240
  209.9 7.9 %collective-permute-start.22 = (f32[192,128]{1,0:T(8,128)S(1)}, f32[192,128]{1,0:T(8,128)S(1)}, u32[]{:S(2)}, u32[]{:S(2)}) collective-permute-start(f32[192,128]{1,0:T(8,128)S(1)} %maximum_select_fusion.3), channel_id=1, source_target_pairs={{0,1},{1,0},{2,3},{3,2},{4,5},{5,4},{6,7},{7,6},{8,9},{9,8},{10,11... | collective-permute-start | bytes 294920 | tf_op jit(solution)/shard_map/ppermute | solution.py:240
  215.6 10.0 %collective-permute-start.15 = (f32[128,256]{1,0:T(8,128)S(1)}, f32[128,256]{1,0:T(8,128)S(1)}, u32[]{:S(2)}, u32[]{:S(2)}) collective-permute-start(f32[128,256]{1,0:T(8,128)S(1)} %maximum_select_fusion.2), channel_id=1, source_target_pairs={{0,1},{1,0},{2,3},{3,2},{4,5},{5,4},{6,7},{7,6},{8,9},{9,8},{10,11... | collective-permute-start | bytes 393224 | tf_op jit(solution)/shard_map/ppermute | solution.py:240

commit v9 on v8

--- a/solution.py
+++ b/solution.py
@@ -245,8 +245,8 @@
 def sum_both(corner, below, wide, narrow):
     core, y = ("narrow", narrow, 1), ("narrow", narrow, 2)
     x, z_near, z_far = [("wide", wide, 1 << b) for b in range(3)]
-    corner = sum_over_all(corner, [core, y], [z_near, x, z_far])
-    below = sum_over_all(below, [core, x], [y, z_far, z_near])
+    corner = sum_over_all(corner, [core, z_near], [x, y, z_far])
+    below = sum_over_all(below, [core, x], [z_near, z_far, y])
     return corner, below
 
 

time: 232 us -> 232 us (level)
  starting transfers between devices: 116 us -> 113 us
  waiting for transfers between devices: 66.2 us -> 69.1 us
    ppermute x6, starting transfers between devices: 11.6 us -> 6.51 us  [sum_over_all(): x = x + over(step)(x)]
    ppermute x6, waiting for transfers between devices: 2.99 us -> 6.26 us  [sum_over_all(): x = x + over(step)(x)]
    ppermute x4, starting transfers between devices: 6.83 us -> 9.55 us  [sum_over_all(): x = keep + over(step)(send)]
  transfers between devices with their start and end apart: 23 -> 23, of which waited for: 12 -> 14; matrix products, arithmetic and copies ran while one was open for 8% -> 8% of each run, Pallas kernels for 9% -> 9%
where the time goes in v9:
time: 232 us
  starting transfers between devices  113 us (49%)
  waiting for transfers between devices  69.1 us (30%)
  Pallas kernels  27.6 us (12%)
  local copies, waits for them, and re-layouts  20.9 us (9%)
    ppermute x4, starting transfers between devices, on_device_blocks(): over(('wide', wide, k))(tie(block_for(snapshot, here ^ k, nz), *deps))  46.8 us
    ppermute x1, starting transfers between devices, on_device_blocks(): late[5] = over(('wide', wide, 5))(tie(blocks[5], got[7]))  33.4 us
    ppermute x2, waiting for transfers between devices, on_device_blocks(): got[k] = over(('wide', wide, k))(block[:split_at])  26.7 us
    ppermute x4, waiting for transfers between devices, on_device_blocks(): over(('wide', wide, k))(tie(block_for(snapshot, here ^ k, nz), *deps))  20.6 us
    transpose x10, local copies, waits for them, and re-layouts, block_for(): return cut.transpose(1, 2, 0, 3).reshape(ny * nz, rows, fields)  15.8 us
    pallas_call x4, Pallas kernels, call(): pl.pallas_call(kernel, grid=(steps,), in_specs=[pl.BlockSpec(memory_space...  13.8 us
    ppermute x1, waiting for transfers between devices, on_device_blocks(): got[6] = over(('wide', wide, 6))(first)  10.5 us
    ppermute x4, starting transfers between devices, sum_over_all(): x = keep + over(step)(send)  9.55 us
  transfers between devices with their start and end apart: 23, of which 14 were waited for; matrix products, arithmetic and copies ran while one was open for 8% of the time, Pallas kernels for 9%

profile of v9, /device:TPU:1, one launch (start us, length us, event | category | flops | bytes accessed | tf_op | source)
XLA Modules:
  0.0 231.6 jit_solution(14507136667353017428)
XLA Ops:
  0.6 1.3 dynamic-slice_bitcast_fusion.7
  2.6 4.2 %collective-permute-start.2 = (f32[32,64,128]{2,1,0:T(8,128)S(1)}, f32[32,64,128]{2,1,0:T(8,128)S(1)}, u32[]{:S(2)}, u32[]{:S(2)}) collective-permute-start(f32[32,64,128]{2,1,0:T(8,128)S(1)} %bitcast.30), channel_id=1, source_target_pairs={{0,24},{4,28},{8,16},{12,20},{16,8},{20,12},{24,0},{28,4},{1,25},{... | collective-permute-start | bytes 3145736 | tf_op jit(solution)/shard_map/ppermute | solution.py:421
  6.8 5.4 %dynamic-slice_bitcast_fusion = (f32[4,8,64,128]{3,1,0,2:T(8,128)S(1)}, f32[4,8,64,128]{3,1,0,2:T(8,128)S(1)}, f32[4,8,64,128]{3,1,0,2:T(8,128)S(1)}, f32[4,8,64...) fusion(f32[64,4,64,128]{3,2,1,0:T(8,128)} %param.1, ...), kind=kLoop, calls=%fused_computation | loop fusion | bytes 14680092 | tf_op jit(solution)/shard_map/transpose | solution.py:410
  12.9 1.6 copy.7
  14.5 1.2 collective-permute-start
  15.7 1.6 copy.8
  17.7 1.6 copy.9
  19.3 10.5 %collective-permute-done.2.far = f32[32,64,128]{2,1,0:T(8,128)S(1)} collective-permute-done((f32[32,64,128]{2,1,0:T(8,128)S(1)}, f32[32,64,128]{2,1,0:T(8,128)S(1)}, u32[]{:S(2)}, u32[]{:S(2)}) %collective-permute-start.2) | collective-permute-done | bytes 1048608 | tf_op jit(solution)/shard_map/ppermute | solution.py:421
  29.8 45.2 %collective-permute-start.3 = (f32[32,64,128]{2,1,0:T(8,128)}, f32[32,64,128]{2,1,0:T(8,128)}, u32[]{:S(2)}, u32[]{:S(2)}) collective-permute-start(f32[32,64,128]{2,1,0:T(8,128)} %bitcast.10), channel_id=1, source_target_pairs={{0,12},{4,8},{8,4},{12,0},{16,28},{20,24},{24,20},{28,16},{1,13},{... | collective-permute-start | bytes 3145736 | tf_op jit(solution)/shard_map/ppermute | solution.py:420
  75.6 20.6 %collective-permute-done.4.near = f32[32,64,128]{2,1,0:T(8,128)S(1)} collective-permute-done((f32[32,64,128]{2,1,0:T(8,128)S(1)}, f32[32,64,128]{2,1,0:T(8,128)S(1)}, u32[]{:S(2)}, u32[]{:S(2)}) %collective-permute-start.4) | collective-permute-done | bytes 1048608 | tf_op jit(solution)/shard_map/ppermute | solution.py:420
  97.1 2.9 %collective-permute-start.6 = (f32[24,64,128]{2,1,0:T(8,128)}, f32[24,64,128]{2,1,0:T(8,128)S(1)}, u32[]{:S(2)}, u32[]{:S(2)}) collective-permute-start(f32[24,64,128]{2,1,0:T(8,128)} %slice.45), channel_id=1, source_target_pairs={{0,28},{4,24},{8,20},{12,16},{16,12},{20,8},{24,4},{28,0},{1,29},{... | collective-permute-start | bytes 2359304 | tf_op jit(solution)/shard_map/ppermute | solution.py:428
  102.8 1.8 copy.6
  106.6 11.2 %collective-permute-done.6.far = f32[24,64,128]{2,1,0:T(8,128)S(1)} collective-permute-done((f32[24,64,128]{2,1,0:T(8,128)}, f32[24,64,128]{2,1,0:T(8,128)S(1)}, u32[]{:S(2)}, u32[]{:S(2)}) %collective-permute-start.6) | collective-permute-done | bytes 786464 | tf_op jit(solution)/shard_map/ppermute | solution.py:428
  117.7 33.4 %collective-permute-start.7 = (f32[8,64,128]{2,1,0:T(8,128)S(1)}, f32[8,64,128]{2,1,0:T(8,128)S(1)}, u32[]{:S(2)}, u32[]{:S(2)}) collective-permute-start(f32[8,64,128]{2,1,0:T(8,128)S(1)} %slice.46), channel_id=1, source_target_pairs={{0,20},{4,16},{8,28},{12,24},{16,4},{20,0},{24,12},{28,8},{1,21},{... | collective-permute-start | bytes 786440 | tf_op jit(solution)/shard_map/ppermute | solution.py:430
  152.0 5.1 %own_gram.1 = (f32[256,256]{1,0:T(8,128)S(1)}, bf16[16,256,256]{2,1,0:T(8,128)(2,1)S(1)}, bf16[16,256,256]{2,1,0:T(8,128)(2,1)S(1)}) custom-call(s32[1]{0:T(128)} %bitcast.place_ref, f32[32,64,128]{2,1,0:T(8,128)S(1)} %bitcast.25, f32[32,64,128]{2,1,0:T(8,128)} %collective-permute-done.refs_1_, f32[32,64,128]{2,1,0:T(8,128)} %collective-permute-done.1.refs_2_, ...), custom_call_target="tpu_custom_call" | custom-call | flops 2147483648 | bytes 8388608 | tf_op jit(solution)/shard_map/own_gram/pallas_call | solution.py:159
  157.1 4.3 %even_gram.1 = (f32[128,256]{1,0:T(8,128)S(1)}, f32[128,128]{1,0:T(8,128)S(1)}, bf16[16,128,256]{2,1,0:T(8,128)(2,1)S(1)}, bf16[16,128,256]{2,1,0:T(8,128)(2,1)S(1)}) custom-call(s32[1]{0:T(128)} %bitcast.place_ref, f32[32,64,128]{2,1,0:T(8,128)S(1)} %collective-permute-done.4.near, f32[32,64,128]{2,1,0:T(8,128)S(1)} %collective-permute-done.2.far, ...), custom_call_target="tpu_custom_call" | custom-call | flops 1610612736 | bytes 4194304 | tf_op jit(solution)/shard_map/even_gram/pallas_call | solution.py:159
  161.4 15.5 %collective-permute-done.5.near = f32[24,64,128]{2,1,0:T(8,128)} collective-permute-done((f32[24,64,128]{2,1,0:T(8,128)}, f32[24,64,128]{2,1,0:T(8,128)}, u32[]{:S(2)}, u32[]{:S(2)}) %collective-permute-start.5) | collective-permute-done | bytes 786464 | tf_op jit(solution)/shard_map/ppermute | solution.py:428
  176.9 3.5 %odd_gram.1 = (f32[512,128]{1,0:T(8,128)S(1)}, bf16[16,128,256]{2,1,0:T(8,128)(2,1)S(1)}, bf16[16,128,256]{2,1,0:T(8,128)(2,1)S(1)}) custom-call(s32[1]{0:T(128)} %bitcast.place_ref, f32[24,64,128]{2,1,0:T(8,128)} %collective-permute-done.5.near, f32[24,64,128]{2,1,0:T(8,128)S(1)} %collective-permute-done.6.far, ...), custom_call_target="tpu_custom_call" | custom-call | flops 1610612736 | bytes 3670016 | tf_op jit(solution)/shard_map/odd_gram/pallas_call | solution.py:159
  180.4 2.1 collective-permute-done.7.near
  183.4 4.2 %collective-permute-start.16 = (f32[192,128]{1,0:T(8,128)S(1)}, f32[192,128]{1,0:T(8,128)S(1)}, u32[]{:S(2)}, u32[]{:S(2)}) collective-permute-start(f32[192,128]{1,0:T(8,128)S(1)} %slice_select_fusion.1), channel_id=1, source_target_pairs={{0,1},{1,0},{2,3},{3,2},{4,5},{5,4},{6,7},{7,6},{8,9},{9,8},{10,11... | collective-permute-start | bytes 294920 | tf_op jit(solution)/shard_map/ppermute | solution.py:236
  188.6 4.1 %collective-permute-start.17 = (f32[96,128]{1,0:T(8,128)S(1)}, f32[96,128]{1,0:T(8,128)S(1)}, u32[]{:S(2)}, u32[]{:S(2)}) collective-permute-start(f32[96,128]{1,0:T(8,128)S(1)} %slice_select_fusion.3), channel_id=1, source_target_pairs={{0,8},{4,12},{8,0},{12,4},{16,24},{20,28},{24,16},{28,20},{1,9},{5... | collective-permute-start | bytes 147464 | tf_op jit(solution)/shard_map/ppermute | solution.py:236
  194.2 1.7 collective-permute-done.10
  197.9 1.8 collective-permute-done.18
  199.8 1.3 collective-permute-start.19
  201.1 1.5 collective-permute-start.12
  202.8 1.5 collective-permute-start.20
  204.2 1.6 collective-permute-done.12
  207.5 1.6 collective-permute-done.13
  210.5 5.1 %collective-permute-start.22 = (f32[192,128]{1,0:T(8,128)S(1)}, f32[192,128]{1,0:T(8,128)S(1)}, u32[]{:S(2)}, u32[]{:S(2)}) collective-permute-start(f32[192,128]{1,0:T(8,128)S(1)} %maximum_select_fusion.3), channel_id=1, source_target_pairs={{0,1},{1,0},{2,3},{3,2},{4,5},{5,4},{6,7},{7,6},{8,9},{9,8},{10,11... | collective-permute-start | bytes 294920 | tf_op jit(solution)/shard_map/ppermute | solution.py:240
  215.7 2.1 collective-permute-start.15
  217.8 7.8 %cholesky256.1 = (f32[256,256]{1,0:T(8,128)S(1)}, f32[256,256]{1,0:T(8,128)S(1)}) custom-call(f32[384,128]{1,0:T(8,128)S(1)} %maximum_select_fusion.1.gram_ref), custom_call_target="tpu_custom_call" | custom-call | flops 1073741824 | bytes 786432 | tf_op jit(solution)/shard_map/cholesky256/pallas_call | solution.py:340
  225.6 6.0 %core.1 = (f32[512,256]{1,0:T(8,128)}, f32[256,4,8,128]{3,2,1,0:T(8,128)}) custom-call(s32[1]{0:T(128)} %bitcast.place_ref, f32[256,256]{1,0:T(8,128)S(1)} %maximum_select_fusion.below, f32[256,256]{1,0:T(8,128)S(1)} %get-tuple-element.44.upper, f32[256,256]{1,0:T(8,128)S(1)} %get-tuple-element.45.inverse, ...), custom_call_target="tpu_custom_call" | custom-call | flops 3221225472 | bytes 12582912 | tf_op jit(solution)/shard_map/core/pallas_call | solution.py:384
  (56 shorter events, 17.6 us)
Async XLA Ops:
  2.6 27.2 %collective-permute-start.2 = (f32[32,64,128]{2,1,0:T(8,128)S(1)}, f32[32,64,128]{2,1,0:T(8,128)S(1)}, u32[]{:S(2)}, u32[]{:S(2)}) collective-permute-start(f32[32,64,128]{2,1,0:T(8,128)S(1)} %bitcast.30), channel_id=1, source_target_pairs={{0,24},{4,28},{8,16},{12,20},{16,8},{20,12},{24,0},{28,4},{1,25},{... | collective-permute-start | bytes 3145736 | tf_op jit(solution)/shard_map/ppermute | solution.py:421
  12.8 83.3 %collective-permute-start.4 = (f32[32,64,128]{2,1,0:T(8,128)S(1)}, f32[32,64,128]{2,1,0:T(8,128)S(1)}, u32[]{:S(2)}, u32[]{:S(2)}) collective-permute-start(f32[32,64,128]{2,1,0:T(8,128)S(1)} %bitcast.31), channel_id=1, source_target_pairs={{0,16},{4,20},{8,24},{12,28},{16,0},{20,4},{24,8},{28,12},{1,17},{... | collective-permute-start | bytes 3145736 | tf_op jit(solution)/shard_map/ppermute | solution.py:420
  14.5 136.6 %collective-permute-start = (f32[32,64,128]{2,1,0:T(8,128)}, f32[32,64,128]{2,1,0:T(8,128)}, u32[]{:S(2)}, u32[]{:S(2)}) collective-permute-start(f32[32,64,128]{2,1,0:T(8,128)} %bitcast.6), channel_id=1, source_target_pairs={{0,4},{4,0},{8,12},{12,8},{16,20},{20,16},{24,28},{28,24},{1,5},{5... | collective-permute-start | bytes 3145736 | tf_op jit(solution)/shard_map/ppermute | solution.py:420
  17.3 134.7 %collective-permute-start.1 = (f32[32,64,128]{2,1,0:T(8,128)}, f32[32,64,128]{2,1,0:T(8,128)}, u32[]{:S(2)}, u32[]{:S(2)}) collective-permute-start(f32[32,64,128]{2,1,0:T(8,128)} %bitcast.8), channel_id=1, source_target_pairs={{0,8},{4,12},{8,0},{12,4},{16,24},{20,28},{24,16},{28,20},{1,9},{5... | collective-permute-start | bytes 3145736 | tf_op jit(solution)/shard_map/ppermute | solution.py:420
  29.8 122.3 %collective-permute-start.3 = (f32[32,64,128]{2,1,0:T(8,128)}, f32[32,64,128]{2,1,0:T(8,128)}, u32[]{:S(2)}, u32[]{:S(2)}) collective-permute-start(f32[32,64,128]{2,1,0:T(8,128)} %bitcast.10), channel_id=1, source_target_pairs={{0,12},{4,8},{8,4},{12,0},{16,28},{20,24},{24,20},{28,16},{1,13},{... | collective-permute-start | bytes 3145736 | tf_op jit(solution)/shard_map/ppermute | solution.py:420
  75.6 25.1 %copy-start = (f32[4,8,64,128]{3,2,1,0:T(8,128)}, f32[4,8,64,128]{3,2,1,0:T(8,128)S(1)}, u32[]{:S(2)}) copy-start(f32[4,8,64,128]{3,2,1,0:T(8,128)S(1)} %copy.12) | copy-start | bytes 3145732
  97.1 20.6 %collective-permute-start.6 = (f32[24,64,128]{2,1,0:T(8,128)}, f32[24,64,128]{2,1,0:T(8,128)S(1)}, u32[]{:S(2)}, u32[]{:S(2)}) collective-permute-start(f32[24,64,128]{2,1,0:T(8,128)} %slice.45), channel_id=1, source_target_pairs={{0,28},{4,24},{8,20},{12,16},{16,12},{20,8},{24,4},{28,0},{1,29},{... | collective-permute-start | bytes 2359304 | tf_op jit(solution)/shard_map/ppermute | solution.py:428
  100.7 1.1 copy-start.1
  102.8 74.2 %collective-permute-start.5 = (f32[24,64,128]{2,1,0:T(8,128)}, f32[24,64,128]{2,1,0:T(8,128)}, u32[]{:S(2)}, u32[]{:S(2)}) collective-permute-start(f32[24,64,128]{2,1,0:T(8,128)} %slice.44), channel_id=1, source_target_pairs={{0,20},{4,16},{8,28},{12,24},{16,4},{20,0},{24,12},{28,8},{1,21},{... | collective-permute-start | bytes 2359304 | tf_op jit(solution)/shard_map/ppermute | solution.py:428
  117.7 64.7 %collective-permute-start.7 = (f32[8,64,128]{2,1,0:T(8,128)S(1)}, f32[8,64,128]{2,1,0:T(8,128)S(1)}, u32[]{:S(2)}, u32[]{:S(2)}) collective-permute-start(f32[8,64,128]{2,1,0:T(8,128)S(1)} %slice.46), channel_id=1, source_target_pairs={{0,20},{4,16},{8,28},{12,24},{16,4},{20,0},{24,12},{28,8},{1,21},{... | collective-permute-start | bytes 786440 | tf_op jit(solution)/shard_map/ppermute | solution.py:430
  151.1 31.4 %collective-permute-start.8 = (f32[8,64,128]{2,1,0:T(8,128)S(1)}, f32[8,64,128]{2,1,0:T(8,128)S(1)}, u32[]{:S(2)}, u32[]{:S(2)}) collective-permute-start(f32[8,64,128]{2,1,0:T(8,128)S(1)} %slice.47), channel_id=1, source_target_pairs={{0,28},{4,24},{8,20},{12,16},{16,12},{20,8},{24,4},{28,0},{1,29},{... | collective-permute-start | bytes 786440 | tf_op jit(solution)/shard_map/ppermute | solution.py:431
  183.4 5.1 %collective-permute-start.16 = (f32[192,128]{1,0:T(8,128)S(1)}, f32[192,128]{1,0:T(8,128)S(1)}, u32[]{:S(2)}, u32[]{:S(2)}) collective-permute-start(f32[192,128]{1,0:T(8,128)S(1)} %slice_select_fusion.1), channel_id=1, source_target_pairs={{0,1},{1,0},{2,3},{3,2},{4,5},{5,4},{6,7},{7,6},{8,9},{9,8},{10,11... | collective-permute-start | bytes 294920 | tf_op jit(solution)/shard_map/ppermute | solution.py:236
  187.6 5.1 %collective-permute-start.9 = (f32[128,256]{1,0:T(8,128)S(1)}, f32[128,256]{1,0:T(8,128)S(1)}, u32[]{:S(2)}, u32[]{:S(2)}) collective-permute-start(f32[128,256]{1,0:T(8,128)S(1)} %slice_select_fusion), channel_id=1, source_target_pairs={{0,1},{1,0},{2,3},{3,2},{4,5},{5,4},{6,7},{7,6},{8,9},{9,8},{10,11... | collective-permute-start | bytes 393224 | tf_op jit(solution)/shard_map/ppermute | solution.py:236
  188.6 5.6 %collective-permute-start.17 = (f32[96,128]{1,0:T(8,128)S(1)}, f32[96,128]{1,0:T(8,128)S(1)}, u32[]{:S(2)}, u32[]{:S(2)}) collective-permute-start(f32[96,128]{1,0:T(8,128)S(1)} %slice_select_fusion.3), channel_id=1, source_target_pairs={{0,8},{4,12},{8,0},{12,4},{16,24},{20,28},{24,16},{28,20},{1,9},{5... | collective-permute-start | bytes 147464 | tf_op jit(solution)/shard_map/ppermute | solution.py:236
  192.7 3.2 %collective-permute-start.10 = (f32[64,256]{1,0:T(8,128)S(1)}, f32[64,256]{1,0:T(8,128)S(1)}, u32[]{:S(2)}, u32[]{:S(2)}) collective-permute-start(f32[64,256]{1,0:T(8,128)S(1)} %slice_select_fusion.2), channel_id=1, source_target_pairs={{0,4},{4,0},{8,12},{12,8},{16,20},{20,16},{24,28},{28,24},{1,5},{5... | collective-permute-start | bytes 196616 | tf_op jit(solution)/shard_map/ppermute | solution.py:236
  195.9 5.1 %collective-permute-start.11 = (f32[64,256]{1,0:T(8,128)S(1)}, f32[64,256]{1,0:T(8,128)S(1)}, u32[]{:S(2)}, u32[]{:S(2)}) collective-permute-start(f32[64,256]{1,0:T(8,128)S(1)} %select_add_fusion.2), channel_id=1, source_target_pairs={{0,8},{4,12},{8,0},{12,4},{16,24},{20,28},{24,16},{28,20},{1,9},{5... | collective-permute-start | bytes 196616 | tf_op jit(solution)/shard_map/ppermute | solution.py:238
  196.8 2.9 %collective-permute-start.18 = (f32[96,128]{1,0:T(8,128)S(1)}, f32[96,128]{1,0:T(8,128)S(1)}, u32[]{:S(2)}, u32[]{:S(2)}) collective-permute-start(f32[96,128]{1,0:T(8,128)S(1)} %select_add_fusion.3), channel_id=1, source_target_pairs={{0,4},{4,0},{8,12},{12,8},{16,20},{20,16},{24,28},{28,24},{1,5},{5... | collective-permute-start | bytes 147464 | tf_op jit(solution)/shard_map/ppermute | solution.py:238
  199.8 3.0 %collective-permute-start.19 = (f32[96,128]{1,0:T(8,128)S(1)}, f32[96,128]{1,0:T(8,128)S(1)}, u32[]{:S(2)}, u32[]{:S(2)}) collective-permute-start(f32[96,128]{1,0:T(8,128)S(1)} %add.69), channel_id=1, source_target_pairs={{0,2},{1,3},{2,0},{3,1},{4,6},{5,7},{6,4},{7,5},{8,10},{9,11},{10,... | collective-permute-start | bytes 147464 | tf_op jit(solution)/shard_map/ppermute | solution.py:238
  201.1 4.8 %collective-permute-start.12 = (f32[64,256]{1,0:T(8,128)S(1)}, f32[64,256]{1,0:T(8,128)S(1)}, u32[]{:S(2)}, u32[]{:S(2)}) collective-permute-start(f32[64,256]{1,0:T(8,128)S(1)} %add.64), channel_id=1, source_target_pairs={{0,16},{4,20},{8,24},{12,28},{16,0},{20,4},{24,8},{28,12},{1,17},{... | collective-permute-start | bytes 196616 | tf_op jit(solution)/shard_map/ppermute | solution.py:238
  202.8 4.4 %collective-permute-start.20 = (f32[96,128]{1,0:T(8,128)S(1)}, f32[96,128]{1,0:T(8,128)S(1)}, u32[]{:S(2)}, u32[]{:S(2)}) collective-permute-start(f32[96,128]{1,0:T(8,128)S(1)} %add.70), channel_id=1, source_target_pairs={{0,16},{4,20},{8,24},{12,28},{16,0},{20,4},{24,8},{28,12},{1,17},{... | collective-permute-start | bytes 147464 | tf_op jit(solution)/shard_map/ppermute | solution.py:238
  205.9 3.2 %collective-permute-start.13 = (f32[64,256]{1,0:T(8,128)S(1)}, f32[64,256]{1,0:T(8,128)S(1)}, u32[]{:S(2)}, u32[]{:S(2)}) collective-permute-start(f32[64,256]{1,0:T(8,128)S(1)} %add.65), channel_id=1, source_target_pairs={{0,2},{1,3},{2,0},{3,1},{4,6},{5,7},{6,4},{7,5},{8,10},{9,11},{10,... | collective-permute-start | bytes 196616 | tf_op jit(solution)/shard_map/ppermute | solution.py:238
  207.2 3.3 %collective-permute-start.21 = (f32[96,128]{1,0:T(8,128)S(1)}, f32[96,128]{1,0:T(8,128)S(1)}, u32[]{:S(2)}, u32[]{:S(2)}) collective-permute-start(f32[96,128]{1,0:T(8,128)S(1)} %add.71), channel_id=1, source_target_pairs={{0,8},{4,12},{8,0},{12,4},{16,24},{20,28},{24,16},{28,20},{1,9},{5... | collective-permute-start | bytes 147464 | tf_op jit(solution)/shard_map/ppermute | solution.py:240
  209.1 6.6 %collective-permute-start.14 = (f32[64,256]{1,0:T(8,128)S(1)}, f32[64,256]{1,0:T(8,128)S(1)}, u32[]{:S(2)}, u32[]{:S(2)}) collective-permute-start(f32[64,256]{1,0:T(8,128)S(1)} %add.66), channel_id=1, source_target_pairs={{0,4},{4,0},{8,12},{12,8},{16,20},{20,16},{24,28},{28,24},{1,5},{5... | collective-permute-start | bytes 196616 | tf_op jit(solution)/shard_map/ppermute | solution.py:240
  210.5 7.2 %collective-permute-start.22 = (f32[192,128]{1,0:T(8,128)S(1)}, f32[192,128]{1,0:T(8,128)S(1)}, u32[]{:S(2)}, u32[]{:S(2)}) collective-permute-start(f32[192,128]{1,0:T(8,128)S(1)} %maximum_select_fusion.3), channel_id=1, source_target_pairs={{0,1},{1,0},{2,3},{3,2},{4,5},{5,4},{6,7},{7,6},{8,9},{9,8},{10,11... | collective-permute-start | bytes 294920 | tf_op jit(solution)/shard_map/ppermute | solution.py:240
  215.7 9.9 %collective-permute-start.15 = (f32[128,256]{1,0:T(8,128)S(1)}, f32[128,256]{1,0:T(8,128)S(1)}, u32[]{:S(2)}, u32[]{:S(2)}) collective-permute-start(f32[128,256]{1,0:T(8,128)S(1)} %maximum_select_fusion.2), channel_id=1, source_target_pairs={{0,1},{1,0},{2,3},{3,2},{4,5},{5,4},{6,7},{7,6},{8,9},{9,8},{10,11... | collective-permute-start | bytes 393224 | tf_op jit(solution)/shard_map/ppermute | solution.py:240
